TPU v7x, 32 devices: a whole 2x2x4 slice. The times are simulated.
32 devices in a mesh: group: 4 (over x, core), seq: 4 (over z), tp: 2 (over y).
Axes of the slice: x: 2, y: 2, z: 4, core: 2. Of those that a mesh axis runs over, the one named last changes fastest.
Arguments:
- queries: bfloat16 [4, 512, 4096], P('seq', 'group', 'tp'), may hold values from -256 to 256
- keys: bfloat16 [4, 512, 512], P('seq', 'group', 'tp'), may hold values from -12 to 12
- values: bfloat16 [4, 512, 512], P('seq', 'group', 'tp'), may hold values from -6 to 6
- moe_x: bfloat16 [4, 128, 2048], P('group', ('seq', 'tp')), may hold values from -6 to 6
- expert_ids: int32 [4, 128, 8], P('group', ('seq', 'tp')), may hold values from 0 to 63, all different within a row; in each aligned block of 16 rows (0 to 15, 16 to 31, ..., all dimensions but the last counted through in order) at most 3 rows name the same one
- gates: float32 [4, 128, 8], P('group', ('seq', 'tp')), may hold values from 0.05 to 0.5
- grad_out: bfloat16 [4, 128, 2048], P('group', ('seq', 'tp')), may hold values from -6 to 6
- w_gate: bfloat16 [64, 2048, 384], P(('seq', 'tp')), may hold values from -0.125 to 0.125
- w_up: bfloat16 [64, 2048, 384], P(('seq', 'tp')), may hold values from -0.125 to 0.125
- w_down: bfloat16 [64, 384, 2048], P(('seq', 'tp')), may hold values from -0.3125 to 0.3125
Outputs:
- attn_out: bfloat16 [4, 512, 4096], P('seq', 'group', 'tp')
- moe_out: bfloat16 [4, 128, 2048], P('group', ('seq', 'tp'))
- moe_grad_in: bfloat16 [4, 128, 2048], P('group', ('seq', 'tp'))
Inputs may be any that keep to these rules, and one draw needn't show every extreme that they name: `expert_ids`: each token names 8 different experts. Within each aligned block of 16 tokens (the tokens of one device, in order), no expert is named by more than 3 tokens, and in every draw some block names some expert exactly 3 times.
All inputs are finite; a program needn't handle non-finite values.
Results may differ from a plain program's by a relative error of at most 0.0064.
Values may be sent and summed in bfloat16 or wider, within the bound.
No kernel may reach another device: no remote copies, remote signals or barrier semaphores. Data moves between devices by JAX's collectives and lax.ppermute only.
A program may use at most 128 MiB of HBM per device.

v0:
```python
import jax
import jax.numpy as jnp
from jax import lax
from jax.sharding import PartitionSpec as P

H = 32
KVH = 4
HD = 128
EXPERTS = 64
CAP = 3


def for_sending(array):
    return jax.tree.map(lambda a: a.astype(jnp.bfloat16) if a.dtype == jnp.float32 else a, array)


def attend_head(query_rows, key_rows, value_rows):
    seq_len = query_rows.shape[0]
    block_len = min(512, seq_len)
    score_scale = 1.0 / query_rows.shape[1] ** 0.5
    pieces = []
    for first_row in range(0, seq_len, block_len):
        last_row = first_row + block_len
        scores = (
            lax.dot_general(
                query_rows[first_row:last_row],
                key_rows[:last_row],
                (((1,), (1,)), ((), ())),
                preferred_element_type=jnp.float32,
            )
            * score_scale
        )
        row_pos = first_row + lax.broadcasted_iota(jnp.int32, (block_len, last_row), 0)
        col_pos = lax.broadcasted_iota(jnp.int32, (block_len, last_row), 1)
        scores = jnp.where(col_pos <= row_pos, scores, -jnp.inf)
        row_max = jnp.max(scores, axis=1, keepdims=True)
        exp_scores = jnp.exp(scores - row_max)
        row_total = jnp.sum(exp_scores, axis=1, keepdims=True)
        mixed_rows = jnp.dot(
            exp_scores.astype(jnp.bfloat16),
            value_rows[:last_row],
            preferred_element_type=jnp.float32,
        )
        pieces.append((mixed_rows / row_total).astype(jnp.bfloat16))
    return jnp.concatenate(pieces, axis=0)


def route_tables(expert_ids, gates):
    route_ids = expert_ids[0]
    flat_ids = route_ids.reshape(-1)
    onehot = (
        flat_ids[:, None] == lax.broadcasted_iota(jnp.int32, (flat_ids.shape[0], EXPERTS), 1)
    ).astype(jnp.int32)
    before = jnp.cumsum(onehot, axis=0) - onehot
    slot_place = (flat_ids * CAP + jnp.sum(before * onehot, axis=1)).reshape(route_ids.shape)
    slot_match = slot_place[None, :, :] == lax.broadcasted_iota(
        jnp.int32, (EXPERTS * CAP, route_ids.shape[0], route_ids.shape[1]), 0
    )
    selector = jnp.sum(slot_match.astype(jnp.float32), axis=2)
    weighted = jnp.sum(jnp.where(slot_match, gates[0][None, :, :], 0.0), axis=2)
    return (selector, weighted)


def expert_math(token_rows, grad_rows, w_gate, w_up, w_down):
    hgate = jnp.einsum("secd,edf->secf", token_rows, w_gate, preferred_element_type=jnp.float32)
    hup = jnp.einsum("secd,edf->secf", token_rows, w_up, preferred_element_type=jnp.float32)
    sigmoid_gate = jax.nn.sigmoid(hgate)
    silu_gate = hgate * sigmoid_gate
    activated = (silu_gate * hup).astype(jnp.bfloat16)
    expert_out = jnp.einsum(
        "secf,efd->secd", activated, w_down, preferred_element_type=jnp.float32
    ).astype(jnp.bfloat16)
    grad_act = jnp.einsum("secd,efd->secf", grad_rows, w_down, preferred_element_type=jnp.float32)
    grad_gate = (grad_act * hup * sigmoid_gate * (1.0 + hgate * (1.0 - sigmoid_gate))).astype(
        jnp.bfloat16
    )
    grad_up = (grad_act * silu_gate).astype(jnp.bfloat16)
    input_grad = jnp.einsum("secf,edf->secd", grad_gate, w_gate, preferred_element_type=jnp.float32)
    input_grad = input_grad + jnp.einsum(
        "secf,edf->secd", grad_up, w_up, preferred_element_type=jnp.float32
    )
    return (expert_out, input_grad.astype(jnp.bfloat16))


def shards(queries, keys, values, moe_x, expert_ids, gates, grad_out, w_gate, w_up, w_down):
    tok_rows = queries.shape[1]
    group_count = lax.axis_size("group")
    tp_count = lax.axis_size("tp")
    local_queries = H // tp_count
    per_device = local_queries // group_count
    kv_local = KVH // tp_count
    repeats = group_count // kv_local
    query_heads = queries[0].reshape(tok_rows, group_count, per_device, HD)
    key_heads = jnp.broadcast_to(
        keys[0].reshape(tok_rows, kv_local, 1, HD), (tok_rows, kv_local, repeats, HD)
    ).reshape(tok_rows, group_count, 1, HD)
    value_heads = jnp.broadcast_to(
        values[0].reshape(tok_rows, kv_local, 1, HD), (tok_rows, kv_local, repeats, HD)
    ).reshape(tok_rows, group_count, 1, HD)
    head_queries, head_keys, head_values = (
        lax.all_to_all(query_heads, "group", split_axis=1, concat_axis=0, tiled=True),
        lax.all_to_all(key_heads, "group", split_axis=1, concat_axis=0, tiled=True),
        lax.all_to_all(value_heads, "group", split_axis=1, concat_axis=0, tiled=True),
    )
    attended = jax.vmap(attend_head, in_axes=(1, None, None), out_axes=1)(
        head_queries[:, 0], head_keys[:, 0, 0], head_values[:, 0, 0]
    )
    restored = lax.all_to_all(
        for_sending(attended[:, None]), "group", split_axis=0, concat_axis=1, tiled=True
    )
    attn_out = restored.reshape(1, tok_rows, local_queries * HD)
    selector, weighted = route_tables(expert_ids, gates)
    send_rows = jnp.dot(
        selector.astype(jnp.bfloat16), moe_x[0], preferred_element_type=jnp.float32
    ).astype(jnp.bfloat16)
    send_grads = jnp.dot(
        weighted, grad_out[0].astype(jnp.float32), precision=lax.Precision.HIGHEST
    ).astype(jnp.bfloat16)
    devices = lax.axis_size(("seq", "tp"))
    local_experts = EXPERTS // devices
    width = send_rows.shape[1]
    buffer_shape = (devices, local_experts, CAP, width)
    recv_rows, recv_grads = (
        lax.all_to_all(
            send_rows.reshape(buffer_shape), ("seq", "tp"), split_axis=0, concat_axis=0, tiled=True
        ),
        lax.all_to_all(
            send_grads.reshape(buffer_shape), ("seq", "tp"), split_axis=0, concat_axis=0, tiled=True
        ),
    )
    expert_out, input_grad = expert_math(recv_rows, recv_grads, w_gate, w_up, w_down)
    back_out, back_grad = (
        lax.all_to_all(expert_out, ("seq", "tp"), split_axis=0, concat_axis=0, tiled=True),
        lax.all_to_all(input_grad, ("seq", "tp"), split_axis=0, concat_axis=0, tiled=True),
    )
    slot_out = back_out.reshape(EXPERTS * CAP, width).astype(jnp.float32)
    slot_grad = back_grad.reshape(EXPERTS * CAP, width).astype(jnp.float32)
    moe_out = lax.dot_general(
        weighted, slot_out, (((0,), (0,)), ((), ())), precision=lax.Precision.HIGHEST
    )
    moe_grad_in = lax.dot_general(
        selector, slot_grad, (((0,), (0,)), ((), ())), precision=lax.Precision.HIGHEST
    )
    return (attn_out, moe_out.astype(jnp.bfloat16)[None], moe_grad_in.astype(jnp.bfloat16)[None])


def solution(mesh):
    placed = (
        P("seq", "group", "tp"),
        P("seq", "group", "tp"),
        P("seq", "group", "tp"),
        P("group", ("seq", "tp"), None),
        P("group", ("seq", "tp"), None),
        P("group", ("seq", "tp"), None),
        P("group", ("seq", "tp"), None),
        P(("seq", "tp"), None, None),
        P(("seq", "tp"), None, None),
        P(("seq", "tp"), None, None),
    )
    return jax.shard_map(
        shards,
        mesh=mesh,
        in_specs=placed,
        out_specs=(
            P("seq", "group", "tp"),
            P("group", ("seq", "tp"), None),
            P("group", ("seq", "tp"), None),
        ),
        check_vma=False,
    )
```

profile of v0, /device:TPU:0, one launch (start us, length us, event | category | flops | bytes accessed | tf_op | source)
XLA Modules:
  0.0 144.7 jit_solution(3739812047276055498)
XLA Ops:
  0.6 0.0 copy-start
  0.6 0.0 copy-start.1
  0.7 0.9 broadcast_in_dim.51
  1.6 0.7 broadcast_in_dim.52
  2.2 4.2 %all-to-all-start.2 = ((bf16[128,4,1,128]{3,0,2,1:T(8,128)(2,1)}), bf16[128,4,1,128]{3,0,2,1:T(8,128)(2,1)S(1)}, u32[]{:S(2)}, u32[]{:S(2)}) async-start(bf16[128,4,1,128]{3,0,2,1:T(8,128)(2,1)} %bitcast.10), calls=%async_computation.2 | async-start | bytes 262144 | tf_op jit(solution)/shard_map/all_to_all | solution.py:103
  6.5 0.8 copy.125
  7.2 0.1 eq.20
  7.3 0.1 fusion.59
  7.4 1.3 copy.117
  8.7 1.0 copy.118
  9.7 0.9 broadcast_in_dim.48
  10.6 0.2 reduce_window_sum.11
  10.8 0.3 all-to-all-done.2
  11.1 0.7 broadcast_in_dim.49
  11.7 3.3 %all-to-all-start.1 = ((bf16[128,4,1,128]{3,0,2,1:T(8,128)(2,1)}), bf16[128,4,1,128]{3,0,2,1:T(8,128)(2,1)S(1)}, u32[]{:S(2)}, u32[]{:S(2)}) async-start(bf16[128,4,1,128]{3,0,2,1:T(8,128)(2,1)} %bitcast.4), calls=%async_computation.1 | async-start | bytes 262144 | tf_op jit(solution)/shard_map/all_to_all | solution.py:102
  15.1 0.2 select_reduce_fusion.1
  15.3 0.1 reduce_sum.40
  15.3 0.1 copy.126
  15.4 4.3 %all-to-all-done.1 = bf16[128,4,1,128]{3,0,2,1:T(8,128)(2,1)S(1)} async-done(((bf16[128,4,1,128]{3,0,2,1:T(8,128)(2,1)}), bf16[128,4,1,128]{3,0,2,1:T(8,128)(2,1)S(1)}, u32[]{:S(2)}, u32[]{:S(2)}) %all-to-all-start.1) | async-done | bytes 131104 | tf_op jit(solution)/shard_map/all_to_all | solution.py:102
  19.7 3.5 %all-to-all-start = ((bf16[128,4,4,128]{3,0,2,1:T(8,128)(2,1)}), bf16[128,4,4,128]{3,0,2,1:T(8,128)(2,1)S(1)}, u32[]{:S(2)}, u32[]{:S(2)}) async-start(bf16[128,4,4,128]{3,0,2,1:T(8,128)(2,1)} %copy.118), calls=%async_computation | async-start | bytes 1048576 | tf_op jit(solution)/shard_map/all_to_all | solution.py:101
  23.2 0.1 copy.127
  23.3 0.1 copy.128
  23.3 0.1 convert_reduce_fusion
  23.5 0.4 convolution_convert_fusion.1
  23.9 0.5 reshape.40
  24.4 1.5 %copy.129 = bf16[8,8,3,2048]{3,1,2,0:T(8,128)(2,1)} copy(bf16[8,8,3,2048]{3,2,1,0:T(4,128)(2,1)S(1)} %reshape.40) | data formatting | bytes 1572864 | tf_op jit(solution)/shard_map/reshape | solution.py:125
  25.9 6.1 %all-to-all-done = bf16[128,4,4,128]{3,0,2,1:T(8,128)(2,1)S(1)} async-done(((bf16[128,4,4,128]{3,0,2,1:T(8,128)(2,1)}), bf16[128,4,4,128]{3,0,2,1:T(8,128)(2,1)S(1)}, u32[]{:S(2)}, u32[]{:S(2)}) %all-to-all-start) | async-done | bytes 524320 | tf_op jit(solution)/shard_map/all_to_all | solution.py:101
  32.0 6.4 %all-to-all-start.4 = ((bf16[8,8,3,2048]{3,1,2,0:T(8,128)(2,1)}), bf16[8,8,3,2048]{3,1,2,0:T(8,128)(2,1)S(1)}, u32[]{:S(2)}, u32[]{:S(2)}) async-start(bf16[8,8,3,2048]{3,1,2,0:T(8,128)(2,1)} %copy.129), calls=%async_computation.4 | async-start | bytes 1572864 | tf_op jit(solution)/shard_map/all_to_all | solution.py:124
  38.3 1.7 %convolution_convert_fusion = bf16[192,2048]{1,0:T(8,128)(2,1)S(1)} fusion(f32[192,16]{0,1:T(8,128)S(1)} %get-tuple-element.4, bf16[1,16,2048]{2,1,0:T(8,128)(2,1)} %param.16), kind=kOutput, calls=%fused_computation.21 | convolution fusion | flops 75890688 | bytes 864256 | tf_op jit(solution)/shard_map/dot_general | solution.py:116
  40.0 0.5 reshape.42
  40.5 1.5 %copy.134 = bf16[8,8,3,2048]{3,1,2,0:T(8,128)(2,1)} copy(bf16[8,8,3,2048]{3,2,1,0:T(4,128)(2,1)S(1)} %reshape.42) | data formatting | bytes 1572864 | tf_op jit(solution)/shard_map/reshape | solution.py:128
  42.0 0.1 iota_compare_fusion
  42.1 0.9 bitcast_reduce_fusion
  43.0 0.9 fusion.13
  43.9 1.3 fusion.49
  45.2 1.2 copy.123
  46.4 11.9 %all-to-all-done.4 = bf16[8,8,3,2048]{3,1,2,0:T(8,128)(2,1)S(1)} async-done(((bf16[8,8,3,2048]{3,1,2,0:T(8,128)(2,1)}), bf16[8,8,3,2048]{3,1,2,0:T(8,128)(2,1)S(1)}, u32[]{:S(2)}, u32[]{:S(2)}) %all-to-all-start.4) | async-done | bytes 786464 | tf_op jit(solution)/shard_map/all_to_all | solution.py:124
  58.4 3.7 %all-to-all-start.6 = ((bf16[8,8,3,2048]{3,1,2,0:T(8,128)(2,1)}), bf16[8,8,3,2048]{3,1,2,0:T(8,128)(2,1)S(1)}, u32[]{:S(2)}, u32[]{:S(2)}) async-start(bf16[8,8,3,2048]{3,1,2,0:T(8,128)(2,1)} %copy.134), calls=%async_computation.6 | async-start | bytes 1572864 | tf_op jit(solution)/shard_map/all_to_all | solution.py:127
  62.1 0.0 slice-start
  62.1 0.0 slice-start.1
  62.1 6.8 %fusion.44 = f32[8,8,3,384]{3,0,2,1:T(8,128)S(1)} fusion(bf16[8,2048,384]{2,1,0:T(8,128)(2,1)} %param.18, bf16[8,8,3,2048]{3,1,2,0:T(8,128)(2,1)S(1)} %all-to-all-done.4), kind=kOutput, calls=%fused_computation.34 | convolution fusion | flops 301989888 | bytes 13664256 | tf_op jit(solution)/shard_map/secd,edf->secf/dot_general | solution.py:66
  68.9 0.0 slice-start.2
  68.9 6.8 %fusion.41 = f32[8,8,3,384]{3,0,2,1:T(8,128)S(1)} fusion(bf16[8,2048,384]{2,1,0:T(8,128)(2,1)} %param.17, bf16[8,8,3,2048]{3,1,2,0:T(8,128)(2,1)S(1)} %all-to-all-done.4), kind=kOutput, calls=%fused_computation.33 | convolution fusion | flops 301989888 | bytes 13664256 | tf_op jit(solution)/shard_map/secd,edf->secf/dot_general | solution.py:65
  75.7 1.8 %fusion.24 = bf16[8,8,3,2048]{3,0,2,1:T(8,128)(2,1)S(1)} fusion(bf16[8,384,2048]{2,1,0:T(8,128)(2,1)S(1)} %bitcast.120, f32[8,8,3,384]{3,0,2,1:T(8,128)S(1)} %fusion.44, f32[8,8,3,384]{3,0,2,1:T(8,128)S(1)} %fusion.41), kind=kOutput, calls=%fused_computation.23 | convolution fusion | flops 302825472 | bytes 13959168 | tf_op jit(solution)/shard_map/secf,efd->secd/dot_general | solution.py:70
  77.5 1.3 copy.132
  78.8 3.4 %all-to-all-done.6 = bf16[8,8,3,2048]{3,1,2,0:T(8,128)(2,1)S(1)} async-done(((bf16[8,8,3,2048]{3,1,2,0:T(8,128)(2,1)}), bf16[8,8,3,2048]{3,1,2,0:T(8,128)(2,1)S(1)}, u32[]{:S(2)}, u32[]{:S(2)}) %all-to-all-start.6) | async-done | bytes 786464 | tf_op jit(solution)/shard_map/all_to_all | solution.py:127
  82.2 3.5 %all-to-all-start.3 = ((bf16[512,1,4,128]{3,2,1,0:T(4,128)(2,1)}), bf16[512,1,4,128]{3,2,1,0:T(4,128)(2,1)S(1)}, u32[]{:S(2)}, u32[]{:S(2)}) async-start(bf16[512,1,4,128]{3,2,1,0:T(4,128)(2,1)} %copy.123), calls=%async_computation.3 | async-start | bytes 1048576 | tf_op jit(solution)/shard_map/all_to_all | solution.py:108
  85.7 7.9 %fusion.38 = f32[8,8,3,384]{3,0,2,1:T(8,128)S(1)} fusion(bf16[8,384,2048]{2,1,0:T(8,128)(2,1)} %param.19, bf16[8,8,3,2048]{3,1,2,0:T(8,128)(2,1)S(1)} %all-to-all-done.6), kind=kOutput, calls=%fused_computation.32 | convolution fusion | flops 301989888 | bytes 13664256 | tf_op jit(solution)/shard_map/secd,efd->secf/dot_general | solution.py:73
  93.7 0.9 all-to-all-done.3
  94.5 3.8 %all-to-all-start.5 = ((bf16[8,8,3,2048]{3,1,2,0:T(8,128)(2,1)}), bf16[8,8,3,2048]{3,1,2,0:T(8,128)(2,1)S(1)}, u32[]{:S(2)}, u32[]{:S(2)}) async-start(bf16[8,8,3,2048]{3,1,2,0:T(8,128)(2,1)} %copy.132), calls=%async_computation.5 | async-start | bytes 1572864 | tf_op jit(solution)/shard_map/all_to_all | solution.py:133
  98.3 7.9 %fusion = f32[8,8,3,2048]{3,1,2,0:T(8,128)S(1)} fusion(bf16[8,2048,384]{2,1,0:T(8,128)(2,1)} %param.18, f32[8,8,3,384]{3,0,2,1:T(8,128)S(1)} %fusion.38, f32[8,8,3,384]{3,0,2,1:T(8,128)S(1)} %fusion.41), kind=kOutput, calls=%fused_computation | convolution fusion | flops 302432256 | bytes 14745600 | tf_op jit(solution)/shard_map/secf,edf->secd/dot_general | solution.py:79
  106.2 7.9 %fusion.27 = bf16[8,8,3,2048]{3,0,2,1:T(8,128)(2,1)S(1)} fusion(f32[8,8,3,2048]{3,1,2,0:T(8,128)S(1)} %fusion, bf16[8,2048,384]{2,1,0:T(8,128)(2,1)} %param.17, f32[8,8,3,384]{3,0,2,1:T(8,128)S(1)} %fusion.41, f32[8,8,3,384]{3,0,2,1:T(8,128)S(1)} %fusion.38, f32[8,8,3,384]{3,0,2,1:T(8,128)S(1)} %fusion.44), kind=kOutput, calls=%fused_computation.24 | convolution fusion | flops 303513600 | bytes 15826944 | tf_op jit(solution)/shard_map/secf,edf->secd/dot_general | solution.py:78
  114.2 1.4 copy.136
  115.5 2.7 %all-to-all-done.5 = bf16[8,8,3,2048]{3,1,2,0:T(8,128)(2,1)S(1)} async-done(((bf16[8,8,3,2048]{3,1,2,0:T(8,128)(2,1)}), bf16[8,8,3,2048]{3,1,2,0:T(8,128)(2,1)S(1)}, u32[]{:S(2)}, u32[]{:S(2)}) %all-to-all-start.5) | async-done | bytes 786464 | tf_op jit(solution)/shard_map/all_to_all | solution.py:133
  118.2 3.6 %all-to-all-start.7 = ((bf16[8,8,3,2048]{3,1,2,0:T(8,128)(2,1)}), bf16[8,8,3,2048]{3,1,2,0:T(8,128)(2,1)S(1)}, u32[]{:S(2)}, u32[]{:S(2)}) async-start(bf16[8,8,3,2048]{3,1,2,0:T(8,128)(2,1)} %copy.136), calls=%async_computation.7 | async-start | bytes 1572864 | tf_op jit(solution)/shard_map/all_to_all | solution.py:134
  121.8 0.2 copy.124
  122.0 1.2 reshape.39
  123.2 0.7 copy.133
  123.9 0.7 reshape.41
  124.6 1.1 fusion.30
  125.6 16.6 %all-to-all-done.7 = bf16[8,8,3,2048]{3,1,2,0:T(8,128)(2,1)S(1)} async-done(((bf16[8,8,3,2048]{3,1,2,0:T(8,128)(2,1)}), bf16[8,8,3,2048]{3,1,2,0:T(8,128)(2,1)S(1)}, u32[]{:S(2)}, u32[]{:S(2)}) %all-to-all-start.7) | async-done | bytes 786464 | tf_op jit(solution)/shard_map/all_to_all | solution.py:134
  142.2 0.7 copy.137
  142.9 0.7 reshape.43
  143.6 1.1 fusion.31
  (12 shorter events, 0.1 us)
Async XLA Ops:
  0.6 22.9 %copy-start = (bf16[1,16,2048]{2,1,0:T(8,128)(2,1)S(1)}, bf16[1,16,2048]{2,1,0:T(8,128)(2,1)}, u32[]{:S(2)}) copy-start(bf16[1,16,2048]{2,1,0:T(8,128)(2,1)} %param.13) | copy-start | bytes 196612
  0.6 22.5 %copy-start.1 = (s32[1,16,8]{1,2,0:T(8,128)S(1)}, s32[1,16,8]{1,2,0:T(8,128)}, u32[]{:S(2)}) copy-start(s32[1,16,8]{1,2,0:T(8,128)} %param.14) | copy-start | bytes 1540
  0.7 22.6 %copy-start.2 = (f32[1,16,8]{1,2,0:T(8,128)S(1)}, f32[1,16,8]{1,2,0:T(8,128)}, u32[]{:S(2)}) copy-start(f32[1,16,8]{1,2,0:T(8,128)} %param.15) | copy-start | bytes 1540
  2.2 8.8 %all-to-all-start.2 = ((bf16[128,4,1,128]{3,0,2,1:T(8,128)(2,1)}), bf16[128,4,1,128]{3,0,2,1:T(8,128)(2,1)S(1)}, u32[]{:S(2)}, u32[]{:S(2)}) async-start(bf16[128,4,1,128]{3,0,2,1:T(8,128)(2,1)} %bitcast.10), calls=%async_computation.2 | async-start | bytes 262144 | tf_op jit(solution)/shard_map/all_to_all | solution.py:103
  11.7 7.9 %all-to-all-start.1 = ((bf16[128,4,1,128]{3,0,2,1:T(8,128)(2,1)}), bf16[128,4,1,128]{3,0,2,1:T(8,128)(2,1)S(1)}, u32[]{:S(2)}, u32[]{:S(2)}) async-start(bf16[128,4,1,128]{3,0,2,1:T(8,128)(2,1)} %bitcast.4), calls=%async_computation.1 | async-start | bytes 262144 | tf_op jit(solution)/shard_map/all_to_all | solution.py:102
  19.7 12.3 %all-to-all-start = ((bf16[128,4,4,128]{3,0,2,1:T(8,128)(2,1)}), bf16[128,4,4,128]{3,0,2,1:T(8,128)(2,1)S(1)}, u32[]{:S(2)}, u32[]{:S(2)}) async-start(bf16[128,4,4,128]{3,0,2,1:T(8,128)(2,1)} %copy.118), calls=%async_computation | async-start | bytes 1048576 | tf_op jit(solution)/shard_map/all_to_all | solution.py:101
  32.0 26.4 %all-to-all-start.4 = ((bf16[8,8,3,2048]{3,1,2,0:T(8,128)(2,1)}), bf16[8,8,3,2048]{3,1,2,0:T(8,128)(2,1)S(1)}, u32[]{:S(2)}, u32[]{:S(2)}) async-start(bf16[8,8,3,2048]{3,1,2,0:T(8,128)(2,1)} %copy.129), calls=%async_computation.4 | async-start | bytes 1572864 | tf_op jit(solution)/shard_map/all_to_all | solution.py:124
  58.4 23.9 %all-to-all-start.6 = ((bf16[8,8,3,2048]{3,1,2,0:T(8,128)(2,1)}), bf16[8,8,3,2048]{3,1,2,0:T(8,128)(2,1)S(1)}, u32[]{:S(2)}, u32[]{:S(2)}) async-start(bf16[8,8,3,2048]{3,1,2,0:T(8,128)(2,1)} %copy.134), calls=%async_computation.6 | async-start | bytes 1572864 | tf_op jit(solution)/shard_map/all_to_all | solution.py:127
  62.1 13.6 %slice-start = ((s8[12582912]{0:T(1024)(128)(4,1)}), s8[4194304]{0:T(1024)(128)(4,1)S(1)}, s32[]{:S(2)}) async-start(s8[12582912]{0:T(1024)(128)(4,1)} %bitcast.119), calls=%async_computation.8 | async-start | bytes 8388608
  62.1 13.6 %slice-start.1 = ((s8[12582912]{0:T(1024)(128)(4,1)}), s8[4194304]{0:T(1024)(128)(4,1)S(1)}, s32[]{:S(2)}) async-start(s8[12582912]{0:T(1024)(128)(4,1)} %bitcast.119), calls=%async_computation.9 | async-start | bytes 8388608
  68.9 6.8 %slice-start.2 = ((s8[12582912]{0:T(1024)(128)(4,1)}), s8[4194304]{0:T(1024)(128)(4,1)S(1)}, s32[]{:S(2)}) async-start(s8[12582912]{0:T(1024)(128)(4,1)} %bitcast.119), calls=%async_computation.10 | async-start | bytes 8388608
  82.2 12.3 %all-to-all-start.3 = ((bf16[512,1,4,128]{3,2,1,0:T(4,128)(2,1)}), bf16[512,1,4,128]{3,2,1,0:T(4,128)(2,1)S(1)}, u32[]{:S(2)}, u32[]{:S(2)}) async-start(bf16[512,1,4,128]{3,2,1,0:T(4,128)(2,1)} %copy.123), calls=%async_computation.3 | async-start | bytes 1048576 | tf_op jit(solution)/shard_map/all_to_all | solution.py:108
  94.5 23.7 %all-to-all-start.5 = ((bf16[8,8,3,2048]{3,1,2,0:T(8,128)(2,1)}), bf16[8,8,3,2048]{3,1,2,0:T(8,128)(2,1)S(1)}, u32[]{:S(2)}, u32[]{:S(2)}) async-start(bf16[8,8,3,2048]{3,1,2,0:T(8,128)(2,1)} %copy.132), calls=%async_computation.5 | async-start | bytes 1572864 | tf_op jit(solution)/shard_map/all_to_all | solution.py:133
  118.2 24.0 %all-to-all-start.7 = ((bf16[8,8,3,2048]{3,1,2,0:T(8,128)(2,1)}), bf16[8,8,3,2048]{3,1,2,0:T(8,128)(2,1)S(1)}, u32[]{:S(2)}, u32[]{:S(2)}) async-start(bf16[8,8,3,2048]{3,1,2,0:T(8,128)(2,1)} %copy.136), calls=%async_computation.7 | async-start | bytes 1572864 | tf_op jit(solution)/shard_map/all_to_all | solution.py:134
where the time goes:
time: 146 us; the launch traced here: 145 us
  waiting for transfers between devices  46.2 us (32%)
  matrix products  45.4 us (31%)
  starting transfers between devices  31.9 us (22%)
  local copies, waits for them, and re-layouts  18.6 us (13%)
  other arithmetic  1.57 us (1%)
    all_to_all x1, waiting for transfers between devices, shards(): lax.all_to_all(input_grad, ('seq', 'tp'), split_axis=0, concat_axis=0, ti...  16.6 us
    all_to_all x1, waiting for transfers between devices, shards(): lax.all_to_all(send_rows.reshape(buffer_shape), ('seq', 'tp'), split_axis...  11.9 us
    dot_general x1, matrix products, expert_math(): jnp.einsum('secf,edf->secd', grad_gate, w_gate, preferred_element_type=jn...  7.94 us
    dot_general x1, matrix products, expert_math(): jnp.einsum('secd,efd->secf', grad_rows, w_down, preferred_element_type=jn...  7.93 us
    dot_general x1, matrix products, expert_math(): jnp.einsum('secf,edf->secd', grad_up, w_up, preferred_element_type=jnp.fl...  7.93 us
    dot_general x1, matrix products, expert_math(): jnp.einsum('secd,edf->secf', token_rows, w_gate, preferred_element_type=j...  6.76 us
    dot_general x1, matrix products, expert_math(): jnp.einsum('secd,edf->secf', token_rows, w_up, preferred_element_type=jnp...  6.76 us
    all_to_all x1, starting transfers between devices, shards(): lax.all_to_all(send_rows.reshape(buffer_shape), ('seq', 'tp'), split_axis...  6.37 us
  transfers between devices with their start and end apart: 8, of which 8 were waited for; matrix products, arithmetic and copies ran while one was open for 42% of the time, Pallas kernels for 0%

commit v1 on v0

v1 whole, which is shorter than its diff:
```python
import functools

import jax
import jax.numpy as jnp
from jax import lax
from jax.experimental import pallas as pl
from jax.experimental.pallas import tpu as pltpu
from jax.sharding import PartitionSpec as P

H = 32
KVH = 4
HD = 128
EXPERTS = 64
NT = (((1,), (1,)), ((), ()))
VMEM = pl.BlockSpec(memory_space=pltpu.VMEM)
SMEM = pl.BlockSpec(memory_space=pltpu.SMEM)
F32 = jnp.float32
BF16 = jnp.bfloat16


def swap(array, axis, offset):
    count = lax.axis_size(axis)
    return lax.ppermute(array, axis, [(i, i ^ offset) for i in range(count)])


def pack_kernel(ids_ref, gates_ref, x_ref, out_ref):
    rows, width = x_ref.shape
    topk = ids_ref.shape[0]
    expert = lax.broadcasted_iota(jnp.int32, (EXPERTS, rows), 0)
    table = jnp.zeros((EXPERTS, rows), F32)
    for k in range(topk):
        table = table + jnp.where(ids_ref[k : k + 1] == expert, gates_ref[k : k + 1], 0.0)
    high = table.astype(BF16).astype(F32)
    low = table - high
    both = jnp.concatenate([high, low], axis=0)
    out_ref[:, :width] = x_ref[...]
    out_ref[:, width:] = jnp.transpose(both).astype(BF16)


def pack_rows(ids, gates, x):
    rows, width = x.shape
    return pl.pallas_call(
        pack_kernel,
        in_specs=[VMEM] * 3,
        out_specs=VMEM,
        out_shape=jax.ShapeDtypeStruct((rows, width + 2 * EXPERTS), BF16),
        name="pack_rows",
    )(ids, gates, x)


def attention_kernel(base_ref, q_ref, *refs):
    out_ref = refs[-1]
    kv_refs = refs[:-1]
    rows, width = q_ref.shape
    half = kv_refs[0].shape[1] // 2
    kv_heads = half // HD
    heads = width // HD
    repeat = heads // kv_heads
    scale = 1.0 / HD**0.5
    pieces = len(kv_refs)
    row_pos = base_ref[0] * rows + lax.broadcasted_iota(jnp.int32, (rows, rows), 0)
    col_pos = lax.broadcasted_iota(jnp.int32, (rows, rows), 1)
    bias = jnp.concatenate(
        [
            jnp.where(col_pos + base_ref[p] * rows <= row_pos, 0.0, -jnp.inf)
            for p in range(pieces)
        ],
        axis=1,
    )
    for g in range(kv_heads):
        keys = jnp.concatenate([r[:, g * HD : (g + 1) * HD] for r in kv_refs], axis=0)
        vals = jnp.concatenate(
            [r[:, half + g * HD : half + (g + 1) * HD] for r in kv_refs], axis=0
        )
        for h in range(g * repeat, (g + 1) * repeat):
            cols = slice(h * HD, (h + 1) * HD)
            scores = lax.dot_general(q_ref[:, cols], keys, NT, preferred_element_type=F32)
            scores = scores * scale + bias
            top = jnp.max(scores, axis=1, keepdims=True)
            exps = jnp.exp(scores - top)
            total = jnp.sum(exps, axis=1, keepdims=True)
            mixed = jnp.dot(exps.astype(BF16), vals, preferred_element_type=F32)
            out_ref[:, cols] = (mixed / total).astype(BF16)


def attend(base, q, kv):
    rows, width = q.shape
    keys = rows * len(kv)
    return pl.pallas_call(
        attention_kernel,
        in_specs=[SMEM] + [VMEM] * (1 + len(kv)),
        out_specs=VMEM,
        out_shape=jax.ShapeDtypeStruct((rows, width), BF16),
        cost_estimate=pl.CostEstimate(
            flops=4 * rows * keys * width, bytes_accessed=4 * rows * width, transcendentals=0
        ),
        name="attention",
    )(base, q, *kv)


def forward_kernel(shard_ref, *refs, count):
    x_refs = refs[:count]
    gate_ref, up_ref, down_ref = refs[count : count + 3]
    outs = refs[count + 3 : 2 * count + 3]
    silu_ref, rest_ref = refs[2 * count + 3 : 2 * count + 5]
    rows_scr, gates_scr, act_scr = refs[-3:]
    local, width, _ = gate_ref.shape
    piece = x_refs[0].shape[0]
    tokens = count * piece
    for p in range(count):
        rows_scr[p * piece : (p + 1) * piece] = x_refs[p][:, :width]
        gates_scr[p * piece : (p + 1) * piece] = x_refs[p][:, width:]
    lane = lax.broadcasted_iota(jnp.int32, gates_scr.shape, 1)

    @pl.loop(0, local)
    def _(e):
        col = shard_ref[0] * local + e
        gates = gates_scr[...].astype(F32)
        mine = jnp.sum(
            jnp.where((lane == col) | (lane == col + EXPERTS), gates, 0.0), axis=1, keepdims=True
        )
        hgate = jnp.dot(rows_scr[...], gate_ref[e], preferred_element_type=F32)
        hup = jnp.dot(rows_scr[...], up_ref[e], preferred_element_type=F32)
        sig = jax.nn.sigmoid(hgate)
        silu = hgate * sig * mine
        silu_ref[e] = silu
        rest_ref[e] = hup * sig * (1.0 + hgate * (1.0 - sig)) * mine
        act_scr[e] = (silu * hup).astype(BF16)

    chunk = 256

    @pl.loop(0, width // chunk)
    def _(c):
        cols = pl.ds(pl.multiple_of(c * chunk, chunk), chunk)
        total = jnp.zeros((tokens, chunk), F32)
        for e in range(local):
            total = total + jnp.dot(act_scr[e], down_ref[e, :, cols], preferred_element_type=F32)
        total = total.astype(BF16)
        for p in range(count):
            outs[p][:, cols] = total[p * piece : (p + 1) * piece]


def experts_forward(shard, pieces, w_gate, w_up, w_down):
    count = len(pieces)
    local, width, hidden = w_gate.shape
    piece = pieces[0].shape[0]
    tokens = count * piece
    shapes = [jax.ShapeDtypeStruct((piece, width), BF16)] * count
    shapes += [jax.ShapeDtypeStruct((local, tokens, hidden), F32)] * 2
    shapes += [jax.ShapeDtypeStruct(w.shape, w.dtype) for w in (w_gate, w_up, w_down)]

    def body(shard_ref, *refs):
        ins, outs = refs[: count + 3], refs[count + 3 : 2 * count + 5]
        forward_kernel(shard_ref, *ins, *outs, *refs[-3:], count=count)

    res = pl.pallas_call(
        body,
        in_specs=[SMEM] + [VMEM] * (count + 3),
        out_specs=[VMEM] * (count + 5),
        out_shape=shapes,
        input_output_aliases={1 + count + i: count + 2 + i for i in range(3)},
        scratch_shapes=[
            pltpu.VMEM((tokens, width), BF16),
            pltpu.VMEM((tokens, pieces[0].shape[1] - width), BF16),
            pltpu.VMEM((local, tokens, hidden), BF16),
        ],
        compiler_params=pltpu.CompilerParams(vmem_limit_bytes=16 * 2**20),
        cost_estimate=pl.CostEstimate(
            flops=6 * tokens * local * width * hidden,
            bytes_accessed=6 * local * width * hidden,
            transcendentals=0,
        ),
        name="experts_forward",
    )(shard, *pieces, w_gate, w_up, w_down)
    return res[:count], res[count], res[count + 1], res[count + 2 :]


def backward_kernel(*refs, count):
    g_refs = refs[:count]
    gate_ref, up_ref, down_ref, silu_ref, rest_ref = refs[count : count + 5]
    outs = refs[count + 5 : 2 * count + 5]
    rows_scr, gate_scr, up_scr = refs[-3:]
    local, width, _ = gate_ref.shape
    piece = g_refs[0].shape[0]
    tokens = count * piece
    for p in range(count):
        rows_scr[p * piece : (p + 1) * piece] = g_refs[p][...]

    @pl.loop(0, local)
    def _(e):
        grad_act = lax.dot_general(rows_scr[...], down_ref[e], NT, preferred_element_type=F32)
        gate_scr[e] = (grad_act * rest_ref[e]).astype(BF16)
        up_scr[e] = (grad_act * silu_ref[e]).astype(BF16)

    chunk = 256

    @pl.loop(0, width // chunk)
    def _(c):
        cols = pl.ds(pl.multiple_of(c * chunk, chunk), chunk)
        total = jnp.zeros((tokens, chunk), F32)
        for e in range(local):
            total = total + lax.dot_general(
                gate_scr[e], gate_ref[e, cols, :], NT, preferred_element_type=F32
            )
            total = total + lax.dot_general(
                up_scr[e], up_ref[e, cols, :], NT, preferred_element_type=F32
            )
        total = total.astype(BF16)
        for p in range(count):
            outs[p][:, cols] = total[p * piece : (p + 1) * piece]


def experts_backward(pieces, weights, silu, rest):
    count = len(pieces)
    local, width, hidden = weights[0].shape
    piece = pieces[0].shape[0]
    tokens = count * piece
    return pl.pallas_call(
        functools.partial(backward_kernel, count=count),
        in_specs=[VMEM] * (count + 5),
        out_specs=[VMEM] * count,
        out_shape=[jax.ShapeDtypeStruct((piece, width), BF16)] * count,
        scratch_shapes=[
            pltpu.VMEM((tokens, width), BF16),
            pltpu.VMEM((local, tokens, hidden), BF16),
            pltpu.VMEM((local, tokens, hidden), BF16),
        ],
        compiler_params=pltpu.CompilerParams(vmem_limit_bytes=16 * 2**20),
        cost_estimate=pl.CostEstimate(
            flops=6 * tokens * local * width * hidden,
            bytes_accessed=6 * local * width * hidden,
            transcendentals=0,
        ),
        name="experts_backward",
    )(*pieces, *weights, silu, rest)


def spread(rows):
    near = [rows] + [swap(rows, "seq", d) for d in range(1, lax.axis_size("seq"))]
    pieces = list(near)
    for t in range(1, lax.axis_size("tp")):
        pieces += [swap(a, "tp", t) for a in near]
    return pieces


def collect(pieces):
    seq, tp = lax.axis_size("seq"), lax.axis_size("tp")
    sums = []
    for d in range(seq):
        terms = [pieces[d]] + [swap(pieces[t * seq + d], "tp", t) for t in range(1, tp)]
        total = sum(a.astype(F32) for a in terms)
        sums.append(total if d == 0 else swap(total.astype(BF16), "seq", d).astype(F32))
    return sum(sums).astype(BF16)


def shards(queries, keys, values, moe_x, expert_ids, gates, grad_out, w_gate, w_up, w_down):
    group = lax.axis_index("group")
    weights = [pltpu.with_memory_space_constraint(w, pltpu.VMEM) for w in (w_gate, w_up, w_down)]
    shard = (lax.axis_index("seq") * lax.axis_size("tp") + lax.axis_index("tp")).reshape(1)
    x_pieces = spread(pack_rows(expert_ids[0].T, gates[0].T, moe_x[0]))
    g_pieces = spread(grad_out[0])
    kv = jnp.concatenate([keys[0], values[0]], axis=1)
    offsets = range(lax.axis_size("group"))
    kv_pieces = [kv] + [swap(kv, "group", d) for d in offsets[1:]]
    base = jnp.stack([group ^ d for d in offsets])
    attn_out = attend(base, queries[0], kv_pieces)
    outs, silu, rest, weights = experts_forward(shard, x_pieces, *weights)
    moe_out = collect(outs)
    moe_grad_in = collect(experts_backward(g_pieces, weights, silu, rest))
    return attn_out[None], moe_out[None], moe_grad_in[None]


def solution(mesh):
    rows = P("seq", "group", "tp")
    tokens = P("group", ("seq", "tp"), None)
    experts = P(("seq", "tp"), None, None)
    return jax.shard_map(
        shards,
        mesh=mesh,
        in_specs=(rows, rows, rows, tokens, tokens, tokens, tokens, experts, experts, experts),
        out_specs=(rows, tokens, tokens),
        check_vma=False,
    )
```

time: 146 us -> 158 us (1.082)
  local copies, waits for them, and re-layouts: 18.6 us -> 66.5 us
  matrix products: 45.4 us -> 0 us
  waiting for transfers between devices: 46.2 us -> 9.24 us
  Pallas kernels: 0 us -> 36.6 us
  starting transfers between devices: 31.9 us -> 42.6 us
    unnamed x14 -> x47, local copies, waits for them, and re-layouts: 2.11 us -> 66.5 us
    all_to_all x8 -> x0, waiting for transfers between devices: 46.2 us -> none  [the longest x1 16.6 us: shards(): lax.all_to_all(input_grad, ('seq', 'tp'), split_axis=0, concat_axis=0, ti...]
    dot_general x12 -> x0, matrix products: 45.4 us -> none  [the longest x1 7.94 us: expert_math(): jnp.einsum('secf,edf->secd', grad_gate, w_gate, preferred_element_type=jn...]
    ppermute x0 -> x31, starting transfers between devices: none -> 42.6 us  [swap(): return lax.ppermute(array, axis, [(i, i ^ offset) for i in range(count)])]
    pallas_call x0 -> x4, Pallas kernels: none -> 36.6 us  [the longest x1 17.7 us: experts_backward(): pl.pallas_call(functools.partial(backward_kernel, count=count), in_specs=...]
    all_to_all x8 -> x0, starting transfers between devices: 31.9 us -> none  [the longest x1 6.37 us: shards(): lax.all_to_all(send_rows.reshape(buffer_shape), ('seq', 'tp'), split_axis...]
    ppermute x0 -> x31, waiting for transfers between devices: none -> 9.24 us  [swap(): return lax.ppermute(array, axis, [(i, i ^ offset) for i in range(count)])]
    reshape x7 -> x0, local copies, waits for them, and re-layouts: 6.56 us -> none  [the longest x2 2.01 us: shards(): send_grads.reshape(buffer_shape)]
  transfers between devices with their start and end apart: 8 -> 31, of which waited for: 8 -> 8; matrix products, arithmetic and copies ran while one was open for 42% -> 1% of each run, Pallas kernels for 0% -> 22%
where the time goes in v1:
time: 158 us
  local copies, waits for them, and re-layouts  66.5 us (42%)
  starting transfers between devices  42.6 us (27%)
  Pallas kernels  36.6 us (23%)
  waiting for transfers between devices  9.24 us (6%)
  other arithmetic  2.04 us (1%)
    unnamed x47, local copies, waits for them, and re-layouts  66.5 us
    ppermute x31, starting transfers between devices, swap(): return lax.ppermute(array, axis, [(i, i ^ offset) for i in range(count)])  42.6 us
    pallas_call x1, Pallas kernels, experts_backward(): pl.pallas_call(functools.partial(backward_kernel, count=count), in_specs=...  17.7 us
    pallas_call x1, Pallas kernels, experts_forward(): pl.pallas_call(body, in_specs=[SMEM] + [VMEM] * (count + 3), out_specs=[V...  11 us
    ppermute x31, waiting for transfers between devices, swap(): return lax.ppermute(array, axis, [(i, i ^ offset) for i in range(count)])  9.24 us
    pallas_call x1, Pallas kernels, attend(): pl.pallas_call(attention_kernel, in_specs=[SMEM] + [VMEM] * (1 + len(kv))...  6.36 us
  transfers between devices with their start and end apart: 31, of which 8 were waited for; matrix products, arithmetic and copies ran while one was open for 1% of the time, Pallas kernels for 22%

profile of v1, /device:TPU:0, one launch (start us, length us, event | category | flops | bytes accessed | tf_op | source)
XLA Modules:
  0.0 157.8 jit_solution(14976909434018968597)
XLA Ops:
  0.6 0.0 slice-start
  0.7 0.0 slice-start.1
  0.7 12.3 %copy.22.refs_8_ = bf16[8,2048,384]{2,1,0:T(8,128)(2,1)} copy(bf16[8,2048,384]{2,1,0:T(8,128)(2,1)} %param.17) | data formatting | bytes 25165824
  13.0 6.4 %copy.23.refs_9_ = bf16[8,2048,384]{2,1,0:T(8,128)(2,1)} copy(bf16[8,2048,384]{2,1,0:T(8,128)(2,1)S(1)} %copy-done.12) | data formatting | bytes 25165824
  19.4 1.1 slice-done.1
  20.5 1.3 slice-done.2
  21.8 4.6 %copy.24.refs_10_ = bf16[8,384,2048]{2,1,0:T(8,128)(2,1)} copy(bf16[8,384,2048]{2,1,0:T(8,128)(2,1)S(1)} %bitcast.27) | data formatting | bytes 25165824
  26.4 1.6 %pack_rows.1.refs_0_ = bf16[16,2176]{1,0:T(8,128)(2,1)} custom-call(s32[8,16]{1,0:T(8,128)} %bitcast.31, f32[8,16]{1,0:T(8,128)} %bitcast.32, bf16[16,2048]{1,0:T(8,128)(2,1)} %bitcast.28), custom_call_target="tpu_custom_call" | custom-call | tf_op jit(solution)/shard_map/pack_rows/pallas_call | solution.py:42
  28.0 3.0 %collective-permute-start.3 = (bf16[16,2176]{1,0:T(8,128)(2,1)}, bf16[16,2176]{1,0:T(8,128)(2,1)S(1)}, u32[]{:S(2)}, u32[]{:S(2)}) collective-permute-start(bf16[16,2176]{1,0:T(8,128)(2,1)} %pack_rows.1.refs_0_), channel_id=1, source_target_pairs={{0,2},{2,0},{4,6},{6,4},{1,3},{3,1},{5,7},{7,5},{8,10},{10,8},{12,... | collective-permute-start | bytes 208904 | tf_op jit(solution)/shard_map/ppermute | solution.py:23
  31.0 2.6 %collective-permute-start.4 = (bf16[16,2176]{1,0:T(8,128)(2,1)}, bf16[16,2176]{1,0:T(8,128)(2,1)S(1)}, u32[]{:S(2)}, u32[]{:S(2)}) collective-permute-start(bf16[16,2176]{1,0:T(8,128)(2,1)} %pack_rows.1.refs_0_), channel_id=1, source_target_pairs={{0,4},{2,6},{4,0},{6,2},{1,5},{3,7},{5,1},{7,3},{8,12},{10,14},{12... | collective-permute-start | bytes 208904 | tf_op jit(solution)/shard_map/ppermute | solution.py:23
  33.6 0.9 collective-permute-start.17
  34.5 3.5 %collective-permute-start.18 = (bf16[16,2048]{1,0:T(8,128)(2,1)S(1)}, bf16[16,2048]{1,0:T(8,128)(2,1)S(1)}, u32[]{:S(2)}, u32[]{:S(2)}) collective-permute-start(bf16[16,2048]{1,0:T(8,128)(2,1)S(1)} %bitcast.22), channel_id=1, source_target_pairs={{0,4},{2,6},{4,0},{6,2},{1,5},{3,7},{5,1},{7,3},{8,12},{10,14},{12... | collective-permute-start | bytes 196616 | tf_op jit(solution)/shard_map/ppermute | solution.py:23
  38.0 1.3 collective-permute-done.17.refs_1_
  39.3 1.6 %collective-permute-start.6 = (bf16[16,2176]{1,0:T(8,128)(2,1)}, bf16[16,2176]{1,0:T(8,128)(2,1)S(1)}, u32[]{:S(2)}, u32[]{:S(2)}) collective-permute-start(bf16[16,2176]{1,0:T(8,128)(2,1)} %pack_rows.1.refs_0_), channel_id=1, source_target_pairs={{0,1},{1,0},{2,3},{3,2},{4,5},{5,4},{6,7},{7,6},{8,9},{9,8},{10,11... | collective-permute-start | bytes 208904 | tf_op jit(solution)/shard_map/ppermute | solution.py:23
  40.9 2.3 %collective-permute-done.18.refs_2_ = bf16[16,2048]{1,0:T(8,128)(2,1)S(1)} collective-permute-done((bf16[16,2048]{1,0:T(8,128)(2,1)S(1)}, bf16[16,2048]{1,0:T(8,128)(2,1)S(1)}, u32[]{:S(2)}, u32[]{:S(2)}) %collective-permute-start.18) | collective-permute-done | bytes 65568 | tf_op jit(solution)/shard_map/ppermute | solution.py:23
  43.2 2.8 %collective-permute-start.19 = (bf16[16,2048]{1,0:T(8,128)(2,1)S(1)}, bf16[16,2048]{1,0:T(8,128)(2,1)S(1)}, u32[]{:S(2)}, u32[]{:S(2)}) collective-permute-start(bf16[16,2048]{1,0:T(8,128)(2,1)S(1)} %bitcast.23), channel_id=1, source_target_pairs={{0,6},{2,4},{4,2},{6,0},{1,7},{3,5},{5,3},{7,1},{8,14},{10,12},{12... | collective-permute-start | bytes 196616 | tf_op jit(solution)/shard_map/ppermute | solution.py:23
  46.0 1.5 collective-permute-start.7
  47.5 0.5 collective-permute-start.8
  48.0 0.0 collective-permute-done.5.refs_3_
  48.0 1.5 collective-permute-start.9
  49.6 1.2 collective-permute-start.20
  50.8 0.2 collective-permute-done.7.refs_5_
  50.9 1.5 collective-permute-start.21
  52.5 0.8 collective-permute-start.22
  53.3 1.2 collective-permute-start.23
  54.5 4.6 %copy-done = bf16[8,2048,384]{2,1,0:T(8,128)(2,1)S(1)} copy-done((bf16[8,2048,384]{2,1,0:T(8,128)(2,1)S(1)}, bf16[8,2048,384]{2,1,0:T(8,128)(2,1)}, u32[]{:S(2)}) %copy-start) | copy-done | bytes 12582936
  59.1 4.6 %copy-done.3 = bf16[8,2048,384]{2,1,0:T(8,128)(2,1)S(1)} copy-done((bf16[8,2048,384]{2,1,0:T(8,128)(2,1)S(1)}, bf16[8,2048,384]{2,1,0:T(8,128)(2,1)}, u32[]{:S(2)}) %copy-start.3) | copy-done | bytes 12582936
  63.6 4.6 %copy-done.6 = bf16[8,384,2048]{2,1,0:T(8,128)(2,1)S(1)} copy-done((bf16[8,384,2048]{2,1,0:T(8,128)(2,1)S(1)}, bf16[8,384,2048]{2,1,0:T(8,128)(2,1)}, u32[]{:S(2)}) %copy-start.6) | copy-done | bytes 12582936
  68.2 0.9 copy-done.10
  69.1 11.0 %experts_forward.1 = (bf16[16,2048]{1,0:T(8,128)(2,1)S(1)}, bf16[16,2048]{1,0:T(8,128)(2,1)S(1)}, bf16[16,2048]{1,0:T(8,128)(2,1)S(1)}, bf16[16,2048]{1,0:T(8,12...) custom-call(s32[1]{0:T(128)} %bitcast.8.shard_ref, ...), custom_call_target="tpu_custom_call", output_to_operand_aliasing={{10}: (9, {}), {11}: (10, {}), {12}: (11, {})} | custom-call | flops 4831838208 | bytes 37748736 | tf_op jit(solution)/shard_map/experts_forward/pallas_call | solution.py:156
  80.1 4.5 %copy-done.1 = bf16[8,2048,384]{2,1,0:T(8,128)(2,1)} copy-done((bf16[8,2048,384]{2,1,0:T(8,128)(2,1)}, bf16[8,2048,384]{2,1,0:T(8,128)(2,1)S(1)}, u32[]{:S(2)}) %copy-start.1) | copy-done | bytes 12582936
  84.6 4.5 %copy-done.4 = bf16[8,2048,384]{2,1,0:T(8,128)(2,1)} copy-done((bf16[8,2048,384]{2,1,0:T(8,128)(2,1)}, bf16[8,2048,384]{2,1,0:T(8,128)(2,1)S(1)}, u32[]{:S(2)}) %copy-start.4) | copy-done | bytes 12582936
  89.1 4.5 %copy-done.7 = bf16[8,384,2048]{2,1,0:T(8,128)(2,1)} copy-done((bf16[8,384,2048]{2,1,0:T(8,128)(2,1)}, bf16[8,384,2048]{2,1,0:T(8,128)(2,1)S(1)}, u32[]{:S(2)}) %copy-start.7) | copy-done | bytes 12582936
  93.6 1.5 collective-permute-start.1
  95.1 4.6 %copy-done.2 = bf16[8,2048,384]{2,1,0:T(8,128)(2,1)S(1)} copy-done((bf16[8,2048,384]{2,1,0:T(8,128)(2,1)S(1)}, bf16[8,2048,384]{2,1,0:T(8,128)(2,1)}, u32[]{:S(2)}) %copy-start.2) | copy-done | bytes 12582936
  99.7 4.6 %copy-done.5 = bf16[8,2048,384]{2,1,0:T(8,128)(2,1)S(1)} copy-done((bf16[8,2048,384]{2,1,0:T(8,128)(2,1)S(1)}, bf16[8,2048,384]{2,1,0:T(8,128)(2,1)}, u32[]{:S(2)}) %copy-start.5) | copy-done | bytes 12582936
  104.2 1.4 copy-done.8
  105.6 1.4 copy-done.9
  107.1 17.7 %experts_backward.1 = (bf16[16,2048]{1,0:T(8,128)(2,1)S(1)}, bf16[16,2048]{1,0:T(8,128)(2,1)S(1)}, bf16[16,2048]{1,0:T(8,128)(2,1)S(1)}, bf16[16,2048]{1,0:T(8,1...) custom-call(bf16[16,2048]{1,0:T(8,128)(2,1)S(1)} %bitcast.25, ...), custom_call_target="tpu_custom_call" | custom-call | flops 4831838208 | bytes 37748736 | tf_op jit(solution)/shard_map/experts_backward/pallas_call | solution.py:218
  124.7 0.9 collective-permute-start.25
  125.6 0.6 pad_add_fusion.base_ref
  126.2 0.6 copy-done.16
  126.8 0.0 copy-done.17
  126.8 0.1 copy-done.18
  126.9 6.4 %attention.1 = bf16[128,2048]{1,0:T(8,128)(2,1)} custom-call(s32[4]{0:T(128)} %pad_add_fusion.base_ref, bf16[128,2048]{1,0:T(8,128)(2,1)} %bitcast.33, bf16[128,512]{1,0:T(8,128)(2,1)} %copy-done.13, bf16[128,512]{1,0:T(8,128)(2,1)} %copy-done.16, bf16[128,512]{1,0:T(8,128)(2,1)} %copy-done.17, bf16[128,512]{1,0:T(8,128)(2,1)} %copy-done.18), custom_call_target="tpu_custom_call" | custom-call | flops 536870912 | bytes 1048576 | tf_op jit(solution)/shard_map/attention/pallas_call | solution.py:89
  133.3 1.2 collective-permute-start.27
  134.5 0.8 collective-permute-start.29
  135.3 1.2 collective-permute-start.24
  136.5 0.8 collective-permute-start.11
  137.3 1.2 collective-permute-start.13
  138.6 0.9 collective-permute-start.15
  139.5 1.3 collective-permute-start.10
  140.8 1.4 collective-permute-done.11
  142.3 1.4 collective-permute-done.13
  143.7 1.8 %collective-permute-start.28 = (bf16[16,2048]{1,0:T(8,128)(2,1)S(1)}, bf16[16,2048]{1,0:T(8,128)(2,1)S(1)}, u32[]{:S(2)}, u32[]{:S(2)}) collective-permute-start(bf16[16,2048]{1,0:T(8,128)(2,1)S(1)} %add_convert_fusion.2), channel_id=1, source_target_pairs={{0,4},{2,6},{4,0},{6,2},{1,5},{3,7},{5,1},{7,3},{8,12},{10,14},{12... | collective-permute-start | bytes 196616 | tf_op jit(solution)/shard_map/ppermute | solution.py:23
  145.5 2.1 %collective-permute-start.30 = (bf16[16,2048]{1,0:T(8,128)(2,1)S(1)}, bf16[16,2048]{1,0:T(8,128)(2,1)S(1)}, u32[]{:S(2)}, u32[]{:S(2)}) collective-permute-start(bf16[16,2048]{1,0:T(8,128)(2,1)S(1)} %add_convert_fusion.1), channel_id=1, source_target_pairs={{0,6},{2,4},{4,2},{6,0},{1,7},{3,5},{5,3},{7,1},{8,14},{10,12},{12... | collective-permute-start | bytes 196616 | tf_op jit(solution)/shard_map/ppermute | solution.py:23
  147.7 0.1 collective-permute-start.12
  147.8 2.3 %collective-permute-start.14 = (bf16[16,2048]{1,0:T(8,128)(2,1)S(1)}, bf16[16,2048]{1,0:T(8,128)(2,1)S(1)}, u32[]{:S(2)}, u32[]{:S(2)}) collective-permute-start(bf16[16,2048]{1,0:T(8,128)(2,1)S(1)} %add_convert_fusion.6), channel_id=1, source_target_pairs={{0,4},{2,6},{4,0},{6,2},{1,5},{3,7},{5,1},{7,3},{8,12},{10,14},{12... | collective-permute-start | bytes 196616 | tf_op jit(solution)/shard_map/ppermute | solution.py:23
  150.1 0.9 collective-permute-done.28
  151.0 3.7 %collective-permute-start.16 = (bf16[16,2048]{1,0:T(8,128)(2,1)S(1)}, bf16[16,2048]{1,0:T(8,128)(2,1)S(1)}, u32[]{:S(2)}, u32[]{:S(2)}) collective-permute-start(bf16[16,2048]{1,0:T(8,128)(2,1)S(1)} %add_convert_fusion.5), channel_id=1, source_target_pairs={{0,6},{2,4},{4,2},{6,0},{1,7},{3,5},{5,3},{7,1},{8,14},{10,12},{12... | collective-permute-start | bytes 196616 | tf_op jit(solution)/shard_map/ppermute | solution.py:23
  154.7 0.7 fusion.1
  155.4 0.7 collective-permute-done.14
  156.1 1.0 collective-permute-done.16
  157.1 0.7 fusion
  (60 shorter events, 0.2 us)
Async XLA Ops:
  0.6 12.4 %copy-start.12 = (bf16[8,2048,384]{2,1,0:T(8,128)(2,1)S(1)}, bf16[8,2048,384]{2,1,0:T(8,128)(2,1)}, u32[]{:S(2)}) copy-start(bf16[8,2048,384]{2,1,0:T(8,128)(2,1)} %param.18) | copy-start | bytes 37748740
  0.6 18.7 %slice-start = ((s8[12582912]{0:T(1024)(128)(4,1)}), s8[4194304]{0:T(1024)(128)(4,1)S(1)}, s32[]{:S(2)}) async-start(s8[12582912]{0:T(1024)(128)(4,1)} %bitcast.26), calls=%async_computation | async-start | bytes 8388608
  0.7 19.8 %slice-start.1 = ((s8[12582912]{0:T(1024)(128)(4,1)}), s8[4194304]{0:T(1024)(128)(4,1)S(1)}, s32[]{:S(2)}) async-start(s8[12582912]{0:T(1024)(128)(4,1)} %bitcast.26), calls=%async_computation.1 | async-start | bytes 8388608
  13.0 8.8 %slice-start.2 = ((s8[12582912]{0:T(1024)(128)(4,1)}), s8[4194304]{0:T(1024)(128)(4,1)S(1)}, s32[]{:S(2)}) async-start(s8[12582912]{0:T(1024)(128)(4,1)} %bitcast.26), calls=%async_computation.2 | async-start | bytes 8388608
  21.8 11.8 %copy-start.11 = (bf16[1,16,2048]{2,1,0:T(8,128)(2,1)S(1)}, bf16[1,16,2048]{2,1,0:T(8,128)(2,1)}, u32[]{:S(2)}) copy-start(bf16[1,16,2048]{2,1,0:T(8,128)(2,1)} %param.16) | copy-start | bytes 196612
  21.8 27.8 %copy-start.14 = (bf16[1,128,256]{2,1,0:T(8,128)(2,1)S(1)}, bf16[1,128,256]{2,1,0:T(8,128)(2,1)}, u32[]{:S(2)}) copy-start(bf16[1,128,256]{2,1,0:T(8,128)(2,1)} %param.12) | copy-start | bytes 196612
  21.8 27.8 %copy-start.15 = (bf16[1,128,256]{2,1,0:T(8,128)(2,1)S(1)}, bf16[1,128,256]{2,1,0:T(8,128)(2,1)}, u32[]{:S(2)}) copy-start(bf16[1,128,256]{2,1,0:T(8,128)(2,1)} %param.11) | copy-start | bytes 196612
  28.0 18.0 %collective-permute-start.3 = (bf16[16,2176]{1,0:T(8,128)(2,1)}, bf16[16,2176]{1,0:T(8,128)(2,1)S(1)}, u32[]{:S(2)}, u32[]{:S(2)}) collective-permute-start(bf16[16,2176]{1,0:T(8,128)(2,1)} %pack_rows.1.refs_0_), channel_id=1, source_target_pairs={{0,2},{2,0},{4,6},{6,4},{1,3},{3,1},{5,7},{7,5},{8,10},{10,8},{12,... | collective-permute-start | bytes 208904 | tf_op jit(solution)/shard_map/ppermute | solution.py:23
  31.0 16.5 %collective-permute-start.4 = (bf16[16,2176]{1,0:T(8,128)(2,1)}, bf16[16,2176]{1,0:T(8,128)(2,1)S(1)}, u32[]{:S(2)}, u32[]{:S(2)}) collective-permute-start(bf16[16,2176]{1,0:T(8,128)(2,1)} %pack_rows.1.refs_0_), channel_id=1, source_target_pairs={{0,4},{2,6},{4,0},{6,2},{1,5},{3,7},{5,1},{7,3},{8,12},{10,14},{12... | collective-permute-start | bytes 208904 | tf_op jit(solution)/shard_map/ppermute | solution.py:23
  33.6 14.4 %collective-permute-start.5 = (bf16[16,2176]{1,0:T(8,128)(2,1)}, bf16[16,2176]{1,0:T(8,128)(2,1)S(1)}, u32[]{:S(2)}, u32[]{:S(2)}) collective-permute-start(bf16[16,2176]{1,0:T(8,128)(2,1)} %pack_rows.1.refs_0_), channel_id=1, source_target_pairs={{0,6},{2,4},{4,2},{6,0},{1,7},{3,5},{5,3},{7,1},{8,14},{10,12},{12... | collective-permute-start | bytes 208904 | tf_op jit(solution)/shard_map/ppermute | solution.py:23
  33.6 5.7 %collective-permute-start.17 = (bf16[16,2048]{1,0:T(8,128)(2,1)S(1)}, bf16[16,2048]{1,0:T(8,128)(2,1)S(1)}, u32[]{:S(2)}, u32[]{:S(2)}) collective-permute-start(bf16[16,2048]{1,0:T(8,128)(2,1)S(1)} %bitcast.21), channel_id=1, source_target_pairs={{0,2},{2,0},{4,6},{6,4},{1,3},{3,1},{5,7},{7,5},{8,10},{10,8},{12,... | collective-permute-start | bytes 196616 | tf_op jit(solution)/shard_map/ppermute | solution.py:23
  34.5 8.7 %collective-permute-start.18 = (bf16[16,2048]{1,0:T(8,128)(2,1)S(1)}, bf16[16,2048]{1,0:T(8,128)(2,1)S(1)}, u32[]{:S(2)}, u32[]{:S(2)}) collective-permute-start(bf16[16,2048]{1,0:T(8,128)(2,1)S(1)} %bitcast.22), channel_id=1, source_target_pairs={{0,4},{2,6},{4,0},{6,2},{1,5},{3,7},{5,1},{7,3},{8,12},{10,14},{12... | collective-permute-start | bytes 196616 | tf_op jit(solution)/shard_map/ppermute | solution.py:23
  39.3 11.5 %collective-permute-start.6 = (bf16[16,2176]{1,0:T(8,128)(2,1)}, bf16[16,2176]{1,0:T(8,128)(2,1)S(1)}, u32[]{:S(2)}, u32[]{:S(2)}) collective-permute-start(bf16[16,2176]{1,0:T(8,128)(2,1)} %pack_rows.1.refs_0_), channel_id=1, source_target_pairs={{0,1},{1,0},{2,3},{3,2},{4,5},{5,4},{6,7},{7,6},{8,9},{9,8},{10,11... | collective-permute-start | bytes 208904 | tf_op jit(solution)/shard_map/ppermute | solution.py:23
  43.2 6.4 %collective-permute-start.19 = (bf16[16,2048]{1,0:T(8,128)(2,1)S(1)}, bf16[16,2048]{1,0:T(8,128)(2,1)S(1)}, u32[]{:S(2)}, u32[]{:S(2)}) collective-permute-start(bf16[16,2048]{1,0:T(8,128)(2,1)S(1)} %bitcast.23), channel_id=1, source_target_pairs={{0,6},{2,4},{4,2},{6,0},{1,7},{3,5},{5,3},{7,1},{8,14},{10,12},{12... | collective-permute-start | bytes 196616 | tf_op jit(solution)/shard_map/ppermute | solution.py:23
  46.0 4.9 %collective-permute-start.7 = (bf16[16,2176]{1,0:T(8,128)(2,1)S(1)}, bf16[16,2176]{1,0:T(8,128)(2,1)S(1)}, u32[]{:S(2)}, u32[]{:S(2)}) collective-permute-start(bf16[16,2176]{1,0:T(8,128)(2,1)S(1)} %collective-permute-done.3.refs_1_), channel_id=1, source_target_pairs={{0,1},{1,0},{2,3},{3,2},{4,5},{5,4},{6,7},{7,6},{8,9},{9,8},{10,11... | collective-permute-start | bytes 208904 | tf_op jit(solution)/shard_map/ppermute | solution.py:23
  47.5 4.9 %collective-permute-start.8 = (bf16[16,2176]{1,0:T(8,128)(2,1)S(1)}, bf16[16,2176]{1,0:T(8,128)(2,1)S(1)}, u32[]{:S(2)}, u32[]{:S(2)}) collective-permute-start(bf16[16,2176]{1,0:T(8,128)(2,1)S(1)} %collective-permute-done.4.refs_2_), channel_id=1, source_target_pairs={{0,1},{1,0},{2,3},{3,2},{4,5},{5,4},{6,7},{7,6},{8,9},{9,8},{10,11... | collective-permute-start | bytes 208904 | tf_op jit(solution)/shard_map/ppermute | solution.py:23
  48.0 5.2 %collective-permute-start.9 = (bf16[16,2176]{1,0:T(8,128)(2,1)S(1)}, bf16[16,2176]{1,0:T(8,128)(2,1)S(1)}, u32[]{:S(2)}, u32[]{:S(2)}) collective-permute-start(bf16[16,2176]{1,0:T(8,128)(2,1)S(1)} %collective-permute-done.5.refs_3_), channel_id=1, source_target_pairs={{0,1},{1,0},{2,3},{3,2},{4,5},{5,4},{6,7},{7,6},{8,9},{9,8},{10,11... | collective-permute-start | bytes 208904 | tf_op jit(solution)/shard_map/ppermute | solution.py:23
  49.6 45.5 %copy-start.13 = (bf16[128,512]{1,0:T(8,128)(2,1)}, bf16[128,512]{1,0:T(8,128)(2,1)S(1)}, u32[]{:S(2)}) copy-start(bf16[128,512]{1,0:T(8,128)(2,1)S(1)} %pad_maximum_fusion.refs_0_) | copy-start | bytes 393220
  49.6 44.0 %collective-permute-start.20 = (bf16[16,2048]{1,0:T(8,128)(2,1)S(1)}, bf16[16,2048]{1,0:T(8,128)(2,1)S(1)}, u32[]{:S(2)}, u32[]{:S(2)}) collective-permute-start(bf16[16,2048]{1,0:T(8,128)(2,1)S(1)} %bitcast.24), channel_id=1, source_target_pairs={{0,1},{1,0},{2,3},{3,2},{4,5},{5,4},{6,7},{7,6},{8,9},{9,8},{10,11... | collective-permute-start | bytes 196616 | tf_op jit(solution)/shard_map/ppermute | solution.py:23
  50.7 75.4 %collective-permute-start = (bf16[128,512]{1,0:T(8,128)(2,1)S(1)}, bf16[128,512]{1,0:T(8,128)(2,1)S(1)}, u32[]{:S(2)}, u32[]{:S(2)}) collective-permute-start(bf16[128,512]{1,0:T(8,128)(2,1)S(1)} %pad_maximum_fusion.refs_0_), channel_id=1, source_target_pairs={{0,8},{8,0},{16,24},{24,16},{1,9},{9,1},{17,25},{25,17},{2,10},{10... | collective-permute-start | bytes 393224 | tf_op jit(solution)/shard_map/ppermute | solution.py:23
  50.9 44.1 %collective-permute-start.21 = (bf16[16,2048]{1,0:T(8,128)(2,1)S(1)}, bf16[16,2048]{1,0:T(8,128)(2,1)S(1)}, u32[]{:S(2)}, u32[]{:S(2)}) collective-permute-start(bf16[16,2048]{1,0:T(8,128)(2,1)S(1)} %collective-permute-done.17.refs_1_), channel_id=1, source_target_pairs={{0,1},{1,0},{2,3},{3,2},{4,5},{5,4},{6,7},{7,6},{8,9},{9,8},{10,11... | collective-permute-start | bytes 196616 | tf_op jit(solution)/shard_map/ppermute | solution.py:23
  52.5 42.6 %collective-permute-start.22 = (bf16[16,2048]{1,0:T(8,128)(2,1)S(1)}, bf16[16,2048]{1,0:T(8,128)(2,1)S(1)}, u32[]{:S(2)}, u32[]{:S(2)}) collective-permute-start(bf16[16,2048]{1,0:T(8,128)(2,1)S(1)} %collective-permute-done.18.refs_2_), channel_id=1, source_target_pairs={{0,1},{1,0},{2,3},{3,2},{4,5},{5,4},{6,7},{7,6},{8,9},{9,8},{10,11... | collective-permute-start | bytes 196616 | tf_op jit(solution)/shard_map/ppermute | solution.py:23
  53.3 41.8 %collective-permute-start.23 = (bf16[16,2048]{1,0:T(8,128)(2,1)S(1)}, bf16[16,2048]{1,0:T(8,128)(2,1)S(1)}, u32[]{:S(2)}, u32[]{:S(2)}) collective-permute-start(bf16[16,2048]{1,0:T(8,128)(2,1)S(1)} %collective-permute-done.19.refs_3_), channel_id=1, source_target_pairs={{0,1},{1,0},{2,3},{3,2},{4,5},{5,4},{6,7},{7,6},{8,9},{9,8},{10,11... | collective-permute-start | bytes 196616 | tf_op jit(solution)/shard_map/ppermute | solution.py:23
  54.5 4.6 %copy-start = (bf16[8,2048,384]{2,1,0:T(8,128)(2,1)S(1)}, bf16[8,2048,384]{2,1,0:T(8,128)(2,1)}, u32[]{:S(2)}) copy-start(bf16[8,2048,384]{2,1,0:T(8,128)(2,1)} %copy.22.refs_8_) | copy-start | bytes 37748740
  59.1 4.6 %copy-start.3 = (bf16[8,2048,384]{2,1,0:T(8,128)(2,1)S(1)}, bf16[8,2048,384]{2,1,0:T(8,128)(2,1)}, u32[]{:S(2)}) copy-start(bf16[8,2048,384]{2,1,0:T(8,128)(2,1)} %copy.23.refs_9_) | copy-start | bytes 37748740
  63.6 4.6 %copy-start.6 = (bf16[8,384,2048]{2,1,0:T(8,128)(2,1)S(1)}, bf16[8,384,2048]{2,1,0:T(8,128)(2,1)}, u32[]{:S(2)}) copy-start(bf16[8,384,2048]{2,1,0:T(8,128)(2,1)} %copy.24.refs_10_) | copy-start | bytes 37748740
  68.2 0.9 copy-start.10
  80.1 4.5 %copy-start.1 = (bf16[8,2048,384]{2,1,0:T(8,128)(2,1)}, bf16[8,2048,384]{2,1,0:T(8,128)(2,1)S(1)}, u32[]{:S(2)}) copy-start(bf16[8,2048,384]{2,1,0:T(8,128)(2,1)S(1)} %get-tuple-element.32.refs_8_) | copy-start | bytes 37748740
  84.6 4.5 %copy-start.4 = (bf16[8,2048,384]{2,1,0:T(8,128)(2,1)}, bf16[8,2048,384]{2,1,0:T(8,128)(2,1)S(1)}, u32[]{:S(2)}) copy-start(bf16[8,2048,384]{2,1,0:T(8,128)(2,1)S(1)} %get-tuple-element.33.refs_9_) | copy-start | bytes 37748740
  89.1 4.5 %copy-start.7 = (bf16[8,384,2048]{2,1,0:T(8,128)(2,1)}, bf16[8,384,2048]{2,1,0:T(8,128)(2,1)S(1)}, u32[]{:S(2)}) copy-start(bf16[8,384,2048]{2,1,0:T(8,128)(2,1)S(1)} %get-tuple-element.34.refs_10_) | copy-start | bytes 37748740
  93.6 32.6 %collective-permute-start.1 = (bf16[128,512]{1,0:T(8,128)(2,1)S(1)}, bf16[128,512]{1,0:T(8,128)(2,1)S(1)}, u32[]{:S(2)}, u32[]{:S(2)}) collective-permute-start(bf16[128,512]{1,0:T(8,128)(2,1)S(1)} %pad_maximum_fusion.refs_0_), channel_id=1, source_target_pairs={{0,16},{8,24},{16,0},{24,8},{1,17},{9,25},{17,1},{25,9},{2,18},{10... | collective-permute-start | bytes 393224 | tf_op jit(solution)/shard_map/ppermute | solution.py:23
  95.1 31.1 %collective-permute-start.2 = (bf16[128,512]{1,0:T(8,128)(2,1)S(1)}, bf16[128,512]{1,0:T(8,128)(2,1)S(1)}, u32[]{:S(2)}, u32[]{:S(2)}) collective-permute-start(bf16[128,512]{1,0:T(8,128)(2,1)S(1)} %pad_maximum_fusion.refs_0_), channel_id=1, source_target_pairs={{0,24},{8,16},{16,8},{24,0},{1,25},{9,17},{17,9},{25,1},{2,26},{10... | collective-permute-start | bytes 393224 | tf_op jit(solution)/shard_map/ppermute | solution.py:23
  95.1 4.6 %copy-start.2 = (bf16[8,2048,384]{2,1,0:T(8,128)(2,1)S(1)}, bf16[8,2048,384]{2,1,0:T(8,128)(2,1)}, u32[]{:S(2)}) copy-start(bf16[8,2048,384]{2,1,0:T(8,128)(2,1)} %copy-done.1) | copy-start | bytes 37748740
  99.7 4.6 %copy-start.5 = (bf16[8,2048,384]{2,1,0:T(8,128)(2,1)S(1)}, bf16[8,2048,384]{2,1,0:T(8,128)(2,1)}, u32[]{:S(2)}) copy-start(bf16[8,2048,384]{2,1,0:T(8,128)(2,1)} %copy-done.4) | copy-start | bytes 37748740
  104.2 1.4 copy-start.8
  105.6 1.4 copy-start.9
  124.7 12.6 %collective-permute-start.25 = (bf16[16,2048]{1,0:T(8,128)(2,1)S(1)}, bf16[16,2048]{1,0:T(8,128)(2,1)S(1)}, u32[]{:S(2)}, u32[]{:S(2)}) collective-permute-start(bf16[16,2048]{1,0:T(8,128)(2,1)S(1)} %get-tuple-element.40), channel_id=1, source_target_pairs={{0,1},{1,0},{2,3},{3,2},{4,5},{5,4},{6,7},{7,6},{8,9},{9,8},{10,11... | collective-permute-start | bytes 196616 | tf_op jit(solution)/shard_map/ppermute | solution.py:23
  126.2 0.6 copy-start.16
  126.2 0.7 copy-start.17
  126.2 0.7 copy-start.18
  133.3 5.3 %collective-permute-start.27 = (bf16[16,2048]{1,0:T(8,128)(2,1)S(1)}, bf16[16,2048]{1,0:T(8,128)(2,1)S(1)}, u32[]{:S(2)}, u32[]{:S(2)}) collective-permute-start(bf16[16,2048]{1,0:T(8,128)(2,1)S(1)} %get-tuple-element.42), channel_id=1, source_target_pairs={{0,1},{1,0},{2,3},{3,2},{4,5},{5,4},{6,7},{7,6},{8,9},{9,8},{10,11... | collective-permute-start | bytes 196616 | tf_op jit(solution)/shard_map/ppermute | solution.py:23
  134.5 5.0 %collective-permute-start.29 = (bf16[16,2048]{1,0:T(8,128)(2,1)S(1)}, bf16[16,2048]{1,0:T(8,128)(2,1)S(1)}, u32[]{:S(2)}, u32[]{:S(2)}) collective-permute-start(bf16[16,2048]{1,0:T(8,128)(2,1)S(1)} %get-tuple-element.44), channel_id=1, source_target_pairs={{0,1},{1,0},{2,3},{3,2},{4,5},{5,4},{6,7},{7,6},{8,9},{9,8},{10,11... | collective-permute-start | bytes 196616 | tf_op jit(solution)/shard_map/ppermute | solution.py:23
  135.3 12.4 %collective-permute-start.24 = (bf16[16,2048]{1,0:T(8,128)(2,1)S(1)}, bf16[16,2048]{1,0:T(8,128)(2,1)S(1)}, u32[]{:S(2)}, u32[]{:S(2)}) collective-permute-start(bf16[16,2048]{1,0:T(8,128)(2,1)S(1)} %get-tuple-element.38), channel_id=1, source_target_pairs={{0,1},{1,0},{2,3},{3,2},{4,5},{5,4},{6,7},{7,6},{8,9},{9,8},{10,11... | collective-permute-start | bytes 196616 | tf_op jit(solution)/shard_map/ppermute | solution.py:23
  136.5 5.8 %collective-permute-start.11 = (bf16[16,2048]{1,0:T(8,128)(2,1)S(1)}, bf16[16,2048]{1,0:T(8,128)(2,1)S(1)}, u32[]{:S(2)}, u32[]{:S(2)}) collective-permute-start(bf16[16,2048]{1,0:T(8,128)(2,1)S(1)} %get-tuple-element.27), channel_id=1, source_target_pairs={{0,1},{1,0},{2,3},{3,2},{4,5},{5,4},{6,7},{7,6},{8,9},{9,8},{10,11... | collective-permute-start | bytes 196616 | tf_op jit(solution)/shard_map/ppermute | solution.py:23
  137.3 6.4 %collective-permute-start.13 = (bf16[16,2048]{1,0:T(8,128)(2,1)S(1)}, bf16[16,2048]{1,0:T(8,128)(2,1)S(1)}, u32[]{:S(2)}, u32[]{:S(2)}) collective-permute-start(bf16[16,2048]{1,0:T(8,128)(2,1)S(1)} %get-tuple-element.29), channel_id=1, source_target_pairs={{0,1},{1,0},{2,3},{3,2},{4,5},{5,4},{6,7},{7,6},{8,9},{9,8},{10,11... | collective-permute-start | bytes 196616 | tf_op jit(solution)/shard_map/ppermute | solution.py:23
  138.6 6.9 %collective-permute-start.15 = (bf16[16,2048]{1,0:T(8,128)(2,1)S(1)}, bf16[16,2048]{1,0:T(8,128)(2,1)S(1)}, u32[]{:S(2)}, u32[]{:S(2)}) collective-permute-start(bf16[16,2048]{1,0:T(8,128)(2,1)S(1)} %get-tuple-element.31), channel_id=1, source_target_pairs={{0,1},{1,0},{2,3},{3,2},{4,5},{5,4},{6,7},{7,6},{8,9},{9,8},{10,11... | collective-permute-start | bytes 196616 | tf_op jit(solution)/shard_map/ppermute | solution.py:23
  139.5 15.9 %collective-permute-start.10 = (bf16[16,2048]{1,0:T(8,128)(2,1)S(1)}, bf16[16,2048]{1,0:T(8,128)(2,1)S(1)}, u32[]{:S(2)}, u32[]{:S(2)}) collective-permute-start(bf16[16,2048]{1,0:T(8,128)(2,1)S(1)} %get-tuple-element.25), channel_id=1, source_target_pairs={{0,1},{1,0},{2,3},{3,2},{4,5},{5,4},{6,7},{7,6},{8,9},{9,8},{10,11... | collective-permute-start | bytes 196616 | tf_op jit(solution)/shard_map/ppermute | solution.py:23
  142.3 5.5 %collective-permute-start.26 = (bf16[16,2048]{1,0:T(8,128)(2,1)S(1)}, bf16[16,2048]{1,0:T(8,128)(2,1)S(1)}, u32[]{:S(2)}, u32[]{:S(2)}) collective-permute-start(bf16[16,2048]{1,0:T(8,128)(2,1)S(1)} %add_convert_fusion.3), channel_id=1, source_target_pairs={{0,2},{2,0},{4,6},{6,4},{1,3},{3,1},{5,7},{7,5},{8,10},{10,8},{12,... | collective-permute-start | bytes 196616 | tf_op jit(solution)/shard_map/ppermute | solution.py:23
  143.7 7.3 %collective-permute-start.28 = (bf16[16,2048]{1,0:T(8,128)(2,1)S(1)}, bf16[16,2048]{1,0:T(8,128)(2,1)S(1)}, u32[]{:S(2)}, u32[]{:S(2)}) collective-permute-start(bf16[16,2048]{1,0:T(8,128)(2,1)S(1)} %add_convert_fusion.2), channel_id=1, source_target_pairs={{0,4},{2,6},{4,0},{6,2},{1,5},{3,7},{5,1},{7,3},{8,12},{10,14},{12... | collective-permute-start | bytes 196616 | tf_op jit(solution)/shard_map/ppermute | solution.py:23
  145.5 9.1 %collective-permute-start.30 = (bf16[16,2048]{1,0:T(8,128)(2,1)S(1)}, bf16[16,2048]{1,0:T(8,128)(2,1)S(1)}, u32[]{:S(2)}, u32[]{:S(2)}) collective-permute-start(bf16[16,2048]{1,0:T(8,128)(2,1)S(1)} %add_convert_fusion.1), channel_id=1, source_target_pairs={{0,6},{2,4},{4,2},{6,0},{1,7},{3,5},{5,3},{7,1},{8,14},{10,12},{12... | collective-permute-start | bytes 196616 | tf_op jit(solution)/shard_map/ppermute | solution.py:23
  147.7 7.7 %collective-permute-start.12 = (bf16[16,2048]{1,0:T(8,128)(2,1)S(1)}, bf16[16,2048]{1,0:T(8,128)(2,1)S(1)}, u32[]{:S(2)}, u32[]{:S(2)}) collective-permute-start(bf16[16,2048]{1,0:T(8,128)(2,1)S(1)} %add_convert_fusion.7), channel_id=1, source_target_pairs={{0,2},{2,0},{4,6},{6,4},{1,3},{3,1},{5,7},{7,5},{8,10},{10,8},{12,... | collective-permute-start | bytes 196616 | tf_op jit(solution)/shard_map/ppermute | solution.py:23
  147.8 8.3 %collective-permute-start.14 = (bf16[16,2048]{1,0:T(8,128)(2,1)S(1)}, bf16[16,2048]{1,0:T(8,128)(2,1)S(1)}, u32[]{:S(2)}, u32[]{:S(2)}) collective-permute-start(bf16[16,2048]{1,0:T(8,128)(2,1)S(1)} %add_convert_fusion.6), channel_id=1, source_target_pairs={{0,4},{2,6},{4,0},{6,2},{1,5},{3,7},{5,1},{7,3},{8,12},{10,14},{12... | collective-permute-start | bytes 196616 | tf_op jit(solution)/shard_map/ppermute | solution.py:23
  151.0 6.2 %collective-permute-start.16 = (bf16[16,2048]{1,0:T(8,128)(2,1)S(1)}, bf16[16,2048]{1,0:T(8,128)(2,1)S(1)}, u32[]{:S(2)}, u32[]{:S(2)}) collective-permute-start(bf16[16,2048]{1,0:T(8,128)(2,1)S(1)} %add_convert_fusion.5), channel_id=1, source_target_pairs={{0,6},{2,4},{4,2},{6,0},{1,7},{3,5},{5,3},{7,1},{8,14},{10,12},{12... | collective-permute-start | bytes 196616 | tf_op jit(solution)/shard_map/ppermute | solution.py:23

commit v2 on v1

v2 whole, which is shorter than its diff:
```python
import functools

import jax
import jax.numpy as jnp
from jax import lax
from jax.experimental import pallas as pl
from jax.experimental.pallas import tpu as pltpu
from jax.sharding import PartitionSpec as P

H = 32
KVH = 4
HD = 128
EXPERTS = 64
CAP = 3
NT = (((1,), (1,)), ((), ()))
VMEM = pl.BlockSpec(memory_space=pltpu.VMEM)
SMEM = pl.BlockSpec(memory_space=pltpu.SMEM)
F32 = jnp.float32
BF16 = jnp.bfloat16


def swap(array, axis, offset):
    count = lax.axis_size(axis)
    return lax.ppermute(array, axis, [(i, i ^ offset) for i in range(count)])


def pack_kernel(ids_ref, gates_ref, x_ref, grad_ref, out_ref):
    rows, width = x_ref.shape
    topk = ids_ref.shape[0]
    expert = lax.broadcasted_iota(jnp.int32, (EXPERTS, rows), 0)
    table = jnp.zeros((EXPERTS, rows), F32)
    for k in range(topk):
        table = table + jnp.where(ids_ref[k : k + 1] == expert, gates_ref[k : k + 1], 0.0)
    high = table.astype(BF16).astype(F32)
    both = jnp.concatenate([high, table - high], axis=0)
    out_ref[:, :width] = x_ref[...]
    out_ref[:, width : 2 * width] = grad_ref[...]
    out_ref[:, 2 * width :] = jnp.transpose(both).astype(BF16)


def pack_rows(ids, gates, x, grad):
    rows, width = x.shape
    return pl.pallas_call(
        pack_kernel,
        in_specs=[VMEM] * 4,
        out_specs=VMEM,
        out_shape=jax.ShapeDtypeStruct((rows, 2 * (width + EXPERTS)), BF16),
        name="pack_rows",
    )(ids, gates, x, grad)


def attention_kernel(base_ref, q_ref, *refs):
    out_ref = refs[-1]
    kv_refs = refs[:-1]
    rows, width = q_ref.shape
    half = kv_refs[0].shape[1] // 2
    kv_heads = half // HD
    heads = width // HD
    repeat = heads // kv_heads
    scale = 1.0 / HD**0.5
    pieces = len(kv_refs)
    row_pos = base_ref[0] * rows + lax.broadcasted_iota(jnp.int32, (rows, rows), 0)
    col_pos = lax.broadcasted_iota(jnp.int32, (rows, rows), 1)
    bias = jnp.concatenate(
        [
            jnp.where(col_pos + base_ref[p] * rows <= row_pos, 0.0, -jnp.inf)
            for p in range(pieces)
        ],
        axis=1,
    )
    for g in range(kv_heads):
        keys = jnp.concatenate([r[:, g * HD : (g + 1) * HD] for r in kv_refs], axis=0)
        vals = jnp.concatenate(
            [r[:, half + g * HD : half + (g + 1) * HD] for r in kv_refs], axis=0
        )
        for h in range(g * repeat, (g + 1) * repeat):
            cols = slice(h * HD, (h + 1) * HD)
            scores = lax.dot_general(q_ref[:, cols], keys, NT, preferred_element_type=F32)
            scores = scores * scale + bias
            top = jnp.max(scores, axis=1, keepdims=True)
            exps = jnp.exp(scores - top)
            total = jnp.sum(exps, axis=1, keepdims=True)
            mixed = jnp.dot(exps.astype(BF16), vals, preferred_element_type=F32)
            out_ref[:, cols] = (mixed / total).astype(BF16)


def attend(base, q, kv):
    rows, width = q.shape
    keys = rows * len(kv)
    return pl.pallas_call(
        attention_kernel,
        in_specs=[SMEM] + [VMEM] * (1 + len(kv)),
        out_specs=VMEM,
        out_shape=jax.ShapeDtypeStruct((rows, width), BF16),
        cost_estimate=pl.CostEstimate(
            flops=4 * rows * keys * width, bytes_accessed=4 * rows * width, transcendentals=0
        ),
        name="attention",
    )(base, q, *kv)


def routing_rows(shard, gates, local, slots):
    tokens, lanes = gates.shape
    lane = lax.broadcasted_iota(jnp.int32, (local, lanes), 1)
    mine = shard * local + lax.broadcasted_iota(jnp.int32, (local, lanes), 0)
    columns = ((lane == mine) | (lane == mine + EXPERTS)).astype(BF16)
    weight = lax.dot_general(columns, gates, NT, preferred_element_type=F32)
    live = weight > 0
    earlier = lax.broadcasted_iota(jnp.int32, (tokens, tokens), 0)
    earlier = (earlier < lax.broadcasted_iota(jnp.int32, (tokens, tokens), 1)).astype(BF16)
    rank = jnp.dot(live.astype(BF16), earlier, preferred_element_type=F32)
    slot = lax.broadcasted_iota(jnp.int32, (slots, tokens), 0).astype(F32)
    picks, scales = [], []
    for e in range(local):
        pick = jnp.where((slot == rank[e : e + 1]) & live[e : e + 1], 1.0, 0.0)
        picks.append(pick)
        scales.append(jnp.sum(pick * weight[e : e + 1], axis=1, keepdims=True))
    return jnp.concatenate(picks, axis=0), jnp.concatenate(scales, axis=0)


def experts_kernel(shard_ref, *refs, count, slots):
    pieces = refs[:count]
    weights = refs[count : count + 3]
    outs = refs[count + 3 : 2 * count + 3]
    held, sems, tokens_scr, rows_scr, back_scr, scale_scr, pick_scr = refs[2 * count + 3 :]
    gate_scr, up_scr, down_scr = held
    local, width, hidden = gate_scr.shape
    piece = pieces[0].shape[0]
    both = 2 * width

    def copy(which, e):
        return pltpu.make_async_copy(
            weights[which].at[e], held[which].at[e], sems.at[which, e]
        )

    for e in range(local):
        for which in range(3):
            copy(which, e).start()

    for p in range(count):
        tokens_scr[p * piece : (p + 1) * piece] = pieces[p][:, :both]
    gates = jnp.concatenate([r[:, both:] for r in pieces], axis=0)
    picks, scales = routing_rows(shard_ref[0], gates, local, slots)
    scale_scr[...] = jnp.broadcast_to(scales, scale_scr.shape)
    high = scales.astype(BF16).astype(F32)
    for i, part in enumerate((picks, picks * high, picks * (scales - high))):
        pick_scr[i] = jnp.transpose(part).astype(BF16)
    picks = picks.astype(BF16)
    chunk = 512
    for c in range(0, both, chunk):
        rows_scr[:, c : c + chunk] = jnp.dot(
            picks, tokens_scr[:, c : c + chunk], preferred_element_type=F32
        ).astype(BF16)

    @pl.loop(0, local)
    def _(e):
        mine = pl.ds(pl.multiple_of(e * slots, slots), slots)
        for which in range(3):
            copy(which, e).wait()
        scale = scale_scr[mine, :1]
        entry = jnp.concatenate([gate_scr[e], up_scr[e]], axis=1)
        hidden_both = jnp.dot(rows_scr[mine, :width], entry, preferred_element_type=F32)
        hgate, hup = hidden_both[:, :hidden], hidden_both[:, hidden:]
        sig = jax.nn.sigmoid(hgate)
        silu = hgate * sig
        activated = (silu * hup).astype(BF16)
        back_scr[mine, :width] = jnp.dot(
            activated, down_scr[e], preferred_element_type=F32
        ).astype(BF16)
        row_grad = (rows_scr[mine, width:].astype(F32) * scale).astype(BF16)
        grad_act = lax.dot_general(row_grad, down_scr[e], NT, preferred_element_type=F32)
        grad_gate = (grad_act * hup * sig * (1.0 + hgate * (1.0 - sig))).astype(BF16)
        grad_up = (grad_act * silu).astype(BF16)
        grads = jnp.concatenate([grad_gate, grad_up], axis=1)
        entry = jnp.concatenate([gate_scr[e], up_scr[e]], axis=1)
        back_scr[mine, width:] = lax.dot_general(
            grads, entry, NT, preferred_element_type=F32
        ).astype(BF16)

    for c in range(0, both, chunk):
        rows = back_scr[:, c : c + chunk]
        if c < width:
            total = jnp.dot(pick_scr[1], rows, preferred_element_type=F32)
            total = total + jnp.dot(pick_scr[2], rows, preferred_element_type=F32)
        else:
            total = jnp.dot(pick_scr[0], rows, preferred_element_type=F32)
        total = total.astype(BF16)
        for p in range(count):
            outs[p][:, c : c + chunk] = total[p * piece : (p + 1) * piece]


def experts(shard, pieces, w_gate, w_up, w_down):
    count = len(pieces)
    local, width, hidden = w_gate.shape
    piece = pieces[0].shape[0]
    tokens = count * piece
    slots = -(-CAP * count // 16) * 16
    scratch = [
        tuple(pltpu.VMEM(w.shape, BF16) for w in (w_gate, w_up, w_down)),
        pltpu.SemaphoreType.DMA((3, local)),
        pltpu.VMEM((tokens, 2 * width), BF16),
        pltpu.VMEM((local * slots, 2 * width), BF16),
        pltpu.VMEM((local * slots, 2 * width), BF16),
        pltpu.VMEM((local * slots, 128), F32),
        pltpu.VMEM((3, tokens, local * slots), BF16),
    ]
    held_bytes = 6 * local * width * hidden + 4 * width * (tokens + 2 * local * slots)
    return pl.pallas_call(
        functools.partial(experts_kernel, count=count, slots=slots),
        in_specs=[SMEM] + [VMEM] * count + [pl.BlockSpec(memory_space=pl.ANY)] * 3,
        out_specs=[VMEM] * count,
        out_shape=[jax.ShapeDtypeStruct((piece, 2 * width), BF16)] * count,
        scratch_shapes=scratch,
        compiler_params=pltpu.CompilerParams(vmem_limit_bytes=held_bytes + 10 * 2**20),
        cost_estimate=pl.CostEstimate(
            flops=12 * local * slots * width * hidden,
            bytes_accessed=6 * local * width * hidden,
            transcendentals=0,
        ),
        name="experts",
    )(shard, *pieces, w_gate, w_up, w_down)


def parent(offset):
    return offset & (offset - 1)


def spread(rows):
    near = [rows]
    for d in range(1, lax.axis_size("seq")):
        near.append(swap(near[parent(d)], "seq", d - parent(d)))
    pieces = list(near)
    for t in range(1, lax.axis_size("tp")):
        pieces += [swap(a, "tp", t) for a in near]
    return pieces


def collect(pieces):
    seq, tp = lax.axis_size("seq"), lax.axis_size("tp")
    terms = [[pieces[d]] for d in range(seq)]
    for d in reversed(range(seq)):
        terms[d] += [swap(pieces[t * seq + d], "tp", t) for t in range(1, tp)]
        total = sum(a.astype(F32) for a in terms[d]).astype(BF16)
        if d:
            terms[d] = []
            terms[parent(d)].append(swap(total, "seq", d - parent(d)))
        if d and d % 8 == 0:
            pieces, terms = lax.optimization_barrier((pieces, terms))
    return total


def shards(queries, keys, values, moe_x, expert_ids, gates, grad_out, w_gate, w_up, w_down):
    group = lax.axis_index("group")
    shard = (lax.axis_index("seq") * lax.axis_size("tp") + lax.axis_index("tp")).reshape(1)
    pieces = spread(pack_rows(expert_ids[0].T, gates[0].T, moe_x[0], grad_out[0]))
    kv = jnp.concatenate([keys[0], values[0]], axis=1)
    offsets = range(lax.axis_size("group"))
    kv_pieces = [kv] + [swap(kv, "group", d) for d in offsets[1:]]
    base = jnp.stack([group ^ d for d in offsets])
    attn_out = attend(base, queries[0], kv_pieces)
    total = collect(experts(shard, pieces, w_gate, w_up, w_down))
    width = moe_x.shape[-1]
    return attn_out[None], total[None, :, :width], total[None, :, width:]


def solution(mesh):
    rows = P("seq", "group", "tp")
    tokens = P("group", ("seq", "tp"), None)
    experts = P(("seq", "tp"), None, None)
    return jax.shard_map(
        shards,
        mesh=mesh,
        in_specs=(rows, rows, rows, tokens, tokens, tokens, tokens, experts, experts, experts),
        out_specs=(rows, tokens, tokens),
        check_vma=False,
    )
```

time: 158 us -> 82.8 us (0.52)
  local copies, waits for them, and re-layouts: 66.5 us -> 2.25 us
  starting transfers between devices: 42.6 us -> 21.5 us
  waiting for transfers between devices: 9.24 us -> 24.8 us
  Pallas kernels: 36.6 us -> 32.4 us
    unnamed x47 -> x14, local copies, waits for them, and re-layouts: 66.5 us -> 1.59 us
    ppermute x31 -> x17, starting transfers between devices: 42.6 us -> 21.5 us  [swap(): return lax.ppermute(array, axis, [(i, i ^ offset) for i in range(count)])]
    ppermute x31 -> x17, waiting for transfers between devices: 9.24 us -> 24.8 us  [swap(): return lax.ppermute(array, axis, [(i, i ^ offset) for i in range(count)])]
    pallas_call x3 -> x2, Pallas kernels: 30.2 us -> 26.1 us  [the longest x1 24.4 us: experts(): pl.pallas_call(functools.partial(experts_kernel, count=count, slots=slots...]
  transfers between devices with their start and end apart: 31 -> 17, of which waited for: 8 -> 9; matrix products, arithmetic and copies ran while one was open for 1% -> 1% of each run, Pallas kernels for 22% -> 8%
where the time goes in v2:
time: 82.8 us; the launch traced here: 82.6 us
  Pallas kernels  32.4 us (39%)
  waiting for transfers between devices  24.8 us (30%)
  starting transfers between devices  21.5 us (26%)
  local copies, waits for them, and re-layouts  2.25 us (3%)
  other arithmetic  0.86 us (1%)
    ppermute x17, waiting for transfers between devices, swap(): return lax.ppermute(array, axis, [(i, i ^ offset) for i in range(count)])  24.8 us
    pallas_call x1, Pallas kernels, experts(): pl.pallas_call(functools.partial(experts_kernel, count=count, slots=slots...  24.4 us
    ppermute x17, starting transfers between devices, swap(): return lax.ppermute(array, axis, [(i, i ^ offset) for i in range(count)])  21.5 us
    pallas_call x1, Pallas kernels, attend(): pl.pallas_call(attention_kernel, in_specs=[SMEM] + [VMEM] * (1 + len(kv))...  6.36 us
  transfers between devices with their start and end apart: 17, of which 9 were waited for; matrix products, arithmetic and copies ran while one was open for 1% of the time, Pallas kernels for 8%

profile of v2, /device:TPU:0, one launch (start us, length us, event | category | flops | bytes accessed | tf_op | source)
XLA Modules:
  0.0 82.6 jit_solution(13354343319502235534)
XLA Ops:
  0.6 1.7 %pack_rows.1.refs_0_ = bf16[16,4224]{1,0:T(8,128)(2,1)} custom-call(s32[8,16]{1,0:T(8,128)} %bitcast.25, f32[8,16]{1,0:T(8,128)} %bitcast.26, bf16[16,2048]{1,0:T(8,128)(2,1)} %bitcast.21, bf16[16,2048]{1,0:T(8,128)(2,1)} %bitcast.22), custom_call_target="tpu_custom_call" | custom-call | tf_op jit(solution)/shard_map/pack_rows/pallas_call | solution.py:43
  2.3 4.0 %collective-permute-start.4 = (bf16[16,4224]{1,0:T(8,128)(2,1)}, bf16[16,4224]{1,0:T(8,128)(2,1)S(1)}, u32[]{:S(2)}, u32[]{:S(2)}) collective-permute-start(bf16[16,4224]{1,0:T(8,128)(2,1)} %pack_rows.1.refs_0_), channel_id=1, source_target_pairs={{0,4},{2,6},{4,0},{6,2},{1,5},{3,7},{5,1},{7,3},{8,12},{10,14},{12... | collective-permute-start | bytes 405512 | tf_op jit(solution)/shard_map/ppermute | solution.py:24
  6.3 1.6 %collective-permute-start.3 = (bf16[16,4224]{1,0:T(8,128)(2,1)}, bf16[16,4224]{1,0:T(8,128)(2,1)S(1)}, u32[]{:S(2)}, u32[]{:S(2)}) collective-permute-start(bf16[16,4224]{1,0:T(8,128)(2,1)} %pack_rows.1.refs_0_), channel_id=1, source_target_pairs={{0,2},{2,0},{4,6},{6,4},{1,3},{3,1},{5,7},{7,5},{8,10},{10,8},{12,... | collective-permute-start | bytes 405512 | tf_op jit(solution)/shard_map/ppermute | solution.py:24
  7.9 5.2 %collective-permute-done.4.refs_2_ = bf16[16,4224]{1,0:T(8,128)(2,1)S(1)} collective-permute-done((bf16[16,4224]{1,0:T(8,128)(2,1)}, bf16[16,4224]{1,0:T(8,128)(2,1)S(1)}, u32[]{:S(2)}, u32[]{:S(2)}) %collective-permute-start.4) | collective-permute-done | bytes 135200 | tf_op jit(solution)/shard_map/ppermute | solution.py:24
  13.1 0.7 collective-permute-start.5
  13.8 1.5 %collective-permute-start.6 = (bf16[16,4224]{1,0:T(8,128)(2,1)}, bf16[16,4224]{1,0:T(8,128)(2,1)S(1)}, u32[]{:S(2)}, u32[]{:S(2)}) collective-permute-start(bf16[16,4224]{1,0:T(8,128)(2,1)} %pack_rows.1.refs_0_), channel_id=1, source_target_pairs={{0,1},{1,0},{2,3},{3,2},{4,5},{5,4},{6,7},{7,6},{8,9},{9,8},{10,11... | collective-permute-start | bytes 405512 | tf_op jit(solution)/shard_map/ppermute | solution.py:24
  15.4 0.5 collective-permute-start.8
  15.9 0.0 collective-permute-done.3.refs_1_
  15.9 1.5 %collective-permute-start.7 = (bf16[16,4224]{1,0:T(8,128)(2,1)S(1)}, bf16[16,4224]{1,0:T(8,128)(2,1)S(1)}, u32[]{:S(2)}, u32[]{:S(2)}) collective-permute-start(bf16[16,4224]{1,0:T(8,128)(2,1)S(1)} %collective-permute-done.3.refs_1_), channel_id=1, source_target_pairs={{0,1},{1,0},{2,3},{3,2},{4,5},{5,4},{6,7},{7,6},{8,9},{9,8},{10,11... | collective-permute-start | bytes 405512 | tf_op jit(solution)/shard_map/ppermute | solution.py:24
  17.4 0.7 collective-permute-done.5.refs_3_
  18.1 1.6 %collective-permute-start.9 = (bf16[16,4224]{1,0:T(8,128)(2,1)S(1)}, bf16[16,4224]{1,0:T(8,128)(2,1)S(1)}, u32[]{:S(2)}, u32[]{:S(2)}) collective-permute-start(bf16[16,4224]{1,0:T(8,128)(2,1)S(1)} %collective-permute-done.5.refs_3_), channel_id=1, source_target_pairs={{0,1},{1,0},{2,3},{3,2},{4,5},{5,4},{6,7},{7,6},{8,9},{9,8},{10,11... | collective-permute-start | bytes 405512 | tf_op jit(solution)/shard_map/ppermute | solution.py:24
  19.7 0.8 %collective-permute-done.6.refs_4_ = bf16[16,4224]{1,0:T(8,128)(2,1)S(1)} collective-permute-done((bf16[16,4224]{1,0:T(8,128)(2,1)}, bf16[16,4224]{1,0:T(8,128)(2,1)S(1)}, u32[]{:S(2)}, u32[]{:S(2)}) %collective-permute-start.6) | collective-permute-done | bytes 135200 | tf_op jit(solution)/shard_map/ppermute | solution.py:24
  20.5 2.9 %collective-permute-done.8.refs_6_ = bf16[16,4224]{1,0:T(8,128)(2,1)S(1)} collective-permute-done((bf16[16,4224]{1,0:T(8,128)(2,1)S(1)}, bf16[16,4224]{1,0:T(8,128)(2,1)S(1)}, u32[]{:S(2)}, u32[]{:S(2)}) %collective-permute-start.8) | collective-permute-done | bytes 135200 | tf_op jit(solution)/shard_map/ppermute | solution.py:24
  23.4 2.9 %collective-permute-done.7.refs_5_ = bf16[16,4224]{1,0:T(8,128)(2,1)S(1)} collective-permute-done((bf16[16,4224]{1,0:T(8,128)(2,1)S(1)}, bf16[16,4224]{1,0:T(8,128)(2,1)S(1)}, u32[]{:S(2)}, u32[]{:S(2)}) %collective-permute-start.7) | collective-permute-done | bytes 135200 | tf_op jit(solution)/shard_map/ppermute | solution.py:24
  26.3 1.6 %collective-permute-done.9.refs_7_ = bf16[16,4224]{1,0:T(8,128)(2,1)S(1)} collective-permute-done((bf16[16,4224]{1,0:T(8,128)(2,1)S(1)}, bf16[16,4224]{1,0:T(8,128)(2,1)S(1)}, u32[]{:S(2)}, u32[]{:S(2)}) %collective-permute-start.9) | collective-permute-done | bytes 135200 | tf_op jit(solution)/shard_map/ppermute | solution.py:24
  28.0 0.0 copy-start
  28.0 0.9 %copy-done = bf16[16,4224]{1,0:T(8,128)(2,1)S(1)} copy-done((bf16[16,4224]{1,0:T(8,128)(2,1)S(1)}, bf16[16,4224]{1,0:T(8,128)(2,1)}, u32[]{:S(2)}) %copy-start) | copy-done | bytes 135192
  28.9 0.0 copy-start.2
  28.9 0.0 copy-start.3
  28.9 24.4 %experts.1 = (bf16[16,4096]{1,0:T(8,128)(2,1)S(1)}, bf16[16,4096]{1,0:T(8,128)(2,1)S(1)}, bf16[16,4096]{1,0:T(8,128)(2,1)S(1)}, bf16[16,4096]{1,0:T(8,128)(2,1)S...) custom-call(s32[1]{0:T(128)} %bitcast.8.shard_ref, ...), custom_call_target="tpu_custom_call" | custom-call | flops 2415919104 | bytes 37748736 | tf_op jit(solution)/shard_map/experts/pallas_call | solution.py:208
  53.3 1.6 %collective-permute-start.10 = (bf16[16,4096]{1,0:T(8,128)(2,1)S(1)}, bf16[16,4096]{1,0:T(8,128)(2,1)S(1)}, u32[]{:S(2)}, u32[]{:S(2)}) collective-permute-start(bf16[16,4096]{1,0:T(8,128)(2,1)S(1)} %get-tuple-element.14), channel_id=1, source_target_pairs={{0,1},{1,0},{2,3},{3,2},{4,5},{5,4},{6,7},{7,6},{8,9},{9,8},{10,11... | collective-permute-start | bytes 393224 | tf_op jit(solution)/shard_map/ppermute | solution.py:24
  54.9 0.0 copy-done.2
  54.9 0.0 copy-done.3
  54.9 0.0 copy-start.1
  54.9 0.1 collective-permute-start
  55.0 1.6 %collective-permute-start.1 = (bf16[128,512]{1,0:T(8,128)(2,1)S(1)}, bf16[128,512]{1,0:T(8,128)(2,1)S(1)}, u32[]{:S(2)}, u32[]{:S(2)}) collective-permute-start(bf16[128,512]{1,0:T(8,128)(2,1)S(1)} %pad_maximum_fusion.refs_0_), channel_id=1, source_target_pairs={{0,16},{8,24},{16,0},{24,8},{1,17},{9,25},{17,1},{25,9},{2,18},{10... | collective-permute-start | bytes 393224 | tf_op jit(solution)/shard_map/ppermute | solution.py:24
  56.6 0.3 collective-permute-start.2
  56.9 0.5 collective-permute-start.12
  57.4 1.0 %collective-permute-done.10 = bf16[16,4096]{1,0:T(8,128)(2,1)S(1)} collective-permute-done((bf16[16,4096]{1,0:T(8,128)(2,1)S(1)}, bf16[16,4096]{1,0:T(8,128)(2,1)S(1)}, u32[]{:S(2)}, u32[]{:S(2)}) %collective-permute-start.10) | collective-permute-done | bytes 131104 | tf_op jit(solution)/shard_map/ppermute | solution.py:24
  58.3 1.5 %collective-permute-start.14 = (bf16[16,4096]{1,0:T(8,128)(2,1)S(1)}, bf16[16,4096]{1,0:T(8,128)(2,1)S(1)}, u32[]{:S(2)}, u32[]{:S(2)}) collective-permute-start(bf16[16,4096]{1,0:T(8,128)(2,1)S(1)} %get-tuple-element.17), channel_id=1, source_target_pairs={{0,1},{1,0},{2,3},{3,2},{4,5},{5,4},{6,7},{7,6},{8,9},{9,8},{10,11... | collective-permute-start | bytes 393224 | tf_op jit(solution)/shard_map/ppermute | solution.py:24
  59.9 5.5 %collective-permute-done.14 = bf16[16,4096]{1,0:T(8,128)(2,1)S(1)} collective-permute-done((bf16[16,4096]{1,0:T(8,128)(2,1)S(1)}, bf16[16,4096]{1,0:T(8,128)(2,1)S(1)}, u32[]{:S(2)}, u32[]{:S(2)}) %collective-permute-start.14) | collective-permute-done | bytes 131104 | tf_op jit(solution)/shard_map/ppermute | solution.py:24
  65.4 0.3 collective-permute-start.11
  65.7 0.0 collective-permute-done.12
  65.8 0.6 collective-permute-start.16
  66.3 4.0 %collective-permute-done.11 = bf16[16,4096]{1,0:T(8,128)(2,1)S(1)} collective-permute-done((bf16[16,4096]{1,0:T(8,128)(2,1)S(1)}, bf16[16,4096]{1,0:T(8,128)(2,1)S(1)}, u32[]{:S(2)}, u32[]{:S(2)}) %collective-permute-start.11) | collective-permute-done | bytes 131104 | tf_op jit(solution)/shard_map/ppermute | solution.py:24
  70.4 0.3 collective-permute-start.15
  70.7 0.1 add_convert_fusion.2
  70.7 0.0 collective-permute-done.refs_1_
  70.7 0.0 copy-start.4
  70.7 3.4 %collective-permute-start.13 = (bf16[16,4096]{1,0:T(8,128)(2,1)S(1)}, bf16[16,4096]{1,0:T(8,128)(2,1)S(1)}, u32[]{:S(2)}, u32[]{:S(2)}) collective-permute-start(bf16[16,4096]{1,0:T(8,128)(2,1)S(1)} %add_convert_fusion.2), channel_id=1, source_target_pairs={{0,4},{2,6},{4,0},{6,2},{1,5},{3,7},{5,1},{7,3},{8,12},{10,14},{12... | collective-permute-start | bytes 393224 | tf_op jit(solution)/shard_map/ppermute | solution.py:24
  74.1 0.6 pad_add_fusion.base_ref
  74.8 0.0 collective-permute-done.1.refs_2_
  74.8 0.0 copy-start.5
  74.8 0.0 collective-permute-done.2.refs_3_
  74.8 0.0 copy-start.6
  74.8 0.0 copy-done.1
  74.8 0.0 copy-done.4
  74.8 0.6 copy-done.5
  75.4 0.1 copy-done.6
  75.5 6.4 %attention.1 = bf16[128,2048]{1,0:T(8,128)(2,1)} custom-call(s32[4]{0:T(128)} %pad_add_fusion.base_ref, bf16[128,2048]{1,0:T(8,128)(2,1)} %bitcast.27, bf16[128,512]{1,0:T(8,128)(2,1)} %copy-done.1, bf16[128,512]{1,0:T(8,128)(2,1)} %copy-done.4, bf16[128,512]{1,0:T(8,128)(2,1)} %copy-done.5, bf16[128,512]{1,0:T(8,128)(2,1)} %copy-done.6), custom_call_target="tpu_custom_call" | custom-call | flops 536870912 | bytes 1048576 | tf_op jit(solution)/shard_map/attention/pallas_call | solution.py:90
  81.8 0.0 collective-permute-done.16
  81.8 0.0 collective-permute-done.15
  81.8 0.0 collective-permute-done.13
  81.8 0.1 add_convert_fusion
  81.9 0.7 slice_bitcast_fusion
  (3 shorter events, 0.1 us)
Async XLA Ops:
  2.3 10.8 %collective-permute-start.4 = (bf16[16,4224]{1,0:T(8,128)(2,1)}, bf16[16,4224]{1,0:T(8,128)(2,1)S(1)}, u32[]{:S(2)}, u32[]{:S(2)}) collective-permute-start(bf16[16,4224]{1,0:T(8,128)(2,1)} %pack_rows.1.refs_0_), channel_id=1, source_target_pairs={{0,4},{2,6},{4,0},{6,2},{1,5},{3,7},{5,1},{7,3},{8,12},{10,14},{12... | collective-permute-start | bytes 405512 | tf_op jit(solution)/shard_map/ppermute | solution.py:24
  6.3 9.5 %collective-permute-start.3 = (bf16[16,4224]{1,0:T(8,128)(2,1)}, bf16[16,4224]{1,0:T(8,128)(2,1)S(1)}, u32[]{:S(2)}, u32[]{:S(2)}) collective-permute-start(bf16[16,4224]{1,0:T(8,128)(2,1)} %pack_rows.1.refs_0_), channel_id=1, source_target_pairs={{0,2},{2,0},{4,6},{6,4},{1,3},{3,1},{5,7},{7,5},{8,10},{10,8},{12,... | collective-permute-start | bytes 405512 | tf_op jit(solution)/shard_map/ppermute | solution.py:24
  13.1 5.0 %collective-permute-start.5 = (bf16[16,4224]{1,0:T(8,128)(2,1)S(1)}, bf16[16,4224]{1,0:T(8,128)(2,1)S(1)}, u32[]{:S(2)}, u32[]{:S(2)}) collective-permute-start(bf16[16,4224]{1,0:T(8,128)(2,1)S(1)} %collective-permute-done.4.refs_2_), channel_id=1, source_target_pairs={{0,2},{2,0},{4,6},{6,4},{1,3},{3,1},{5,7},{7,5},{8,10},{10,8},{12,... | collective-permute-start | bytes 405512 | tf_op jit(solution)/shard_map/ppermute | solution.py:24
  13.8 6.7 %collective-permute-start.6 = (bf16[16,4224]{1,0:T(8,128)(2,1)}, bf16[16,4224]{1,0:T(8,128)(2,1)S(1)}, u32[]{:S(2)}, u32[]{:S(2)}) collective-permute-start(bf16[16,4224]{1,0:T(8,128)(2,1)} %pack_rows.1.refs_0_), channel_id=1, source_target_pairs={{0,1},{1,0},{2,3},{3,2},{4,5},{5,4},{6,7},{7,6},{8,9},{9,8},{10,11... | collective-permute-start | bytes 405512 | tf_op jit(solution)/shard_map/ppermute | solution.py:24
  15.4 8.1 %collective-permute-start.8 = (bf16[16,4224]{1,0:T(8,128)(2,1)S(1)}, bf16[16,4224]{1,0:T(8,128)(2,1)S(1)}, u32[]{:S(2)}, u32[]{:S(2)}) collective-permute-start(bf16[16,4224]{1,0:T(8,128)(2,1)S(1)} %collective-permute-done.4.refs_2_), channel_id=1, source_target_pairs={{0,1},{1,0},{2,3},{3,2},{4,5},{5,4},{6,7},{7,6},{8,9},{9,8},{10,11... | collective-permute-start | bytes 405512 | tf_op jit(solution)/shard_map/ppermute | solution.py:24
  15.9 10.5 %collective-permute-start.7 = (bf16[16,4224]{1,0:T(8,128)(2,1)S(1)}, bf16[16,4224]{1,0:T(8,128)(2,1)S(1)}, u32[]{:S(2)}, u32[]{:S(2)}) collective-permute-start(bf16[16,4224]{1,0:T(8,128)(2,1)S(1)} %collective-permute-done.3.refs_1_), channel_id=1, source_target_pairs={{0,1},{1,0},{2,3},{3,2},{4,5},{5,4},{6,7},{7,6},{8,9},{9,8},{10,11... | collective-permute-start | bytes 405512 | tf_op jit(solution)/shard_map/ppermute | solution.py:24
  18.1 9.8 %collective-permute-start.9 = (bf16[16,4224]{1,0:T(8,128)(2,1)S(1)}, bf16[16,4224]{1,0:T(8,128)(2,1)S(1)}, u32[]{:S(2)}, u32[]{:S(2)}) collective-permute-start(bf16[16,4224]{1,0:T(8,128)(2,1)S(1)} %collective-permute-done.5.refs_3_), channel_id=1, source_target_pairs={{0,1},{1,0},{2,3},{3,2},{4,5},{5,4},{6,7},{7,6},{8,9},{9,8},{10,11... | collective-permute-start | bytes 405512 | tf_op jit(solution)/shard_map/ppermute | solution.py:24
  28.0 0.9 %copy-start = (bf16[16,4224]{1,0:T(8,128)(2,1)S(1)}, bf16[16,4224]{1,0:T(8,128)(2,1)}, u32[]{:S(2)}) copy-start(bf16[16,4224]{1,0:T(8,128)(2,1)} %pack_rows.1.refs_0_) | copy-start | bytes 405508
  28.9 26.0 %copy-start.2 = (bf16[1,128,256]{2,1,0:T(8,128)(2,1)S(1)}, bf16[1,128,256]{2,1,0:T(8,128)(2,1)}, u32[]{:S(2)}) copy-start(bf16[1,128,256]{2,1,0:T(8,128)(2,1)} %param.12) | copy-start | bytes 196612
  28.9 26.0 %copy-start.3 = (bf16[1,128,256]{2,1,0:T(8,128)(2,1)S(1)}, bf16[1,128,256]{2,1,0:T(8,128)(2,1)}, u32[]{:S(2)}) copy-start(bf16[1,128,256]{2,1,0:T(8,128)(2,1)} %param.11) | copy-start | bytes 196612
  53.3 5.0 %collective-permute-start.10 = (bf16[16,4096]{1,0:T(8,128)(2,1)S(1)}, bf16[16,4096]{1,0:T(8,128)(2,1)S(1)}, u32[]{:S(2)}, u32[]{:S(2)}) collective-permute-start(bf16[16,4096]{1,0:T(8,128)(2,1)S(1)} %get-tuple-element.14), channel_id=1, source_target_pairs={{0,1},{1,0},{2,3},{3,2},{4,5},{5,4},{6,7},{7,6},{8,9},{9,8},{10,11... | collective-permute-start | bytes 393224 | tf_op jit(solution)/shard_map/ppermute | solution.py:24
  54.9 19.9 %copy-start.1 = (bf16[128,512]{1,0:T(8,128)(2,1)}, bf16[128,512]{1,0:T(8,128)(2,1)S(1)}, u32[]{:S(2)}) copy-start(bf16[128,512]{1,0:T(8,128)(2,1)S(1)} %pad_maximum_fusion.refs_0_) | copy-start | bytes 393220
  54.9 15.8 %collective-permute-start = (bf16[128,512]{1,0:T(8,128)(2,1)S(1)}, bf16[128,512]{1,0:T(8,128)(2,1)S(1)}, u32[]{:S(2)}, u32[]{:S(2)}) collective-permute-start(bf16[128,512]{1,0:T(8,128)(2,1)S(1)} %pad_maximum_fusion.refs_0_), channel_id=1, source_target_pairs={{0,8},{8,0},{16,24},{24,16},{1,9},{9,1},{17,25},{25,17},{2,10},{10... | collective-permute-start | bytes 393224 | tf_op jit(solution)/shard_map/ppermute | solution.py:24
  55.0 19.8 %collective-permute-start.1 = (bf16[128,512]{1,0:T(8,128)(2,1)S(1)}, bf16[128,512]{1,0:T(8,128)(2,1)S(1)}, u32[]{:S(2)}, u32[]{:S(2)}) collective-permute-start(bf16[128,512]{1,0:T(8,128)(2,1)S(1)} %pad_maximum_fusion.refs_0_), channel_id=1, source_target_pairs={{0,16},{8,24},{16,0},{24,8},{1,17},{9,25},{17,1},{25,9},{2,18},{10... | collective-permute-start | bytes 393224 | tf_op jit(solution)/shard_map/ppermute | solution.py:24
  56.6 18.2 %collective-permute-start.2 = (bf16[128,512]{1,0:T(8,128)(2,1)S(1)}, bf16[128,512]{1,0:T(8,128)(2,1)S(1)}, u32[]{:S(2)}, u32[]{:S(2)}) collective-permute-start(bf16[128,512]{1,0:T(8,128)(2,1)S(1)} %pad_maximum_fusion.refs_0_), channel_id=1, source_target_pairs={{0,24},{8,16},{16,8},{24,0},{1,25},{9,17},{17,9},{25,1},{2,26},{10... | collective-permute-start | bytes 393224 | tf_op jit(solution)/shard_map/ppermute | solution.py:24
  56.9 8.9 %collective-permute-start.12 = (bf16[16,4096]{1,0:T(8,128)(2,1)S(1)}, bf16[16,4096]{1,0:T(8,128)(2,1)S(1)}, u32[]{:S(2)}, u32[]{:S(2)}) collective-permute-start(bf16[16,4096]{1,0:T(8,128)(2,1)S(1)} %get-tuple-element.15), channel_id=1, source_target_pairs={{0,1},{1,0},{2,3},{3,2},{4,5},{5,4},{6,7},{7,6},{8,9},{9,8},{10,11... | collective-permute-start | bytes 393224 | tf_op jit(solution)/shard_map/ppermute | solution.py:24
  58.3 7.1 %collective-permute-start.14 = (bf16[16,4096]{1,0:T(8,128)(2,1)S(1)}, bf16[16,4096]{1,0:T(8,128)(2,1)S(1)}, u32[]{:S(2)}, u32[]{:S(2)}) collective-permute-start(bf16[16,4096]{1,0:T(8,128)(2,1)S(1)} %get-tuple-element.17), channel_id=1, source_target_pairs={{0,1},{1,0},{2,3},{3,2},{4,5},{5,4},{6,7},{7,6},{8,9},{9,8},{10,11... | collective-permute-start | bytes 393224 | tf_op jit(solution)/shard_map/ppermute | solution.py:24
  65.4 5.0 %collective-permute-start.11 = (bf16[16,4096]{1,0:T(8,128)(2,1)S(1)}, bf16[16,4096]{1,0:T(8,128)(2,1)S(1)}, u32[]{:S(2)}, u32[]{:S(2)}) collective-permute-start(bf16[16,4096]{1,0:T(8,128)(2,1)S(1)} %add_convert_fusion.3), channel_id=1, source_target_pairs={{0,2},{2,0},{4,6},{6,4},{1,3},{3,1},{5,7},{7,5},{8,10},{10,8},{12,... | collective-permute-start | bytes 393224 | tf_op jit(solution)/shard_map/ppermute | solution.py:24
  65.8 16.1 %collective-permute-start.16 = (bf16[16,4096]{1,0:T(8,128)(2,1)S(1)}, bf16[16,4096]{1,0:T(8,128)(2,1)S(1)}, u32[]{:S(2)}, u32[]{:S(2)}) collective-permute-start(bf16[16,4096]{1,0:T(8,128)(2,1)S(1)} %get-tuple-element.18), channel_id=1, source_target_pairs={{0,1},{1,0},{2,3},{3,2},{4,5},{5,4},{6,7},{7,6},{8,9},{9,8},{10,11... | collective-permute-start | bytes 393224 | tf_op jit(solution)/shard_map/ppermute | solution.py:24
  70.4 11.4 %collective-permute-start.15 = (bf16[16,4096]{1,0:T(8,128)(2,1)S(1)}, bf16[16,4096]{1,0:T(8,128)(2,1)S(1)}, u32[]{:S(2)}, u32[]{:S(2)}) collective-permute-start(bf16[16,4096]{1,0:T(8,128)(2,1)S(1)} %add_convert_fusion.1), channel_id=1, source_target_pairs={{0,2},{2,0},{4,6},{6,4},{1,3},{3,1},{5,7},{7,5},{8,10},{10,8},{12,... | collective-permute-start | bytes 393224 | tf_op jit(solution)/shard_map/ppermute | solution.py:24
  70.7 4.0 %copy-start.4 = (bf16[128,512]{1,0:T(8,128)(2,1)}, bf16[128,512]{1,0:T(8,128)(2,1)S(1)}, u32[]{:S(2)}) copy-start(bf16[128,512]{1,0:T(8,128)(2,1)S(1)} %collective-permute-done.refs_1_) | copy-start | bytes 393220
  70.7 11.1 %collective-permute-start.13 = (bf16[16,4096]{1,0:T(8,128)(2,1)S(1)}, bf16[16,4096]{1,0:T(8,128)(2,1)S(1)}, u32[]{:S(2)}, u32[]{:S(2)}) collective-permute-start(bf16[16,4096]{1,0:T(8,128)(2,1)S(1)} %add_convert_fusion.2), channel_id=1, source_target_pairs={{0,4},{2,6},{4,0},{6,2},{1,5},{3,7},{5,1},{7,3},{8,12},{10,14},{12... | collective-permute-start | bytes 393224 | tf_op jit(solution)/shard_map/ppermute | solution.py:24
  74.8 0.6 copy-start.5
  74.8 0.7 copy-start.6

commit v3 on v2

--- a/solution.py
+++ b/solution.py
@@ -1,4 +1,5 @@
 import functools
+import math
 
 import jax
 import jax.numpy as jnp
@@ -24,7 +25,7 @@
     return lax.ppermute(array, axis, [(i, i ^ offset) for i in range(count)])
 
 
-def pack_kernel(ids_ref, gates_ref, x_ref, grad_ref, out_ref):
+def pack_kernel(ids_ref, gates_ref, x_ref, grad_ref, key_ref, value_ref, out_ref, kv_ref):
     rows, width = x_ref.shape
     topk = ids_ref.shape[0]
     expert = lax.broadcasted_iota(jnp.int32, (EXPERTS, rows), 0)
@@ -36,17 +37,23 @@
     out_ref[:, :width] = x_ref[...]
     out_ref[:, width : 2 * width] = grad_ref[...]
     out_ref[:, 2 * width :] = jnp.transpose(both).astype(BF16)
-
-
-def pack_rows(ids, gates, x, grad):
+    half = key_ref.shape[1]
+    kv_ref[:, :half] = key_ref[...]
+    kv_ref[:, half:] = value_ref[...]
+
+
+def pack(ids, gates, x, grad, keys, values):
     rows, width = x.shape
     return pl.pallas_call(
         pack_kernel,
-        in_specs=[VMEM] * 4,
-        out_specs=VMEM,
-        out_shape=jax.ShapeDtypeStruct((rows, 2 * (width + EXPERTS)), BF16),
-        name="pack_rows",
-    )(ids, gates, x, grad)
+        in_specs=[VMEM] * 6,
+        out_specs=[VMEM] * 2,
+        out_shape=[
+            jax.ShapeDtypeStruct((rows, 2 * (width + EXPERTS)), BF16),
+            jax.ShapeDtypeStruct((keys.shape[0], 2 * keys.shape[1]), BF16),
+        ],
+        name="pack",
+    )(ids, gates, x, grad, keys, values)
 
 
 def attention_kernel(base_ref, q_ref, *refs):
@@ -55,33 +62,28 @@
     rows, width = q_ref.shape
     half = kv_refs[0].shape[1] // 2
     kv_heads = half // HD
-    heads = width // HD
-    repeat = heads // kv_heads
-    scale = 1.0 / HD**0.5
-    pieces = len(kv_refs)
+    repeat = width // HD // kv_heads
+    scale = math.log2(math.e) / HD**0.5
     row_pos = base_ref[0] * rows + lax.broadcasted_iota(jnp.int32, (rows, rows), 0)
     col_pos = lax.broadcasted_iota(jnp.int32, (rows, rows), 1)
-    bias = jnp.concatenate(
-        [
-            jnp.where(col_pos + base_ref[p] * rows <= row_pos, 0.0, -jnp.inf)
-            for p in range(pieces)
-        ],
-        axis=1,
-    )
+    masks = [
+        jnp.where(col_pos + base_ref[p] * rows <= row_pos, 0.0, -jnp.inf)
+        for p in range(len(kv_refs))
+    ]
+    bias = jnp.concatenate(masks, axis=1)
     for g in range(kv_heads):
         keys = jnp.concatenate([r[:, g * HD : (g + 1) * HD] for r in kv_refs], axis=0)
         vals = jnp.concatenate(
             [r[:, half + g * HD : half + (g + 1) * HD] for r in kv_refs], axis=0
         )
+        vals = jnp.concatenate([vals, jnp.ones_like(vals)], axis=1)
         for h in range(g * repeat, (g + 1) * repeat):
             cols = slice(h * HD, (h + 1) * HD)
-            scores = lax.dot_general(q_ref[:, cols], keys, NT, preferred_element_type=F32)
-            scores = scores * scale + bias
+            scores = lax.dot_general(q_ref[:, cols], keys, NT, preferred_element_type=F32) + bias
             top = jnp.max(scores, axis=1, keepdims=True)
-            exps = jnp.exp(scores - top)
-            total = jnp.sum(exps, axis=1, keepdims=True)
-            mixed = jnp.dot(exps.astype(BF16), vals, preferred_element_type=F32)
-            out_ref[:, cols] = (mixed / total).astype(BF16)
+            probs = jnp.exp2((scores - top) * scale).astype(BF16)
+            mixed = jnp.dot(probs, vals, preferred_element_type=F32)
+            out_ref[:, cols] = (mixed[:, :HD] / mixed[:, HD:]).astype(BF16)
 
 
 def attend(base, q, kv):
@@ -152,30 +154,41 @@
             picks, tokens_scr[:, c : c + chunk], preferred_element_type=F32
         ).astype(BF16)
 
-    @pl.loop(0, local)
-    def _(e):
-        mine = pl.ds(pl.multiple_of(e * slots, slots), slots)
-        for which in range(3):
-            copy(which, e).wait()
-        scale = scale_scr[mine, :1]
-        entry = jnp.concatenate([gate_scr[e], up_scr[e]], axis=1)
-        hidden_both = jnp.dot(rows_scr[mine, :width], entry, preferred_element_type=F32)
-        hgate, hup = hidden_both[:, :hidden], hidden_both[:, hidden:]
-        sig = jax.nn.sigmoid(hgate)
-        silu = hgate * sig
-        activated = (silu * hup).astype(BF16)
-        back_scr[mine, :width] = jnp.dot(
-            activated, down_scr[e], preferred_element_type=F32
-        ).astype(BF16)
-        row_grad = (rows_scr[mine, width:].astype(F32) * scale).astype(BF16)
-        grad_act = lax.dot_general(row_grad, down_scr[e], NT, preferred_element_type=F32)
-        grad_gate = (grad_act * hup * sig * (1.0 + hgate * (1.0 - sig))).astype(BF16)
-        grad_up = (grad_act * silu).astype(BF16)
-        grads = jnp.concatenate([grad_gate, grad_up], axis=1)
-        entry = jnp.concatenate([gate_scr[e], up_scr[e]], axis=1)
-        back_scr[mine, width:] = lax.dot_general(
-            grads, entry, NT, preferred_element_type=F32
-        ).astype(BF16)
+    unroll = 2 if local % 2 == 0 else 1
+
+    @pl.loop(0, local // unroll)
+    def _(step):
+        state = []
+        for k in range(unroll):
+            e = step * unroll + k
+            for which in range(3):
+                copy(which, e).wait()
+        for k in range(unroll):
+            e = step * unroll + k
+            mine = pl.ds(pl.multiple_of(e * slots, slots), slots)
+            entry = jnp.concatenate([gate_scr[e], up_scr[e]], axis=1)
+            hidden_both = jnp.dot(rows_scr[mine, :width], entry, preferred_element_type=F32)
+            row_grad = (rows_scr[mine, width:].astype(F32) * scale_scr[mine, :1]).astype(BF16)
+            grad_act = lax.dot_general(row_grad, down_scr[e], NT, preferred_element_type=F32)
+            state.append((hidden_both, grad_act))
+        for k in range(unroll):
+            e = step * unroll + k
+            mine = pl.ds(pl.multiple_of(e * slots, slots), slots)
+            hidden_both, grad_act = state[k]
+            hgate, hup = hidden_both[:, :hidden], hidden_both[:, hidden:]
+            sig = jax.nn.sigmoid(hgate)
+            silu = hgate * sig
+            activated = (silu * hup).astype(BF16)
+            grad_gate = (grad_act * hup * sig * (1.0 + hgate * (1.0 - sig))).astype(BF16)
+            grad_up = (grad_act * silu).astype(BF16)
+            back_scr[mine, :width] = jnp.dot(
+                activated, down_scr[e], preferred_element_type=F32
+            ).astype(BF16)
+            grads = jnp.concatenate([grad_gate, grad_up], axis=1)
+            entry = jnp.concatenate([gate_scr[e], up_scr[e]], axis=1)
+            back_scr[mine, width:] = lax.dot_general(
+                grads, entry, NT, preferred_element_type=F32
+            ).astype(BF16)
 
     for c in range(0, both, chunk):
         rows = back_scr[:, c : c + chunk]
@@ -225,14 +238,17 @@
     return offset & (offset - 1)
 
 
-def spread(rows):
-    near = [rows]
+def spread(rows, held):
+    near, far = [rows], []
     for d in range(1, lax.axis_size("seq")):
-        near.append(swap(near[parent(d)], "seq", d - parent(d)))
-    pieces = list(near)
-    for t in range(1, lax.axis_size("tp")):
-        pieces += [swap(a, "tp", t) for a in near]
-    return pieces
+        block = swap(near[parent(d)], "seq", d - parent(d))
+        far.append([swap(near[d - 1], "tp", t) for t in range(1, lax.axis_size("tp"))])
+        if d > 1:
+            block, far[d - 2] = lax.optimization_barrier((block, far[d - 2]))
+        near.append(block)
+    far.append([swap(near[-1], "tp", t) for t in range(1, lax.axis_size("tp"))])
+    near[-1], result = held(near[-1])
+    return near + [a for blocks in zip(*far) for a in blocks], result
 
 
 def collect(pieces):
@@ -252,12 +268,17 @@
 def shards(queries, keys, values, moe_x, expert_ids, gates, grad_out, w_gate, w_up, w_down):
     group = lax.axis_index("group")
     shard = (lax.axis_index("seq") * lax.axis_size("tp") + lax.axis_index("tp")).reshape(1)
-    pieces = spread(pack_rows(expert_ids[0].T, gates[0].T, moe_x[0], grad_out[0]))
-    kv = jnp.concatenate([keys[0], values[0]], axis=1)
+    rows, kv = pack(expert_ids[0].T, gates[0].T, moe_x[0], grad_out[0], keys[0], values[0])
     offsets = range(lax.axis_size("group"))
     kv_pieces = [kv] + [swap(kv, "group", d) for d in offsets[1:]]
     base = jnp.stack([group ^ d for d in offsets])
-    attn_out = attend(base, queries[0], kv_pieces)
+
+    def attended(block):
+        block, starts = lax.optimization_barrier((block, base))
+        return block, attend(starts, queries[0], kv_pieces)
+
+    pieces, attn_out = spread(rows, attended)
+    pieces, attn_out = lax.optimization_barrier((pieces, attn_out))
     total = collect(experts(shard, pieces, w_gate, w_up, w_down))
     width = moe_x.shape[-1]
     return attn_out[None], total[None, :, :width], total[None, :, width:]

time: 82.8 us -> 73.6 us (0.89)
  waiting for transfers between devices: 24.8 us -> 20.7 us
  Pallas kernels: 32.4 us -> 28.3 us
    ppermute x17, waiting for transfers between devices: 24.8 us -> 20.7 us  [swap(): return lax.ppermute(array, axis, [(i, i ^ offset) for i in range(count)])]
    pallas_call x1, Pallas kernels: 6.36 us -> 3.55 us  [attend(): pl.pallas_call(attention_kernel, in_specs=[SMEM] + [VMEM] * (1 + len(kv))...]
    pallas_call x1, Pallas kernels: 24.4 us -> 23 us  [experts(): pl.pallas_call(functools.partial(experts_kernel, count=count, slots=slots...]
  transfers between devices with their start and end apart: 17 -> 17, of which waited for: 9 -> 8; matrix products, arithmetic and copies ran while one was open for 1% -> 1% of each run, Pallas kernels for 8% -> 5%
where the time goes in v3:
time: 73.6 us; the launch traced here: 73.4 us
  Pallas kernels  28.3 us (38%)
  starting transfers between devices  20.7 us (28%)
  waiting for transfers between devices  20.7 us (28%)
  local copies, waits for them, and re-layouts  2.27 us (3%)
  other arithmetic  0.8 us (1%)
    pallas_call x1, Pallas kernels, experts(): pl.pallas_call(functools.partial(experts_kernel, count=count, slots=slots...  23 us
    ppermute x17, starting transfers between devices, swap(): return lax.ppermute(array, axis, [(i, i ^ offset) for i in range(count)])  20.7 us
    ppermute x17, waiting for transfers between devices, swap(): return lax.ppermute(array, axis, [(i, i ^ offset) for i in range(count)])  20.7 us
    pallas_call x1, Pallas kernels, attend(): pl.pallas_call(attention_kernel, in_specs=[SMEM] + [VMEM] * (1 + len(kv))...  3.55 us
    pallas_call x1, Pallas kernels, pack(): pl.pallas_call(pack_kernel, in_specs=[VMEM] * 6, out_specs=[VMEM] * 2, ou...  1.71 us
    unnamed x8, local copies, waits for them, and re-layouts  1.61 us
  transfers between devices with their start and end apart: 17, of which 8 were waited for; matrix products, arithmetic and copies ran while one was open for 1% of the time, Pallas kernels for 5%

profile of v3, /device:TPU:0, one launch (start us, length us, event | category | flops | bytes accessed | tf_op | source)
XLA Modules:
  0.0 73.4 jit_solution(2941970662009939010)
XLA Ops:
  0.6 1.7 %pack.1 = (bf16[16,4224]{1,0:T(8,128)(2,1)}, bf16[128,512]{1,0:T(8,128)(2,1)}) custom-call(s32[8,16]{1,0:T(8,128)} %bitcast.25, f32[8,16]{1,0:T(8,128)} %bitcast.26, bf16[16,2048]{1,0:T(8,128)(2,1)} %bitcast.21, bf16[16,2048]{1,0:T(8,128)(2,1)} %bitcast.22, bf16[128,256]{1,0:T(8,128)(2,1)} %bitcast.23, bf16[128,256]{1,0:T(8,128)(2,1)} %bitcast.24), custom_call_target="tpu_custom_call" | custom-call | tf_op jit(solution)/shard_map/pack/pallas_call | solution.py:47
  2.3 3.0 %collective-permute-start.2 = (bf16[16,4224]{1,0:T(8,128)(2,1)}, bf16[16,4224]{1,0:T(8,128)(2,1)S(1)}, u32[]{:S(2)}, u32[]{:S(2)}) collective-permute-start(bf16[16,4224]{1,0:T(8,128)(2,1)} %get-tuple-element.37.refs_0_), channel_id=1, source_target_pairs={{0,1},{1,0},{2,3},{3,2},{4,5},{5,4},{6,7},{7,6},{8,9},{9,8},{10,11... | collective-permute-start | bytes 405512 | tf_op jit(solution)/shard_map/ppermute | solution.py:25
  5.3 2.6 %collective-permute-start.1 = (bf16[16,4224]{1,0:T(8,128)(2,1)}, bf16[16,4224]{1,0:T(8,128)(2,1)S(1)}, u32[]{:S(2)}, u32[]{:S(2)}) collective-permute-start(bf16[16,4224]{1,0:T(8,128)(2,1)} %get-tuple-element.37.refs_0_), channel_id=1, source_target_pairs={{0,4},{2,6},{4,0},{6,2},{1,5},{3,7},{5,1},{7,3},{8,12},{10,14},{12... | collective-permute-start | bytes 405512 | tf_op jit(solution)/shard_map/ppermute | solution.py:25
  7.9 1.6 %collective-permute-start = (bf16[16,4224]{1,0:T(8,128)(2,1)}, bf16[16,4224]{1,0:T(8,128)(2,1)S(1)}, u32[]{:S(2)}, u32[]{:S(2)}) collective-permute-start(bf16[16,4224]{1,0:T(8,128)(2,1)} %get-tuple-element.37.refs_0_), channel_id=1, source_target_pairs={{0,2},{2,0},{4,6},{6,4},{1,3},{3,1},{5,7},{7,5},{8,10},{10,8},{12,... | collective-permute-start | bytes 405512 | tf_op jit(solution)/shard_map/ppermute | solution.py:25
  9.5 0.0 collective-permute-done.2.refs_4_
  9.5 5.0 %collective-permute-done.1.refs_2_ = bf16[16,4224]{1,0:T(8,128)(2,1)S(1)} collective-permute-done((bf16[16,4224]{1,0:T(8,128)(2,1)}, bf16[16,4224]{1,0:T(8,128)(2,1)S(1)}, u32[]{:S(2)}, u32[]{:S(2)}) %collective-permute-start.1) | collective-permute-done | bytes 135200 | tf_op jit(solution)/shard_map/ppermute | solution.py:25
  14.5 0.7 collective-permute-start.3
  15.1 0.0 collective-permute-done.refs_1_
  15.1 0.5 collective-permute-start.4
  15.7 0.6 collective-permute-start.9
  16.2 1.0 %collective-permute-start.8 = (bf16[128,512]{1,0:T(8,128)(2,1)}, bf16[128,512]{1,0:T(8,128)(2,1)S(1)}, u32[]{:S(2)}, u32[]{:S(2)}) collective-permute-start(bf16[128,512]{1,0:T(8,128)(2,1)} %get-tuple-element.35.refs_0_), channel_id=1, source_target_pairs={{0,16},{8,24},{16,0},{24,8},{1,17},{9,25},{17,1},{25,9},{2,18},{10... | collective-permute-start | bytes 393224 | tf_op jit(solution)/shard_map/ppermute | solution.py:25
  17.2 0.3 collective-permute-start.7
  17.5 2.0 %collective-permute-done.3.refs_3_ = bf16[16,4224]{1,0:T(8,128)(2,1)S(1)} collective-permute-done((bf16[16,4224]{1,0:T(8,128)(2,1)S(1)}, bf16[16,4224]{1,0:T(8,128)(2,1)S(1)}, u32[]{:S(2)}, u32[]{:S(2)}) %collective-permute-start.3) | collective-permute-done | bytes 135200 | tf_op jit(solution)/shard_map/ppermute | solution.py:25
  19.5 0.5 collective-permute-start.5
  20.0 0.4 collective-permute-done.4.refs_5_
  20.4 1.1 %collective-permute-start.6 = (bf16[16,4224]{1,0:T(8,128)(2,1)S(1)}, bf16[16,4224]{1,0:T(8,128)(2,1)S(1)}, u32[]{:S(2)}, u32[]{:S(2)}) collective-permute-start(bf16[16,4224]{1,0:T(8,128)(2,1)S(1)} %collective-permute-done.3.refs_3_), channel_id=1, source_target_pairs={{0,1},{1,0},{2,3},{3,2},{4,5},{5,4},{6,7},{7,6},{8,9},{9,8},{10,11... | collective-permute-start | bytes 405512 | tf_op jit(solution)/shard_map/ppermute | solution.py:25
  21.5 0.6 pad_add_fusion.base_ref
  22.1 0.0 collective-permute-done.9.refs_3_
  22.2 0.0 copy-start.1
  22.2 2.3 %collective-permute-done.8.refs_2_ = bf16[128,512]{1,0:T(8,128)(2,1)S(1)} collective-permute-done((bf16[128,512]{1,0:T(8,128)(2,1)}, bf16[128,512]{1,0:T(8,128)(2,1)S(1)}, u32[]{:S(2)}, u32[]{:S(2)}) %collective-permute-start.8) | collective-permute-done | bytes 131104 | tf_op jit(solution)/shard_map/ppermute | solution.py:25
  24.5 0.0 copy-start.2
  24.5 0.0 collective-permute-done.7.refs_1_
  24.5 0.0 copy-start.3
  24.5 0.0 copy-done.1
  24.5 0.7 copy-done.2
  25.1 0.1 copy-done.3
  25.2 3.6 %attention.1 = bf16[128,2048]{1,0:T(8,128)(2,1)} custom-call(s32[4]{0:T(128)} %pad_add_fusion.base_ref, bf16[128,2048]{1,0:T(8,128)(2,1)} %bitcast.27, bf16[128,512]{1,0:T(8,128)(2,1)} %get-tuple-element.35.refs_0_, bf16[128,512]{1,0:T(8,128)(2,1)} %copy-done.3, bf16[128,512]{1,0:T(8,128)(2,1)} %copy-done.2, bf16[128,512]{1,0:T(8,128)(2,1)} %copy-done.1), custom_call_target="tpu_custom_call" | custom-call | flops 536870912 | bytes 1048576 | tf_op jit(solution)/shard_map/attention/pallas_call | solution.py:92
  28.7 0.0 collective-permute-done.5.refs_6_
  28.7 0.0 collective-permute-done.6.refs_7_
  28.7 0.0 copy-start
  28.8 0.9 %copy-done = bf16[16,4224]{1,0:T(8,128)(2,1)S(1)} copy-done((bf16[16,4224]{1,0:T(8,128)(2,1)S(1)}, bf16[16,4224]{1,0:T(8,128)(2,1)}, u32[]{:S(2)}) %copy-start) | copy-done | bytes 135192
  29.7 23.0 %experts.1 = (bf16[16,4096]{1,0:T(8,128)(2,1)S(1)}, bf16[16,4096]{1,0:T(8,128)(2,1)S(1)}, bf16[16,4096]{1,0:T(8,128)(2,1)S(1)}, bf16[16,4096]{1,0:T(8,128)(2,1)S...) custom-call(s32[1]{0:T(128)} %bitcast.14.shard_ref, ...), custom_call_target="tpu_custom_call" | custom-call | flops 2415919104 | bytes 37748736 | tf_op jit(solution)/shard_map/experts/pallas_call | solution.py:221
  52.7 1.6 %collective-permute-start.10 = (bf16[16,4096]{1,0:T(8,128)(2,1)S(1)}, bf16[16,4096]{1,0:T(8,128)(2,1)S(1)}, u32[]{:S(2)}, u32[]{:S(2)}) collective-permute-start(bf16[16,4096]{1,0:T(8,128)(2,1)S(1)} %get-tuple-element.48), channel_id=1, source_target_pairs={{0,1},{1,0},{2,3},{3,2},{4,5},{5,4},{6,7},{7,6},{8,9},{9,8},{10,11... | collective-permute-start | bytes 393224 | tf_op jit(solution)/shard_map/ppermute | solution.py:25
  54.3 0.5 collective-permute-start.12
  54.8 1.5 %collective-permute-start.14 = (bf16[16,4096]{1,0:T(8,128)(2,1)S(1)}, bf16[16,4096]{1,0:T(8,128)(2,1)S(1)}, u32[]{:S(2)}, u32[]{:S(2)}) collective-permute-start(bf16[16,4096]{1,0:T(8,128)(2,1)S(1)} %get-tuple-element.51), channel_id=1, source_target_pairs={{0,1},{1,0},{2,3},{3,2},{4,5},{5,4},{6,7},{7,6},{8,9},{9,8},{10,11... | collective-permute-start | bytes 393224 | tf_op jit(solution)/shard_map/ppermute | solution.py:25
  56.3 0.5 collective-permute-start.16
  56.8 2.3 %collective-permute-done.10 = bf16[16,4096]{1,0:T(8,128)(2,1)S(1)} collective-permute-done((bf16[16,4096]{1,0:T(8,128)(2,1)S(1)}, bf16[16,4096]{1,0:T(8,128)(2,1)S(1)}, u32[]{:S(2)}, u32[]{:S(2)}) %collective-permute-start.10) | collective-permute-done | bytes 131104 | tf_op jit(solution)/shard_map/ppermute | solution.py:25
  59.1 1.4 %collective-permute-start.11 = (bf16[16,4096]{1,0:T(8,128)(2,1)S(1)}, bf16[16,4096]{1,0:T(8,128)(2,1)S(1)}, u32[]{:S(2)}, u32[]{:S(2)}) collective-permute-start(bf16[16,4096]{1,0:T(8,128)(2,1)S(1)} %add_convert_fusion.3), channel_id=1, source_target_pairs={{0,2},{2,0},{4,6},{6,4},{1,3},{3,1},{5,7},{7,5},{8,10},{10,8},{12,... | collective-permute-start | bytes 393224 | tf_op jit(solution)/shard_map/ppermute | solution.py:25
  60.5 4.2 %collective-permute-done.14 = bf16[16,4096]{1,0:T(8,128)(2,1)S(1)} collective-permute-done((bf16[16,4096]{1,0:T(8,128)(2,1)S(1)}, bf16[16,4096]{1,0:T(8,128)(2,1)S(1)}, u32[]{:S(2)}, u32[]{:S(2)}) %collective-permute-start.14) | collective-permute-done | bytes 131104 | tf_op jit(solution)/shard_map/ppermute | solution.py:25
  64.8 1.4 %collective-permute-start.15 = (bf16[16,4096]{1,0:T(8,128)(2,1)S(1)}, bf16[16,4096]{1,0:T(8,128)(2,1)S(1)}, u32[]{:S(2)}, u32[]{:S(2)}) collective-permute-start(bf16[16,4096]{1,0:T(8,128)(2,1)S(1)} %add_convert_fusion.1), channel_id=1, source_target_pairs={{0,2},{2,0},{4,6},{6,4},{1,3},{3,1},{5,7},{7,5},{8,10},{10,8},{12,... | collective-permute-start | bytes 393224 | tf_op jit(solution)/shard_map/ppermute | solution.py:25
  66.2 0.0 collective-permute-done.12
  66.2 0.0 collective-permute-done.11
  66.2 0.1 add_convert_fusion.2
  66.2 2.0 %collective-permute-start.13 = (bf16[16,4096]{1,0:T(8,128)(2,1)S(1)}, bf16[16,4096]{1,0:T(8,128)(2,1)S(1)}, u32[]{:S(2)}, u32[]{:S(2)}) collective-permute-start(bf16[16,4096]{1,0:T(8,128)(2,1)S(1)} %add_convert_fusion.2), channel_id=1, source_target_pairs={{0,4},{2,6},{4,0},{6,2},{1,5},{3,7},{5,1},{7,3},{8,12},{10,14},{12... | collective-permute-start | bytes 393224 | tf_op jit(solution)/shard_map/ppermute | solution.py:25
  68.3 0.0 collective-permute-done.16
  68.3 2.3 %collective-permute-done.15 = bf16[16,4096]{1,0:T(8,128)(2,1)S(1)} collective-permute-done((bf16[16,4096]{1,0:T(8,128)(2,1)S(1)}, bf16[16,4096]{1,0:T(8,128)(2,1)S(1)}, u32[]{:S(2)}, u32[]{:S(2)}) %collective-permute-start.15) | collective-permute-done | bytes 131104 | tf_op jit(solution)/shard_map/ppermute | solution.py:25
  70.6 2.1 %collective-permute-done.13 = bf16[16,4096]{1,0:T(8,128)(2,1)S(1)} collective-permute-done((bf16[16,4096]{1,0:T(8,128)(2,1)S(1)}, bf16[16,4096]{1,0:T(8,128)(2,1)S(1)}, u32[]{:S(2)}, u32[]{:S(2)}) %collective-permute-start.13) | collective-permute-done | bytes 131104 | tf_op jit(solution)/shard_map/ppermute | solution.py:25
  72.7 0.1 add_convert_fusion
  72.8 0.7 slice_bitcast_fusion
  (2 shorter events, 0.1 us)
Async XLA Ops:
  2.3 7.1 %collective-permute-start.2 = (bf16[16,4224]{1,0:T(8,128)(2,1)}, bf16[16,4224]{1,0:T(8,128)(2,1)S(1)}, u32[]{:S(2)}, u32[]{:S(2)}) collective-permute-start(bf16[16,4224]{1,0:T(8,128)(2,1)} %get-tuple-element.37.refs_0_), channel_id=1, source_target_pairs={{0,1},{1,0},{2,3},{3,2},{4,5},{5,4},{6,7},{7,6},{8,9},{9,8},{10,11... | collective-permute-start | bytes 405512 | tf_op jit(solution)/shard_map/ppermute | solution.py:25
  5.3 9.2 %collective-permute-start.1 = (bf16[16,4224]{1,0:T(8,128)(2,1)}, bf16[16,4224]{1,0:T(8,128)(2,1)S(1)}, u32[]{:S(2)}, u32[]{:S(2)}) collective-permute-start(bf16[16,4224]{1,0:T(8,128)(2,1)} %get-tuple-element.37.refs_0_), channel_id=1, source_target_pairs={{0,4},{2,6},{4,0},{6,2},{1,5},{3,7},{5,1},{7,3},{8,12},{10,14},{12... | collective-permute-start | bytes 405512 | tf_op jit(solution)/shard_map/ppermute | solution.py:25
  7.9 7.2 %collective-permute-start = (bf16[16,4224]{1,0:T(8,128)(2,1)}, bf16[16,4224]{1,0:T(8,128)(2,1)S(1)}, u32[]{:S(2)}, u32[]{:S(2)}) collective-permute-start(bf16[16,4224]{1,0:T(8,128)(2,1)} %get-tuple-element.37.refs_0_), channel_id=1, source_target_pairs={{0,2},{2,0},{4,6},{6,4},{1,3},{3,1},{5,7},{7,5},{8,10},{10,8},{12,... | collective-permute-start | bytes 405512 | tf_op jit(solution)/shard_map/ppermute | solution.py:25
  14.5 5.0 %collective-permute-start.3 = (bf16[16,4224]{1,0:T(8,128)(2,1)S(1)}, bf16[16,4224]{1,0:T(8,128)(2,1)S(1)}, u32[]{:S(2)}, u32[]{:S(2)}) collective-permute-start(bf16[16,4224]{1,0:T(8,128)(2,1)S(1)} %collective-permute-done.1.refs_2_), channel_id=1, source_target_pairs={{0,2},{2,0},{4,6},{6,4},{1,3},{3,1},{5,7},{7,5},{8,10},{10,8},{12,... | collective-permute-start | bytes 405512 | tf_op jit(solution)/shard_map/ppermute | solution.py:25
  15.1 5.2 %collective-permute-start.4 = (bf16[16,4224]{1,0:T(8,128)(2,1)S(1)}, bf16[16,4224]{1,0:T(8,128)(2,1)S(1)}, u32[]{:S(2)}, u32[]{:S(2)}) collective-permute-start(bf16[16,4224]{1,0:T(8,128)(2,1)S(1)} %collective-permute-done.refs_1_), channel_id=1, source_target_pairs={{0,1},{1,0},{2,3},{3,2},{4,5},{5,4},{6,7},{7,6},{8,9},{9,8},{10,11... | collective-permute-start | bytes 405512 | tf_op jit(solution)/shard_map/ppermute | solution.py:25
  15.7 6.5 %collective-permute-start.9 = (bf16[128,512]{1,0:T(8,128)(2,1)}, bf16[128,512]{1,0:T(8,128)(2,1)S(1)}, u32[]{:S(2)}, u32[]{:S(2)}) collective-permute-start(bf16[128,512]{1,0:T(8,128)(2,1)} %get-tuple-element.35.refs_0_), channel_id=1, source_target_pairs={{0,24},{8,16},{16,8},{24,0},{1,25},{9,17},{17,9},{25,1},{2,26},{10... | collective-permute-start | bytes 393224 | tf_op jit(solution)/shard_map/ppermute | solution.py:25
  16.2 8.3 %collective-permute-start.8 = (bf16[128,512]{1,0:T(8,128)(2,1)}, bf16[128,512]{1,0:T(8,128)(2,1)S(1)}, u32[]{:S(2)}, u32[]{:S(2)}) collective-permute-start(bf16[128,512]{1,0:T(8,128)(2,1)} %get-tuple-element.35.refs_0_), channel_id=1, source_target_pairs={{0,16},{8,24},{16,0},{24,8},{1,17},{9,25},{17,1},{25,9},{2,18},{10... | collective-permute-start | bytes 393224 | tf_op jit(solution)/shard_map/ppermute | solution.py:25
  17.2 7.3 %collective-permute-start.7 = (bf16[128,512]{1,0:T(8,128)(2,1)}, bf16[128,512]{1,0:T(8,128)(2,1)S(1)}, u32[]{:S(2)}, u32[]{:S(2)}) collective-permute-start(bf16[128,512]{1,0:T(8,128)(2,1)} %get-tuple-element.35.refs_0_), channel_id=1, source_target_pairs={{0,8},{8,0},{16,24},{24,16},{1,9},{9,1},{17,25},{25,17},{2,10},{10... | collective-permute-start | bytes 393224 | tf_op jit(solution)/shard_map/ppermute | solution.py:25
  19.5 9.2 %collective-permute-start.5 = (bf16[16,4224]{1,0:T(8,128)(2,1)S(1)}, bf16[16,4224]{1,0:T(8,128)(2,1)S(1)}, u32[]{:S(2)}, u32[]{:S(2)}) collective-permute-start(bf16[16,4224]{1,0:T(8,128)(2,1)S(1)} %collective-permute-done.1.refs_2_), channel_id=1, source_target_pairs={{0,1},{1,0},{2,3},{3,2},{4,5},{5,4},{6,7},{7,6},{8,9},{9,8},{10,11... | collective-permute-start | bytes 405512 | tf_op jit(solution)/shard_map/ppermute | solution.py:25
  20.4 8.4 %collective-permute-start.6 = (bf16[16,4224]{1,0:T(8,128)(2,1)S(1)}, bf16[16,4224]{1,0:T(8,128)(2,1)S(1)}, u32[]{:S(2)}, u32[]{:S(2)}) collective-permute-start(bf16[16,4224]{1,0:T(8,128)(2,1)S(1)} %collective-permute-done.3.refs_3_), channel_id=1, source_target_pairs={{0,1},{1,0},{2,3},{3,2},{4,5},{5,4},{6,7},{7,6},{8,9},{9,8},{10,11... | collective-permute-start | bytes 405512 | tf_op jit(solution)/shard_map/ppermute | solution.py:25
  22.2 2.3 %copy-start.1 = (bf16[128,512]{1,0:T(8,128)(2,1)}, bf16[128,512]{1,0:T(8,128)(2,1)S(1)}, u32[]{:S(2)}) copy-start(bf16[128,512]{1,0:T(8,128)(2,1)S(1)} %collective-permute-done.9.refs_3_) | copy-start | bytes 393220
  24.5 0.7 copy-start.2
  24.5 0.7 copy-start.3
  28.7 0.9 %copy-start = (bf16[16,4224]{1,0:T(8,128)(2,1)S(1)}, bf16[16,4224]{1,0:T(8,128)(2,1)}, u32[]{:S(2)}) copy-start(bf16[16,4224]{1,0:T(8,128)(2,1)} %get-tuple-element.37.refs_0_) | copy-start | bytes 405508
  52.7 6.4 %collective-permute-start.10 = (bf16[16,4096]{1,0:T(8,128)(2,1)S(1)}, bf16[16,4096]{1,0:T(8,128)(2,1)S(1)}, u32[]{:S(2)}, u32[]{:S(2)}) collective-permute-start(bf16[16,4096]{1,0:T(8,128)(2,1)S(1)} %get-tuple-element.48), channel_id=1, source_target_pairs={{0,1},{1,0},{2,3},{3,2},{4,5},{5,4},{6,7},{7,6},{8,9},{9,8},{10,11... | collective-permute-start | bytes 393224 | tf_op jit(solution)/shard_map/ppermute | solution.py:25
  54.3 11.9 %collective-permute-start.12 = (bf16[16,4096]{1,0:T(8,128)(2,1)S(1)}, bf16[16,4096]{1,0:T(8,128)(2,1)S(1)}, u32[]{:S(2)}, u32[]{:S(2)}) collective-permute-start(bf16[16,4096]{1,0:T(8,128)(2,1)S(1)} %get-tuple-element.49), channel_id=1, source_target_pairs={{0,1},{1,0},{2,3},{3,2},{4,5},{5,4},{6,7},{7,6},{8,9},{9,8},{10,11... | collective-permute-start | bytes 393224 | tf_op jit(solution)/shard_map/ppermute | solution.py:25
  54.8 9.9 %collective-permute-start.14 = (bf16[16,4096]{1,0:T(8,128)(2,1)S(1)}, bf16[16,4096]{1,0:T(8,128)(2,1)S(1)}, u32[]{:S(2)}, u32[]{:S(2)}) collective-permute-start(bf16[16,4096]{1,0:T(8,128)(2,1)S(1)} %get-tuple-element.51), channel_id=1, source_target_pairs={{0,1},{1,0},{2,3},{3,2},{4,5},{5,4},{6,7},{7,6},{8,9},{9,8},{10,11... | collective-permute-start | bytes 393224 | tf_op jit(solution)/shard_map/ppermute | solution.py:25
  56.3 12.0 %collective-permute-start.16 = (bf16[16,4096]{1,0:T(8,128)(2,1)S(1)}, bf16[16,4096]{1,0:T(8,128)(2,1)S(1)}, u32[]{:S(2)}, u32[]{:S(2)}) collective-permute-start(bf16[16,4096]{1,0:T(8,128)(2,1)S(1)} %get-tuple-element.52), channel_id=1, source_target_pairs={{0,1},{1,0},{2,3},{3,2},{4,5},{5,4},{6,7},{7,6},{8,9},{9,8},{10,11... | collective-permute-start | bytes 393224 | tf_op jit(solution)/shard_map/ppermute | solution.py:25
  59.1 7.0 %collective-permute-start.11 = (bf16[16,4096]{1,0:T(8,128)(2,1)S(1)}, bf16[16,4096]{1,0:T(8,128)(2,1)S(1)}, u32[]{:S(2)}, u32[]{:S(2)}) collective-permute-start(bf16[16,4096]{1,0:T(8,128)(2,1)S(1)} %add_convert_fusion.3), channel_id=1, source_target_pairs={{0,2},{2,0},{4,6},{6,4},{1,3},{3,1},{5,7},{7,5},{8,10},{10,8},{12,... | collective-permute-start | bytes 393224 | tf_op jit(solution)/shard_map/ppermute | solution.py:25
  64.8 5.8 %collective-permute-start.15 = (bf16[16,4096]{1,0:T(8,128)(2,1)S(1)}, bf16[16,4096]{1,0:T(8,128)(2,1)S(1)}, u32[]{:S(2)}, u32[]{:S(2)}) collective-permute-start(bf16[16,4096]{1,0:T(8,128)(2,1)S(1)} %add_convert_fusion.1), channel_id=1, source_target_pairs={{0,2},{2,0},{4,6},{6,4},{1,3},{3,1},{5,7},{7,5},{8,10},{10,8},{12,... | collective-permute-start | bytes 393224 | tf_op jit(solution)/shard_map/ppermute | solution.py:25
  66.2 6.5 %collective-permute-start.13 = (bf16[16,4096]{1,0:T(8,128)(2,1)S(1)}, bf16[16,4096]{1,0:T(8,128)(2,1)S(1)}, u32[]{:S(2)}, u32[]{:S(2)}) collective-permute-start(bf16[16,4096]{1,0:T(8,128)(2,1)S(1)} %add_convert_fusion.2), channel_id=1, source_target_pairs={{0,4},{2,6},{4,0},{6,2},{1,5},{3,7},{5,1},{7,3},{8,12},{10,14},{12... | collective-permute-start | bytes 393224 | tf_op jit(solution)/shard_map/ppermute | solution.py:25

commit v4 on v3

--- a/solution.py
+++ b/solution.py
@@ -238,48 +238,59 @@
     return offset & (offset - 1)
 
 
-def spread(rows, held):
+def spread(rows, kv):
     near, far = [rows], []
+    kv_pieces, offsets = [kv], [0]
+    step = lax.axis_size("group") // 2
     for d in range(1, lax.axis_size("seq")):
         block = swap(near[parent(d)], "seq", d - parent(d))
         far.append([swap(near[d - 1], "tp", t) for t in range(1, lax.axis_size("tp"))])
         if d > 1:
-            block, far[d - 2] = lax.optimization_barrier((block, far[d - 2]))
+            if step:
+                kv_pieces = kv_pieces + [swap(a, "group", step) for a in kv_pieces]
+                offsets = offsets + [o ^ step for o in offsets]
+                step //= 2
+            block, far[d - 2], kv_pieces = lax.optimization_barrier((block, far[d - 2], kv_pieces))
         near.append(block)
+    while step:
+        kv_pieces = kv_pieces + [swap(a, "group", step) for a in kv_pieces]
+        offsets = offsets + [o ^ step for o in offsets]
+        step //= 2
     far.append([swap(near[-1], "tp", t) for t in range(1, lax.axis_size("tp"))])
-    near[-1], result = held(near[-1])
-    return near + [a for blocks in zip(*far) for a in blocks], result
-
-
-def collect(pieces):
+    return near + [a for blocks in zip(*far) for a in blocks], kv_pieces, offsets
+
+
+def collect(pieces, beside):
     seq, tp = lax.axis_size("seq"), lax.axis_size("tp")
     terms = [[pieces[d]] for d in range(seq)]
-    for d in reversed(range(seq)):
+    order = sorted(range(seq), key=lambda d: (-d.bit_count(), d))
+    last = None
+    for d in order:
         terms[d] += [swap(pieces[t * seq + d], "tp", t) for t in range(1, tp)]
-        total = sum(a.astype(F32) for a in terms[d]).astype(BF16)
-        if d:
-            terms[d] = []
-            terms[parent(d)].append(swap(total, "seq", d - parent(d)))
-        if d and d % 8 == 0:
-            pieces, terms = lax.optimization_barrier((pieces, terms))
-    return total
+        if d == 0:
+            break
+        if last is not None:
+            _, terms[d] = lax.optimization_barrier((last, terms[d]))
+        last = sum(a.astype(F32) for a in terms[d]).astype(BF16)
+        terms[parent(d)].append(swap(last, "seq", d - parent(d)))
+    result = beside(last)
+    terms[0], result = lax.optimization_barrier((terms[0], result))
+    return sum(a.astype(F32) for a in terms[0]).astype(BF16), result
 
 
 def shards(queries, keys, values, moe_x, expert_ids, gates, grad_out, w_gate, w_up, w_down):
     group = lax.axis_index("group")
     shard = (lax.axis_index("seq") * lax.axis_size("tp") + lax.axis_index("tp")).reshape(1)
     rows, kv = pack(expert_ids[0].T, gates[0].T, moe_x[0], grad_out[0], keys[0], values[0])
-    offsets = range(lax.axis_size("group"))
-    kv_pieces = [kv] + [swap(kv, "group", d) for d in offsets[1:]]
+    pieces, kv_pieces, offsets = spread(rows, kv)
     base = jnp.stack([group ^ d for d in offsets])
 
-    def attended(block):
-        block, starts = lax.optimization_barrier((block, base))
-        return block, attend(starts, queries[0], kv_pieces)
-
-    pieces, attn_out = spread(rows, attended)
-    pieces, attn_out = lax.optimization_barrier((pieces, attn_out))
-    total = collect(experts(shard, pieces, w_gate, w_up, w_down))
+    def attended(sums):
+        _, first = lax.optimization_barrier((sums, kv_pieces[0]))
+        return attend(base, queries[0], [first] + kv_pieces[1:])
+
+    partial = experts(shard, pieces, w_gate, w_up, w_down)
+    total, attn_out = collect(partial, attended)
     width = moe_x.shape[-1]
     return attn_out[None], total[None, :, :width], total[None, :, width:]
 

time: 73.6 us -> 70.7 us (0.961)
  waiting for transfers between devices: 20.7 us -> 17.4 us
  starting transfers between devices: 20.7 us -> 21.7 us
    ppermute x17, waiting for transfers between devices: 20.7 us -> 17.4 us  [swap(): return lax.ppermute(array, axis, [(i, i ^ offset) for i in range(count)])]
    ppermute x17, starting transfers between devices: 20.7 us -> 21.7 us  [swap(): return lax.ppermute(array, axis, [(i, i ^ offset) for i in range(count)])]
where the time goes in v4:
time: 70.7 us; the launch traced here: 70.5 us
  Pallas kernels  28.3 us (40%)
  starting transfers between devices  21.7 us (31%)
  waiting for transfers between devices  17.4 us (25%)
  local copies, waits for them, and re-layouts  1.58 us (2%)
  other arithmetic  0.82 us (1%)
  between operations  0.73 us (1%)
    pallas_call x1, Pallas kernels, experts(): pl.pallas_call(functools.partial(experts_kernel, count=count, slots=slots...  23 us
    ppermute x17, starting transfers between devices, swap(): return lax.ppermute(array, axis, [(i, i ^ offset) for i in range(count)])  21.7 us
    ppermute x17, waiting for transfers between devices, swap(): return lax.ppermute(array, axis, [(i, i ^ offset) for i in range(count)])  17.4 us
    pallas_call x1, Pallas kernels, attend(): pl.pallas_call(attention_kernel, in_specs=[SMEM] + [VMEM] * (1 + len(kv))...  3.55 us
    pallas_call x1, Pallas kernels, pack(): pl.pallas_call(pack_kernel, in_specs=[VMEM] * 6, out_specs=[VMEM] * 2, ou...  1.72 us
  transfers between devices with their start and end apart: 17, of which 8 were waited for; matrix products, arithmetic and copies ran while one was open for 1% of the time, Pallas kernels for 5%

profile of v4, /device:TPU:0, one launch (start us, length us, event | category | flops | bytes accessed | tf_op | source)
XLA Modules:
  0.0 70.5 jit_solution(4577862315088167682)
XLA Ops:
  0.6 1.7 %pack.1 = (bf16[16,4224]{1,0:T(8,128)(2,1)}, bf16[128,512]{1,0:T(8,128)(2,1)}) custom-call(s32[8,16]{1,0:T(8,128)} %bitcast.25, f32[8,16]{1,0:T(8,128)} %bitcast.26, bf16[16,2048]{1,0:T(8,128)(2,1)} %bitcast.21, bf16[16,2048]{1,0:T(8,128)(2,1)} %bitcast.22, bf16[128,256]{1,0:T(8,128)(2,1)} %bitcast.23, bf16[128,256]{1,0:T(8,128)(2,1)} %bitcast.24), custom_call_target="tpu_custom_call" | custom-call | tf_op jit(solution)/shard_map/pack/pallas_call | solution.py:47
  2.4 3.0 %collective-permute-start.2 = (bf16[16,4224]{1,0:T(8,128)(2,1)}, bf16[16,4224]{1,0:T(8,128)(2,1)S(1)}, u32[]{:S(2)}, u32[]{:S(2)}) collective-permute-start(bf16[16,4224]{1,0:T(8,128)(2,1)} %get-tuple-element.34.refs_0_), channel_id=1, source_target_pairs={{0,1},{1,0},{2,3},{3,2},{4,5},{5,4},{6,7},{7,6},{8,9},{9,8},{10,11... | collective-permute-start | bytes 405512 | tf_op jit(solution)/shard_map/ppermute | solution.py:25
  5.3 2.6 %collective-permute-start.1 = (bf16[16,4224]{1,0:T(8,128)(2,1)}, bf16[16,4224]{1,0:T(8,128)(2,1)S(1)}, u32[]{:S(2)}, u32[]{:S(2)}) collective-permute-start(bf16[16,4224]{1,0:T(8,128)(2,1)} %get-tuple-element.34.refs_0_), channel_id=1, source_target_pairs={{0,4},{2,6},{4,0},{6,2},{1,5},{3,7},{5,1},{7,3},{8,12},{10,14},{12... | collective-permute-start | bytes 405512 | tf_op jit(solution)/shard_map/ppermute | solution.py:25
  7.9 1.6 %collective-permute-start = (bf16[16,4224]{1,0:T(8,128)(2,1)}, bf16[16,4224]{1,0:T(8,128)(2,1)S(1)}, u32[]{:S(2)}, u32[]{:S(2)}) collective-permute-start(bf16[16,4224]{1,0:T(8,128)(2,1)} %get-tuple-element.34.refs_0_), channel_id=1, source_target_pairs={{0,2},{2,0},{4,6},{6,4},{1,3},{3,1},{5,7},{7,5},{8,10},{10,8},{12,... | collective-permute-start | bytes 405512 | tf_op jit(solution)/shard_map/ppermute | solution.py:25
  9.5 1.5 %collective-permute-start.3 = (bf16[128,512]{1,0:T(8,128)(2,1)}, bf16[128,512]{1,0:T(8,128)(2,1)S(1)}, u32[]{:S(2)}, u32[]{:S(2)}) collective-permute-start(bf16[128,512]{1,0:T(8,128)(2,1)} %get-tuple-element.56.refs_0_), channel_id=1, source_target_pairs={{0,16},{8,24},{16,0},{24,8},{1,17},{9,25},{17,1},{25,9},{2,18},{10... | collective-permute-start | bytes 393224 | tf_op jit(solution)/shard_map/ppermute | solution.py:25
  11.0 3.7 %collective-permute-done.3.refs_1_ = bf16[128,512]{1,0:T(8,128)(2,1)S(1)} collective-permute-done((bf16[128,512]{1,0:T(8,128)(2,1)}, bf16[128,512]{1,0:T(8,128)(2,1)S(1)}, u32[]{:S(2)}, u32[]{:S(2)}) %collective-permute-start.3) | collective-permute-done | bytes 131104 | tf_op jit(solution)/shard_map/ppermute | solution.py:25
  14.7 0.0 copy-start.1
  14.7 0.0 collective-permute-done.2.refs_4_
  14.7 0.0 collective-permute-done.1.refs_2_
  14.7 0.5 collective-permute-start.4
  15.2 0.0 collective-permute-done.refs_1_
  15.2 0.5 collective-permute-start.5
  15.7 0.0 collective-permute-start.6
  15.7 0.5 collective-permute-start.7
  16.2 1.5 %collective-permute-start.8 = (bf16[16,4224]{1,0:T(8,128)(2,1)S(1)}, bf16[16,4224]{1,0:T(8,128)(2,1)S(1)}, u32[]{:S(2)}, u32[]{:S(2)}) collective-permute-start(bf16[16,4224]{1,0:T(8,128)(2,1)S(1)} %collective-permute-done.1.refs_2_), channel_id=1, source_target_pairs={{0,1},{1,0},{2,3},{3,2},{4,5},{5,4},{6,7},{7,6},{8,9},{9,8},{10,11... | collective-permute-start | bytes 405512 | tf_op jit(solution)/shard_map/ppermute | solution.py:25
  17.7 0.0 collective-permute-done.6.refs_2_
  17.7 0.0 copy-start.2
  17.7 0.0 collective-permute-done.7.refs_3_
  17.7 0.0 copy-start.3
  17.8 2.0 %collective-permute-done.4.refs_3_ = bf16[16,4224]{1,0:T(8,128)(2,1)S(1)} collective-permute-done((bf16[16,4224]{1,0:T(8,128)(2,1)S(1)}, bf16[16,4224]{1,0:T(8,128)(2,1)S(1)}, u32[]{:S(2)}, u32[]{:S(2)}) %collective-permute-start.4) | collective-permute-done | bytes 135200 | tf_op jit(solution)/shard_map/ppermute | solution.py:25
  19.8 1.9 %collective-permute-done.5.refs_5_ = bf16[16,4224]{1,0:T(8,128)(2,1)S(1)} collective-permute-done((bf16[16,4224]{1,0:T(8,128)(2,1)S(1)}, bf16[16,4224]{1,0:T(8,128)(2,1)S(1)}, u32[]{:S(2)}, u32[]{:S(2)}) %collective-permute-start.5) | collective-permute-done | bytes 135200 | tf_op jit(solution)/shard_map/ppermute | solution.py:25
  21.7 0.0 collective-permute-start.9
  21.7 2.9 %collective-permute-done.8.refs_6_ = bf16[16,4224]{1,0:T(8,128)(2,1)S(1)} collective-permute-done((bf16[16,4224]{1,0:T(8,128)(2,1)S(1)}, bf16[16,4224]{1,0:T(8,128)(2,1)S(1)}, u32[]{:S(2)}, u32[]{:S(2)}) %collective-permute-start.8) | collective-permute-done | bytes 135200 | tf_op jit(solution)/shard_map/ppermute | solution.py:25
  24.6 2.1 %collective-permute-done.9.refs_7_ = bf16[16,4224]{1,0:T(8,128)(2,1)S(1)} collective-permute-done((bf16[16,4224]{1,0:T(8,128)(2,1)S(1)}, bf16[16,4224]{1,0:T(8,128)(2,1)S(1)}, u32[]{:S(2)}, u32[]{:S(2)}) %collective-permute-start.9) | collective-permute-done | bytes 135200 | tf_op jit(solution)/shard_map/ppermute | solution.py:25
  26.7 0.0 copy-start
  26.7 0.9 %copy-done = bf16[16,4224]{1,0:T(8,128)(2,1)S(1)} copy-done((bf16[16,4224]{1,0:T(8,128)(2,1)S(1)}, bf16[16,4224]{1,0:T(8,128)(2,1)}, u32[]{:S(2)}) %copy-start) | copy-done | bytes 135192
  27.6 23.0 %experts.1 = (bf16[16,4096]{1,0:T(8,128)(2,1)S(1)}, bf16[16,4096]{1,0:T(8,128)(2,1)S(1)}, bf16[16,4096]{1,0:T(8,128)(2,1)S(1)}, bf16[16,4096]{1,0:T(8,128)(2,1)S...) custom-call(s32[1]{0:T(128)} %bitcast.shard_ref, ...), custom_call_target="tpu_custom_call" | custom-call | flops 2415919104 | bytes 37748736 | tf_op jit(solution)/shard_map/experts/pallas_call | solution.py:221
  50.6 0.0 copy-done.1
  50.6 0.0 copy-done.2
  50.7 0.0 copy-done.3
  50.7 0.1 collective-permute-start.10
  50.8 2.0 %collective-permute-start.11 = (bf16[16,4096]{1,0:T(8,128)(2,1)S(1)}, bf16[16,4096]{1,0:T(8,128)(2,1)S(1)}, u32[]{:S(2)}, u32[]{:S(2)}) collective-permute-start(bf16[16,4096]{1,0:T(8,128)(2,1)S(1)} %get-tuple-element.46), channel_id=1, source_target_pairs={{0,1},{1,0},{2,3},{3,2},{4,5},{5,4},{6,7},{7,6},{8,9},{9,8},{10,11... | collective-permute-start | bytes 393224 | tf_op jit(solution)/shard_map/ppermute | solution.py:25
  52.8 0.1 collective-permute-start.14
  52.8 1.9 %collective-permute-start.16 = (bf16[16,4096]{1,0:T(8,128)(2,1)S(1)}, bf16[16,4096]{1,0:T(8,128)(2,1)S(1)}, u32[]{:S(2)}, u32[]{:S(2)}) collective-permute-start(bf16[16,4096]{1,0:T(8,128)(2,1)S(1)} %get-tuple-element.54), channel_id=1, source_target_pairs={{0,1},{1,0},{2,3},{3,2},{4,5},{5,4},{6,7},{7,6},{8,9},{9,8},{10,11... | collective-permute-start | bytes 393224 | tf_op jit(solution)/shard_map/ppermute | solution.py:25
  54.8 2.4 %collective-permute-done.10 = bf16[16,4096]{1,0:T(8,128)(2,1)S(1)} collective-permute-done((bf16[16,4096]{1,0:T(8,128)(2,1)S(1)}, bf16[16,4096]{1,0:T(8,128)(2,1)S(1)}, u32[]{:S(2)}, u32[]{:S(2)}) %collective-permute-start.10) | collective-permute-done | bytes 131104 | tf_op jit(solution)/shard_map/ppermute | solution.py:25
  57.2 1.6 %collective-permute-start.13 = (bf16[16,4096]{1,0:T(8,128)(2,1)S(1)}, bf16[16,4096]{1,0:T(8,128)(2,1)S(1)}, u32[]{:S(2)}, u32[]{:S(2)}) collective-permute-start(bf16[16,4096]{1,0:T(8,128)(2,1)S(1)} %add_convert_fusion.3), channel_id=1, source_target_pairs={{0,2},{2,0},{4,6},{6,4},{1,3},{3,1},{5,7},{7,5},{8,10},{10,8},{12,... | collective-permute-start | bytes 393224 | tf_op jit(solution)/shard_map/ppermute | solution.py:25
  58.8 1.0 %collective-permute-done.11 = bf16[16,4096]{1,0:T(8,128)(2,1)S(1)} collective-permute-done((bf16[16,4096]{1,0:T(8,128)(2,1)S(1)}, bf16[16,4096]{1,0:T(8,128)(2,1)S(1)}, u32[]{:S(2)}, u32[]{:S(2)}) %collective-permute-start.11) | collective-permute-done | bytes 131104 | tf_op jit(solution)/shard_map/ppermute | solution.py:25
  59.8 1.6 %collective-permute-start.12 = (bf16[16,4096]{1,0:T(8,128)(2,1)S(1)}, bf16[16,4096]{1,0:T(8,128)(2,1)S(1)}, u32[]{:S(2)}, u32[]{:S(2)}) collective-permute-start(bf16[16,4096]{1,0:T(8,128)(2,1)S(1)} %add_convert_fusion.2), channel_id=1, source_target_pairs={{0,2},{2,0},{4,6},{6,4},{1,3},{3,1},{5,7},{7,5},{8,10},{10,8},{12,... | collective-permute-start | bytes 393224 | tf_op jit(solution)/shard_map/ppermute | solution.py:25
  61.3 0.0 collective-permute-done.14
  61.4 1.3 %collective-permute-done.13 = bf16[16,4096]{1,0:T(8,128)(2,1)S(1)} collective-permute-done((bf16[16,4096]{1,0:T(8,128)(2,1)S(1)}, bf16[16,4096]{1,0:T(8,128)(2,1)S(1)}, u32[]{:S(2)}, u32[]{:S(2)}) %collective-permute-start.13) | collective-permute-done | bytes 131104 | tf_op jit(solution)/shard_map/ppermute | solution.py:25
  62.7 0.1 add_convert_fusion.1
  62.7 2.8 %collective-permute-start.15 = (bf16[16,4096]{1,0:T(8,128)(2,1)S(1)}, bf16[16,4096]{1,0:T(8,128)(2,1)S(1)}, u32[]{:S(2)}, u32[]{:S(2)}) collective-permute-start(bf16[16,4096]{1,0:T(8,128)(2,1)S(1)} %add_convert_fusion.1), channel_id=1, source_target_pairs={{0,4},{2,6},{4,0},{6,2},{1,5},{3,7},{5,1},{7,3},{8,12},{10,14},{12... | collective-permute-start | bytes 393224 | tf_op jit(solution)/shard_map/ppermute | solution.py:25
  65.6 0.6 pad_add_fusion.base_ref
  66.2 3.6 %attention.1 = bf16[128,2048]{1,0:T(8,128)(2,1)} custom-call(s32[4]{0:T(128)} %pad_add_fusion.base_ref, bf16[128,2048]{1,0:T(8,128)(2,1)} %bitcast.27, bf16[128,512]{1,0:T(8,128)(2,1)} %get-tuple-element.56.refs_0_, bf16[128,512]{1,0:T(8,128)(2,1)} %copy-done.1, bf16[128,512]{1,0:T(8,128)(2,1)} %copy-done.2, bf16[128,512]{1,0:T(8,128)(2,1)} %copy-done.3), custom_call_target="tpu_custom_call" | custom-call | flops 536870912 | bytes 1048576 | tf_op jit(solution)/shard_map/attention/pallas_call | solution.py:92
  69.8 0.0 collective-permute-done.16
  69.8 0.0 collective-permute-done.12
  69.8 0.0 collective-permute-done.15
  69.8 0.1 add_convert_fusion
  69.9 0.7 slice_bitcast_fusion
  (2 shorter events, 0.1 us)
Async XLA Ops:
  2.4 12.3 %collective-permute-start.2 = (bf16[16,4224]{1,0:T(8,128)(2,1)}, bf16[16,4224]{1,0:T(8,128)(2,1)S(1)}, u32[]{:S(2)}, u32[]{:S(2)}) collective-permute-start(bf16[16,4224]{1,0:T(8,128)(2,1)} %get-tuple-element.34.refs_0_), channel_id=1, source_target_pairs={{0,1},{1,0},{2,3},{3,2},{4,5},{5,4},{6,7},{7,6},{8,9},{9,8},{10,11... | collective-permute-start | bytes 405512 | tf_op jit(solution)/shard_map/ppermute | solution.py:25
  5.3 9.4 %collective-permute-start.1 = (bf16[16,4224]{1,0:T(8,128)(2,1)}, bf16[16,4224]{1,0:T(8,128)(2,1)S(1)}, u32[]{:S(2)}, u32[]{:S(2)}) collective-permute-start(bf16[16,4224]{1,0:T(8,128)(2,1)} %get-tuple-element.34.refs_0_), channel_id=1, source_target_pairs={{0,4},{2,6},{4,0},{6,2},{1,5},{3,7},{5,1},{7,3},{8,12},{10,14},{12... | collective-permute-start | bytes 405512 | tf_op jit(solution)/shard_map/ppermute | solution.py:25
  7.9 7.3 %collective-permute-start = (bf16[16,4224]{1,0:T(8,128)(2,1)}, bf16[16,4224]{1,0:T(8,128)(2,1)S(1)}, u32[]{:S(2)}, u32[]{:S(2)}) collective-permute-start(bf16[16,4224]{1,0:T(8,128)(2,1)} %get-tuple-element.34.refs_0_), channel_id=1, source_target_pairs={{0,2},{2,0},{4,6},{6,4},{1,3},{3,1},{5,7},{7,5},{8,10},{10,8},{12,... | collective-permute-start | bytes 405512 | tf_op jit(solution)/shard_map/ppermute | solution.py:25
  9.5 5.2 %collective-permute-start.3 = (bf16[128,512]{1,0:T(8,128)(2,1)}, bf16[128,512]{1,0:T(8,128)(2,1)S(1)}, u32[]{:S(2)}, u32[]{:S(2)}) collective-permute-start(bf16[128,512]{1,0:T(8,128)(2,1)} %get-tuple-element.56.refs_0_), channel_id=1, source_target_pairs={{0,16},{8,24},{16,0},{24,8},{1,17},{9,25},{17,1},{25,9},{2,18},{10... | collective-permute-start | bytes 393224 | tf_op jit(solution)/shard_map/ppermute | solution.py:25
  14.7 36.0 %copy-start.1 = (bf16[128,512]{1,0:T(8,128)(2,1)}, bf16[128,512]{1,0:T(8,128)(2,1)S(1)}, u32[]{:S(2)}) copy-start(bf16[128,512]{1,0:T(8,128)(2,1)S(1)} %collective-permute-done.3.refs_1_) | copy-start | bytes 393220
  14.7 5.1 %collective-permute-start.4 = (bf16[16,4224]{1,0:T(8,128)(2,1)S(1)}, bf16[16,4224]{1,0:T(8,128)(2,1)S(1)}, u32[]{:S(2)}, u32[]{:S(2)}) collective-permute-start(bf16[16,4224]{1,0:T(8,128)(2,1)S(1)} %collective-permute-done.1.refs_2_), channel_id=1, source_target_pairs={{0,2},{2,0},{4,6},{6,4},{1,3},{3,1},{5,7},{7,5},{8,10},{10,8},{12,... | collective-permute-start | bytes 405512 | tf_op jit(solution)/shard_map/ppermute | solution.py:25
  15.2 6.5 %collective-permute-start.5 = (bf16[16,4224]{1,0:T(8,128)(2,1)S(1)}, bf16[16,4224]{1,0:T(8,128)(2,1)S(1)}, u32[]{:S(2)}, u32[]{:S(2)}) collective-permute-start(bf16[16,4224]{1,0:T(8,128)(2,1)S(1)} %collective-permute-done.refs_1_), channel_id=1, source_target_pairs={{0,1},{1,0},{2,3},{3,2},{4,5},{5,4},{6,7},{7,6},{8,9},{9,8},{10,11... | collective-permute-start | bytes 405512 | tf_op jit(solution)/shard_map/ppermute | solution.py:25
  15.7 2.0 %collective-permute-start.6 = (bf16[128,512]{1,0:T(8,128)(2,1)}, bf16[128,512]{1,0:T(8,128)(2,1)S(1)}, u32[]{:S(2)}, u32[]{:S(2)}) collective-permute-start(bf16[128,512]{1,0:T(8,128)(2,1)} %get-tuple-element.56.refs_0_), channel_id=1, source_target_pairs={{0,8},{8,0},{16,24},{24,16},{1,9},{9,1},{17,25},{25,17},{2,10},{10... | collective-permute-start | bytes 393224 | tf_op jit(solution)/shard_map/ppermute | solution.py:25
  15.7 2.0 %collective-permute-start.7 = (bf16[128,512]{1,0:T(8,128)(2,1)S(1)}, bf16[128,512]{1,0:T(8,128)(2,1)S(1)}, u32[]{:S(2)}, u32[]{:S(2)}) collective-permute-start(bf16[128,512]{1,0:T(8,128)(2,1)S(1)} %collective-permute-done.3.refs_1_), channel_id=1, source_target_pairs={{0,8},{8,0},{16,24},{24,16},{1,9},{9,1},{17,25},{25,17},{2,10},{10... | collective-permute-start | bytes 393224 | tf_op jit(solution)/shard_map/ppermute | solution.py:25
  16.2 8.4 %collective-permute-start.8 = (bf16[16,4224]{1,0:T(8,128)(2,1)S(1)}, bf16[16,4224]{1,0:T(8,128)(2,1)S(1)}, u32[]{:S(2)}, u32[]{:S(2)}) collective-permute-start(bf16[16,4224]{1,0:T(8,128)(2,1)S(1)} %collective-permute-done.1.refs_2_), channel_id=1, source_target_pairs={{0,1},{1,0},{2,3},{3,2},{4,5},{5,4},{6,7},{7,6},{8,9},{9,8},{10,11... | collective-permute-start | bytes 405512 | tf_op jit(solution)/shard_map/ppermute | solution.py:25
  17.7 32.9 %copy-start.2 = (bf16[128,512]{1,0:T(8,128)(2,1)}, bf16[128,512]{1,0:T(8,128)(2,1)S(1)}, u32[]{:S(2)}) copy-start(bf16[128,512]{1,0:T(8,128)(2,1)S(1)} %collective-permute-done.6.refs_2_) | copy-start | bytes 393220
  17.7 32.9 %copy-start.3 = (bf16[128,512]{1,0:T(8,128)(2,1)}, bf16[128,512]{1,0:T(8,128)(2,1)S(1)}, u32[]{:S(2)}) copy-start(bf16[128,512]{1,0:T(8,128)(2,1)S(1)} %collective-permute-done.7.refs_3_) | copy-start | bytes 393220
  21.7 5.0 %collective-permute-start.9 = (bf16[16,4224]{1,0:T(8,128)(2,1)S(1)}, bf16[16,4224]{1,0:T(8,128)(2,1)S(1)}, u32[]{:S(2)}, u32[]{:S(2)}) collective-permute-start(bf16[16,4224]{1,0:T(8,128)(2,1)S(1)} %collective-permute-done.4.refs_3_), channel_id=1, source_target_pairs={{0,1},{1,0},{2,3},{3,2},{4,5},{5,4},{6,7},{7,6},{8,9},{9,8},{10,11... | collective-permute-start | bytes 405512 | tf_op jit(solution)/shard_map/ppermute | solution.py:25
  26.7 0.9 %copy-start = (bf16[16,4224]{1,0:T(8,128)(2,1)S(1)}, bf16[16,4224]{1,0:T(8,128)(2,1)}, u32[]{:S(2)}) copy-start(bf16[16,4224]{1,0:T(8,128)(2,1)} %get-tuple-element.34.refs_0_) | copy-start | bytes 405508
  50.7 6.5 %collective-permute-start.10 = (bf16[16,4096]{1,0:T(8,128)(2,1)S(1)}, bf16[16,4096]{1,0:T(8,128)(2,1)S(1)}, u32[]{:S(2)}, u32[]{:S(2)}) collective-permute-start(bf16[16,4096]{1,0:T(8,128)(2,1)S(1)} %get-tuple-element.44), channel_id=1, source_target_pairs={{0,1},{1,0},{2,3},{3,2},{4,5},{5,4},{6,7},{7,6},{8,9},{9,8},{10,11... | collective-permute-start | bytes 393224 | tf_op jit(solution)/shard_map/ppermute | solution.py:25
  50.8 9.0 %collective-permute-start.11 = (bf16[16,4096]{1,0:T(8,128)(2,1)S(1)}, bf16[16,4096]{1,0:T(8,128)(2,1)S(1)}, u32[]{:S(2)}, u32[]{:S(2)}) collective-permute-start(bf16[16,4096]{1,0:T(8,128)(2,1)S(1)} %get-tuple-element.46), channel_id=1, source_target_pairs={{0,1},{1,0},{2,3},{3,2},{4,5},{5,4},{6,7},{7,6},{8,9},{9,8},{10,11... | collective-permute-start | bytes 393224 | tf_op jit(solution)/shard_map/ppermute | solution.py:25
  52.8 8.6 %collective-permute-start.14 = (bf16[16,4096]{1,0:T(8,128)(2,1)S(1)}, bf16[16,4096]{1,0:T(8,128)(2,1)S(1)}, u32[]{:S(2)}, u32[]{:S(2)}) collective-permute-start(bf16[16,4096]{1,0:T(8,128)(2,1)S(1)} %get-tuple-element.50), channel_id=1, source_target_pairs={{0,1},{1,0},{2,3},{3,2},{4,5},{5,4},{6,7},{7,6},{8,9},{9,8},{10,11... | collective-permute-start | bytes 393224 | tf_op jit(solution)/shard_map/ppermute | solution.py:25
  52.8 16.9 %collective-permute-start.16 = (bf16[16,4096]{1,0:T(8,128)(2,1)S(1)}, bf16[16,4096]{1,0:T(8,128)(2,1)S(1)}, u32[]{:S(2)}, u32[]{:S(2)}) collective-permute-start(bf16[16,4096]{1,0:T(8,128)(2,1)S(1)} %get-tuple-element.54), channel_id=1, source_target_pairs={{0,1},{1,0},{2,3},{3,2},{4,5},{5,4},{6,7},{7,6},{8,9},{9,8},{10,11... | collective-permute-start | bytes 393224 | tf_op jit(solution)/shard_map/ppermute | solution.py:25
  57.2 5.5 %collective-permute-start.13 = (bf16[16,4096]{1,0:T(8,128)(2,1)S(1)}, bf16[16,4096]{1,0:T(8,128)(2,1)S(1)}, u32[]{:S(2)}, u32[]{:S(2)}) collective-permute-start(bf16[16,4096]{1,0:T(8,128)(2,1)S(1)} %add_convert_fusion.3), channel_id=1, source_target_pairs={{0,2},{2,0},{4,6},{6,4},{1,3},{3,1},{5,7},{7,5},{8,10},{10,8},{12,... | collective-permute-start | bytes 393224 | tf_op jit(solution)/shard_map/ppermute | solution.py:25
  59.8 10.0 %collective-permute-start.12 = (bf16[16,4096]{1,0:T(8,128)(2,1)S(1)}, bf16[16,4096]{1,0:T(8,128)(2,1)S(1)}, u32[]{:S(2)}, u32[]{:S(2)}) collective-permute-start(bf16[16,4096]{1,0:T(8,128)(2,1)S(1)} %add_convert_fusion.2), channel_id=1, source_target_pairs={{0,2},{2,0},{4,6},{6,4},{1,3},{3,1},{5,7},{7,5},{8,10},{10,8},{12,... | collective-permute-start | bytes 393224 | tf_op jit(solution)/shard_map/ppermute | solution.py:25
  62.7 7.0 %collective-permute-start.15 = (bf16[16,4096]{1,0:T(8,128)(2,1)S(1)}, bf16[16,4096]{1,0:T(8,128)(2,1)S(1)}, u32[]{:S(2)}, u32[]{:S(2)}) collective-permute-start(bf16[16,4096]{1,0:T(8,128)(2,1)S(1)} %add_convert_fusion.1), channel_id=1, source_target_pairs={{0,4},{2,6},{4,0},{6,2},{1,5},{3,7},{5,1},{7,3},{8,12},{10,14},{12... | collective-permute-start | bytes 393224 | tf_op jit(solution)/shard_map/ppermute | solution.py:25

commit v5 on v4

--- a/solution.py
+++ b/solution.py
@@ -16,6 +16,7 @@
 NT = (((1,), (1,)), ((), ()))
 VMEM = pl.BlockSpec(memory_space=pltpu.VMEM)
 SMEM = pl.BlockSpec(memory_space=pltpu.SMEM)
+ANY = pl.BlockSpec(memory_space=pl.ANY)
 F32 = jnp.float32
 BF16 = jnp.bfloat16
 
@@ -25,7 +26,7 @@
     return lax.ppermute(array, axis, [(i, i ^ offset) for i in range(count)])
 
 
-def pack_kernel(ids_ref, gates_ref, x_ref, grad_ref, key_ref, value_ref, out_ref, kv_ref):
+def pack_kernel(ids_ref, gates_ref, x_ref, grad_ref, out_ref, own_ref):
     rows, width = x_ref.shape
     topk = ids_ref.shape[0]
     expert = lax.broadcasted_iota(jnp.int32, (EXPERTS, rows), 0)
@@ -34,26 +35,25 @@
         table = table + jnp.where(ids_ref[k : k + 1] == expert, gates_ref[k : k + 1], 0.0)
     high = table.astype(BF16).astype(F32)
     both = jnp.concatenate([high, table - high], axis=0)
-    out_ref[:, :width] = x_ref[...]
-    out_ref[:, width : 2 * width] = grad_ref[...]
-    out_ref[:, 2 * width :] = jnp.transpose(both).astype(BF16)
-    half = key_ref.shape[1]
-    kv_ref[:, :half] = key_ref[...]
-    kv_ref[:, half:] = value_ref[...]
-
-
-def pack(ids, gates, x, grad, keys, values):
+    both = jnp.transpose(both).astype(BF16)
+    for ref in (out_ref, own_ref):
+        ref[:, :width] = x_ref[...]
+        ref[:, width : 2 * width] = grad_ref[...]
+        ref[:, 2 * width :] = both
+
+
+def pack_rows(ids, gates, x, grad):
     rows, width = x.shape
     return pl.pallas_call(
         pack_kernel,
-        in_specs=[VMEM] * 6,
+        in_specs=[VMEM] * 4,
         out_specs=[VMEM] * 2,
         out_shape=[
             jax.ShapeDtypeStruct((rows, 2 * (width + EXPERTS)), BF16),
-            jax.ShapeDtypeStruct((keys.shape[0], 2 * keys.shape[1]), BF16),
+            pltpu.VMEM((rows, 2 * (width + EXPERTS)), BF16),
         ],
-        name="pack",
-    )(ids, gates, x, grad, keys, values)
+        name="pack_rows",
+    )(ids, gates, x, grad)
 
 
 def attention_kernel(base_ref, q_ref, *refs):
@@ -124,7 +124,9 @@
     pieces = refs[:count]
     weights = refs[count : count + 3]
     outs = refs[count + 3 : 2 * count + 3]
-    held, sems, tokens_scr, rows_scr, back_scr, scale_scr, pick_scr = refs[2 * count + 3 :]
+    held, sems, tokens_scr, gates_scr, rows_scr, back_scr, scale_scr, pick_scr = refs[
+        2 * count + 3 :
+    ]
     gate_scr, up_scr, down_scr = held
     local, width, hidden = gate_scr.shape
     piece = pieces[0].shape[0]
@@ -141,8 +143,8 @@
 
     for p in range(count):
         tokens_scr[p * piece : (p + 1) * piece] = pieces[p][:, :both]
-    gates = jnp.concatenate([r[:, both:] for r in pieces], axis=0)
-    picks, scales = routing_rows(shard_ref[0], gates, local, slots)
+        gates_scr[p * piece : (p + 1) * piece] = pieces[p][:, both:]
+    picks, scales = routing_rows(shard_ref[0], gates_scr[...], local, slots)
     scale_scr[...] = jnp.broadcast_to(scales, scale_scr.shape)
     high = scales.astype(BF16).astype(F32)
     for i, part in enumerate((picks, picks * high, picks * (scales - high))):
@@ -158,37 +160,42 @@
 
     @pl.loop(0, local // unroll)
     def _(step):
-        state = []
+        first = step * unroll
         for k in range(unroll):
-            e = step * unroll + k
             for which in range(3):
-                copy(which, e).wait()
+                copy(which, first + k).wait()
+        every = pl.ds(pl.multiple_of(first * slots, slots), unroll * slots)
+        down = down_scr.at[pl.ds(first, unroll)].reshape(unroll * hidden, width)
+        row_grad = (rows_scr[every, width:].astype(F32) * scale_scr[every, :1]).astype(BF16)
+        hidden_both, mine = [], []
         for k in range(unroll):
-            e = step * unroll + k
-            mine = pl.ds(pl.multiple_of(e * slots, slots), slots)
-            entry = jnp.concatenate([gate_scr[e], up_scr[e]], axis=1)
-            hidden_both = jnp.dot(rows_scr[mine, :width], entry, preferred_element_type=F32)
-            row_grad = (rows_scr[mine, width:].astype(F32) * scale_scr[mine, :1]).astype(BF16)
-            grad_act = lax.dot_general(row_grad, down_scr[e], NT, preferred_element_type=F32)
-            state.append((hidden_both, grad_act))
+            mine.append(pl.ds(pl.multiple_of((first + k) * slots, slots), slots))
+            entry = jnp.concatenate([gate_scr[first + k], up_scr[first + k]], axis=1)
+            hidden_both.append(jnp.dot(rows_scr[mine[k], :width], entry, preferred_element_type=F32))
+        grad_act = lax.dot_general(row_grad, down[...], NT, preferred_element_type=F32)
+        activated = []
         for k in range(unroll):
-            e = step * unroll + k
-            mine = pl.ds(pl.multiple_of(e * slots, slots), slots)
-            hidden_both, grad_act = state[k]
-            hgate, hup = hidden_both[:, :hidden], hidden_both[:, hidden:]
+            part = grad_act[k * slots : (k + 1) * slots, k * hidden : (k + 1) * hidden]
+            hgate, hup = hidden_both[k][:, :hidden], hidden_both[k][:, hidden:]
             sig = jax.nn.sigmoid(hgate)
             silu = hgate * sig
-            activated = (silu * hup).astype(BF16)
-            grad_gate = (grad_act * hup * sig * (1.0 + hgate * (1.0 - sig))).astype(BF16)
-            grad_up = (grad_act * silu).astype(BF16)
-            back_scr[mine, :width] = jnp.dot(
-                activated, down_scr[e], preferred_element_type=F32
-            ).astype(BF16)
+            activated.append((silu * hup).astype(BF16))
+            grad_gate = (part * hup * sig * (1.0 + hgate * (1.0 - sig))).astype(BF16)
+            grad_up = (part * silu).astype(BF16)
             grads = jnp.concatenate([grad_gate, grad_up], axis=1)
-            entry = jnp.concatenate([gate_scr[e], up_scr[e]], axis=1)
-            back_scr[mine, width:] = lax.dot_general(
+            entry = jnp.concatenate([gate_scr[first + k], up_scr[first + k]], axis=1)
+            back_scr[mine[k], width:] = lax.dot_general(
                 grads, entry, NT, preferred_element_type=F32
             ).astype(BF16)
+        blocks = [
+            jnp.concatenate(
+                [a if k == i else jnp.zeros_like(a) for i in range(unroll)], axis=1
+            )
+            for k, a in enumerate(activated)
+        ]
+        back_scr[every, :width] = jnp.dot(
+            jnp.concatenate(blocks, axis=0), down[...], preferred_element_type=F32
+        ).astype(BF16)
 
     for c in range(0, both, chunk):
         rows = back_scr[:, c : c + chunk]
@@ -204,6 +211,7 @@
 
 def experts(shard, pieces, w_gate, w_up, w_down):
     count = len(pieces)
+    pieces = [pltpu.with_memory_space_constraint(pieces[0], pltpu.VMEM)] + pieces[1:]
     local, width, hidden = w_gate.shape
     piece = pieces[0].shape[0]
     tokens = count * piece
@@ -212,6 +220,7 @@
         tuple(pltpu.VMEM(w.shape, BF16) for w in (w_gate, w_up, w_down)),
         pltpu.SemaphoreType.DMA((3, local)),
         pltpu.VMEM((tokens, 2 * width), BF16),
+        pltpu.VMEM((tokens, pieces[0].shape[1] - 2 * width), BF16),
         pltpu.VMEM((local * slots, 2 * width), BF16),
         pltpu.VMEM((local * slots, 2 * width), BF16),
         pltpu.VMEM((local * slots, 128), F32),
@@ -220,7 +229,7 @@
     held_bytes = 6 * local * width * hidden + 4 * width * (tokens + 2 * local * slots)
     return pl.pallas_call(
         functools.partial(experts_kernel, count=count, slots=slots),
-        in_specs=[SMEM] + [VMEM] * count + [pl.BlockSpec(memory_space=pl.ANY)] * 3,
+        in_specs=[SMEM] + [VMEM] * count + [ANY] * 3,
         out_specs=[VMEM] * count,
         out_shape=[jax.ShapeDtypeStruct((piece, 2 * width), BF16)] * count,
         scratch_shapes=scratch,
@@ -238,42 +247,50 @@
     return offset & (offset - 1)
 
 
-def spread(rows, kv):
+def over_tp(block):
+    return [swap(block, "tp", t) for t in range(1, lax.axis_size("tp"))]
+
+
+def spread(rows):
     near, far = [rows], []
-    kv_pieces, offsets = [kv], [0]
-    step = lax.axis_size("group") // 2
     for d in range(1, lax.axis_size("seq")):
         block = swap(near[parent(d)], "seq", d - parent(d))
-        far.append([swap(near[d - 1], "tp", t) for t in range(1, lax.axis_size("tp"))])
-        if d > 1:
-            if step:
-                kv_pieces = kv_pieces + [swap(a, "group", step) for a in kv_pieces]
-                offsets = offsets + [o ^ step for o in offsets]
-                step //= 2
-            block, far[d - 2], kv_pieces = lax.optimization_barrier((block, far[d - 2], kv_pieces))
+        if d == 1:
+            block, rows = lax.optimization_barrier((block, rows))
+            far.append(over_tp(rows))
+        else:
+            far.append(over_tp(near[d - 1]))
+        if d > 2:
+            block, far[: d - 1] = lax.optimization_barrier((block, far[: d - 1]))
         near.append(block)
-    while step:
-        kv_pieces = kv_pieces + [swap(a, "group", step) for a in kv_pieces]
-        offsets = offsets + [o ^ step for o in offsets]
-        step //= 2
-    far.append([swap(near[-1], "tp", t) for t in range(1, lax.axis_size("tp"))])
-    return near + [a for blocks in zip(*far) for a in blocks], kv_pieces, offsets
-
-
-def collect(pieces, beside):
+    far.append(over_tp(near[-1]))
+    return near + [a for blocks in zip(*far) for a in blocks]
+
+
+def collect(pieces, kv, beside):
     seq, tp = lax.axis_size("seq"), lax.axis_size("tp")
     terms = [[pieces[d]] for d in range(seq)]
     order = sorted(range(seq), key=lambda d: (-d.bit_count(), d))
+    step = lax.axis_size("group") // 2
+    kv, offsets = [kv], [0]
     last = None
     for d in order:
         terms[d] += [swap(pieces[t * seq + d], "tp", t) for t in range(1, tp)]
         if d == 0:
             break
         if last is not None:
-            _, terms[d] = lax.optimization_barrier((last, terms[d]))
+            if step:
+                kv = kv + [swap(a, "group", step) for a in kv]
+                offsets = offsets + [o ^ step for o in offsets]
+                step //= 2
+            _, terms[d], kv = lax.optimization_barrier((last, terms[d], kv))
         last = sum(a.astype(F32) for a in terms[d]).astype(BF16)
         terms[parent(d)].append(swap(last, "seq", d - parent(d)))
-    result = beside(last)
+    while step:
+        kv = kv + [swap(a, "group", step) for a in kv]
+        offsets = offsets + [o ^ step for o in offsets]
+        step //= 2
+    result = beside(last, kv, offsets)
     terms[0], result = lax.optimization_barrier((terms[0], result))
     return sum(a.astype(F32) for a in terms[0]).astype(BF16), result
 
@@ -281,16 +298,20 @@
 def shards(queries, keys, values, moe_x, expert_ids, gates, grad_out, w_gate, w_up, w_down):
     group = lax.axis_index("group")
     shard = (lax.axis_index("seq") * lax.axis_size("tp") + lax.axis_index("tp")).reshape(1)
-    rows, kv = pack(expert_ids[0].T, gates[0].T, moe_x[0], grad_out[0], keys[0], values[0])
-    pieces, kv_pieces, offsets = spread(rows, kv)
-    base = jnp.stack([group ^ d for d in offsets])
-
-    def attended(sums):
+    rows, own = pack_rows(expert_ids[0].T, gates[0].T, moe_x[0], grad_out[0])
+    pieces = spread(rows)
+    _, *kv = lax.optimization_barrier((pieces[1], keys[0], values[0]))
+    kv = jnp.concatenate(kv, axis=1)
+    pieces[2:], kv = lax.optimization_barrier((pieces[2:], kv))
+    partial = experts(shard, [own] + pieces[1:], w_gate, w_up, w_down)
+    partial, kv = lax.optimization_barrier((partial, kv))
+
+    def attended(sums, kv_pieces, offsets):
         _, first = lax.optimization_barrier((sums, kv_pieces[0]))
+        base = jnp.stack([group ^ d for d in offsets])
         return attend(base, queries[0], [first] + kv_pieces[1:])
 
-    partial = experts(shard, pieces, w_gate, w_up, w_down)
-    total, attn_out = collect(partial, attended)
+    total, attn_out = collect(partial, kv, attended)
     width = moe_x.shape[-1]
     return attn_out[None], total[None, :, :width], total[None, :, width:]
 

time: 70.7 us -> 69.6 us (0.984)
  waiting for transfers between devices: 17.4 us -> 15.3 us
  starting transfers between devices: 21.7 us -> 23.5 us
  local copies, waits for them, and re-layouts: 1.58 us -> 0.68 us
  other arithmetic: 0.82 us -> 1.68 us
  Pallas kernels: 28.3 us -> 27.5 us
    ppermute x17, waiting for transfers between devices: 17.4 us -> 15.3 us  [swap(): return lax.ppermute(array, axis, [(i, i ^ offset) for i in range(count)])]
    ppermute x17, starting transfers between devices: 21.7 us -> 23.5 us  [swap(): return lax.ppermute(array, axis, [(i, i ^ offset) for i in range(count)])]
    unnamed x8, local copies, waits for them, and re-layouts: 0.92 us -> 0.02 us
    concatenate x0 -> x1, other arithmetic: none -> 0.88 us  [shards(): kv = jnp.concatenate(kv, axis=1)]
    pallas_call x1, Pallas kernels: 23 us -> 22.3 us  [experts(): pl.pallas_call(functools.partial(experts_kernel, count=count, slots=slots...]
  transfers between devices with their start and end apart: 17 -> 17, of which waited for: 8 -> 9; matrix products, arithmetic and copies ran while one was open for 1% -> 2% of each run, Pallas kernels for 5% -> 5%
where the time goes in v5:
time: 69.6 us; the launch traced here: 69.4 us
  Pallas kernels  27.5 us (40%)
  starting transfers between devices  23.5 us (34%)
  waiting for transfers between devices  15.3 us (22%)
  other arithmetic  1.68 us (2%)
  between operations  0.71 us (1%)
    ppermute x17, starting transfers between devices, swap(): return lax.ppermute(array, axis, [(i, i ^ offset) for i in range(count)])  23.5 us
    pallas_call x1, Pallas kernels, experts(): pl.pallas_call(functools.partial(experts_kernel, count=count, slots=slots...  22.3 us
    ppermute x17, waiting for transfers between devices, swap(): return lax.ppermute(array, axis, [(i, i ^ offset) for i in range(count)])  15.3 us
    pallas_call x1, Pallas kernels, attend(): pl.pallas_call(attention_kernel, in_specs=[SMEM] + [VMEM] * (1 + len(kv))...  3.55 us
    pallas_call x1, Pallas kernels, pack_rows(): pl.pallas_call(pack_kernel, in_specs=[VMEM] * 4, out_specs=[VMEM] * 2, ou...  1.66 us
  transfers between devices with their start and end apart: 17, of which 9 were waited for; matrix products, arithmetic and copies ran while one was open for 2% of the time, Pallas kernels for 5%

profile of v5, /device:TPU:0, one launch (start us, length us, event | category | flops | bytes accessed | tf_op | source)
XLA Modules:
  0.0 69.4 jit_solution(281486101773307694)
XLA Ops:
  0.6 1.7 %pack_rows.1 = (bf16[16,4224]{1,0:T(8,128)(2,1)}, bf16[16,4224]{1,0:T(8,128)(2,1)S(1)}) custom-call(s32[8,16]{1,0:T(8,128)} %bitcast.25, f32[8,16]{1,0:T(8,128)} %bitcast.26, bf16[16,2048]{1,0:T(8,128)(2,1)} %bitcast.21, bf16[16,2048]{1,0:T(8,128)(2,1)} %bitcast.22), custom_call_target="tpu_custom_call" | custom-call | tf_op jit(solution)/shard_map/pack_rows/pallas_call | solution.py:47
  2.3 3.0 %collective-permute-start = (bf16[16,4224]{1,0:T(8,128)(2,1)}, bf16[16,4224]{1,0:T(8,128)(2,1)S(1)}, u32[]{:S(2)}, u32[]{:S(2)}) collective-permute-start(bf16[16,4224]{1,0:T(8,128)(2,1)} %get-tuple-element.56), channel_id=1, source_target_pairs={{0,2},{2,0},{4,6},{6,4},{1,3},{3,1},{5,7},{7,5},{8,10},{10,8},{12,... | collective-permute-start | bytes 405512 | tf_op jit(solution)/shard_map/ppermute | solution.py:26
  5.3 2.6 %collective-permute-start.1 = (bf16[16,4224]{1,0:T(8,128)(2,1)}, bf16[16,4224]{1,0:T(8,128)(2,1)S(1)}, u32[]{:S(2)}, u32[]{:S(2)}) collective-permute-start(bf16[16,4224]{1,0:T(8,128)(2,1)} %get-tuple-element.56), channel_id=1, source_target_pairs={{0,4},{2,6},{4,0},{6,2},{1,5},{3,7},{5,1},{7,3},{8,12},{10,14},{12... | collective-permute-start | bytes 405512 | tf_op jit(solution)/shard_map/ppermute | solution.py:26
  7.9 3.2 %collective-permute-done.refs_1_ = bf16[16,4224]{1,0:T(8,128)(2,1)S(1)} collective-permute-done((bf16[16,4224]{1,0:T(8,128)(2,1)}, bf16[16,4224]{1,0:T(8,128)(2,1)S(1)}, u32[]{:S(2)}, u32[]{:S(2)}) %collective-permute-start) | collective-permute-done | bytes 135200 | tf_op jit(solution)/shard_map/ppermute | solution.py:26
  11.1 1.9 %collective-permute-start.3 = (bf16[16,4224]{1,0:T(8,128)(2,1)}, bf16[16,4224]{1,0:T(8,128)(2,1)S(1)}, u32[]{:S(2)}, u32[]{:S(2)}) collective-permute-start(bf16[16,4224]{1,0:T(8,128)(2,1)} %get-tuple-element.56), channel_id=1, source_target_pairs={{0,1},{1,0},{2,3},{3,2},{4,5},{5,4},{6,7},{7,6},{8,9},{9,8},{10,11... | collective-permute-start | bytes 405512 | tf_op jit(solution)/shard_map/ppermute | solution.py:26
  12.9 1.5 %collective-permute-done.1.refs_2_ = bf16[16,4224]{1,0:T(8,128)(2,1)S(1)} collective-permute-done((bf16[16,4224]{1,0:T(8,128)(2,1)}, bf16[16,4224]{1,0:T(8,128)(2,1)S(1)}, u32[]{:S(2)}, u32[]{:S(2)}) %collective-permute-start.1) | collective-permute-done | bytes 135200 | tf_op jit(solution)/shard_map/ppermute | solution.py:26
  14.4 0.4 collective-permute-start.2
  14.9 1.5 %collective-permute-start.4 = (bf16[16,4224]{1,0:T(8,128)(2,1)S(1)}, bf16[16,4224]{1,0:T(8,128)(2,1)S(1)}, u32[]{:S(2)}, u32[]{:S(2)}) collective-permute-start(bf16[16,4224]{1,0:T(8,128)(2,1)S(1)} %collective-permute-done.refs_1_), channel_id=1, source_target_pairs={{0,1},{1,0},{2,3},{3,2},{4,5},{5,4},{6,7},{7,6},{8,9},{9,8},{10,11... | collective-permute-start | bytes 405512 | tf_op jit(solution)/shard_map/ppermute | solution.py:26
  16.4 0.5 collective-permute-start.5
  16.9 2.6 %collective-permute-done.2.refs_3_ = bf16[16,4224]{1,0:T(8,128)(2,1)S(1)} collective-permute-done((bf16[16,4224]{1,0:T(8,128)(2,1)S(1)}, bf16[16,4224]{1,0:T(8,128)(2,1)S(1)}, u32[]{:S(2)}, u32[]{:S(2)}) %collective-permute-start.2) | collective-permute-done | bytes 135200 | tf_op jit(solution)/shard_map/ppermute | solution.py:26
  19.4 0.0 collective-permute-done.3.refs_4_
  19.4 1.2 %collective-permute-done.4.refs_5_ = bf16[16,4224]{1,0:T(8,128)(2,1)S(1)} collective-permute-done((bf16[16,4224]{1,0:T(8,128)(2,1)S(1)}, bf16[16,4224]{1,0:T(8,128)(2,1)S(1)}, u32[]{:S(2)}, u32[]{:S(2)}) %collective-permute-start.4) | collective-permute-done | bytes 135200 | tf_op jit(solution)/shard_map/ppermute | solution.py:26
  20.7 2.0 %collective-permute-start.6 = (bf16[16,4224]{1,0:T(8,128)(2,1)S(1)}, bf16[16,4224]{1,0:T(8,128)(2,1)S(1)}, u32[]{:S(2)}, u32[]{:S(2)}) collective-permute-start(bf16[16,4224]{1,0:T(8,128)(2,1)S(1)} %collective-permute-done.2.refs_3_), channel_id=1, source_target_pairs={{0,1},{1,0},{2,3},{3,2},{4,5},{5,4},{6,7},{7,6},{8,9},{9,8},{10,11... | collective-permute-start | bytes 405512 | tf_op jit(solution)/shard_map/ppermute | solution.py:26
  22.6 0.9 %pad_maximum_fusion.refs_0_ = bf16[128,512]{1,0:T(8,128)(2,1)S(1)} fusion(bf16[128,256]{1,0:T(8,128)(2,1)} %bitcast.23, bf16[128,256]{1,0:T(8,128)(2,1)} %bitcast.24), kind=kLoop, calls=%fused_computation.4 | loop fusion | flops 262144 | bytes 262144 | tf_op jit(solution)/shard_map/concatenate | solution.py:304
  23.5 0.0 copy-start
  23.5 0.0 collective-permute-done.5.refs_6_
  23.6 2.1 %collective-permute-done.6.refs_7_ = bf16[16,4224]{1,0:T(8,128)(2,1)S(1)} collective-permute-done((bf16[16,4224]{1,0:T(8,128)(2,1)S(1)}, bf16[16,4224]{1,0:T(8,128)(2,1)S(1)}, u32[]{:S(2)}, u32[]{:S(2)}) %collective-permute-start.6) | collective-permute-done | bytes 135200 | tf_op jit(solution)/shard_map/ppermute | solution.py:26
  25.7 22.3 %experts.1 = (bf16[16,4096]{1,0:T(8,128)(2,1)S(1)}, bf16[16,4096]{1,0:T(8,128)(2,1)S(1)}, bf16[16,4096]{1,0:T(8,128)(2,1)S(1)}, bf16[16,4096]{1,0:T(8,128)(2,1)S...) custom-call(s32[1]{0:T(128)} %bitcast.shard_ref, ...), custom_call_target="tpu_custom_call" | custom-call | flops 2415919104 | bytes 37748736 | tf_op jit(solution)/shard_map/experts/pallas_call | solution.py:230
  48.0 2.0 %collective-permute-start.7 = (bf16[16,4096]{1,0:T(8,128)(2,1)S(1)}, bf16[16,4096]{1,0:T(8,128)(2,1)S(1)}, u32[]{:S(2)}, u32[]{:S(2)}) collective-permute-start(bf16[16,4096]{1,0:T(8,128)(2,1)S(1)} %get-tuple-element.79), channel_id=1, source_target_pairs={{0,1},{1,0},{2,3},{3,2},{4,5},{5,4},{6,7},{7,6},{8,9},{9,8},{10,11... | collective-permute-start | bytes 393224 | tf_op jit(solution)/shard_map/ppermute | solution.py:26
  50.0 0.1 collective-permute-start.8
  50.1 1.9 %collective-permute-start.12 = (bf16[16,4096]{1,0:T(8,128)(2,1)S(1)}, bf16[16,4096]{1,0:T(8,128)(2,1)S(1)}, u32[]{:S(2)}, u32[]{:S(2)}) collective-permute-start(bf16[16,4096]{1,0:T(8,128)(2,1)S(1)} %get-tuple-element.86), channel_id=1, source_target_pairs={{0,1},{1,0},{2,3},{3,2},{4,5},{5,4},{6,7},{7,6},{8,9},{9,8},{10,11... | collective-permute-start | bytes 393224 | tf_op jit(solution)/shard_map/ppermute | solution.py:26
  52.1 0.1 collective-permute-start.16
  52.1 1.9 %collective-permute-start.9 = (bf16[128,512]{1,0:T(8,128)(2,1)S(1)}, bf16[128,512]{1,0:T(8,128)(2,1)S(1)}, u32[]{:S(2)}, u32[]{:S(2)}) collective-permute-start(bf16[128,512]{1,0:T(8,128)(2,1)S(1)} %pad_maximum_fusion.refs_0_), channel_id=1, source_target_pairs={{0,16},{8,24},{16,0},{24,8},{1,17},{9,25},{17,1},{25,9},{2,18},{10... | collective-permute-start | bytes 393224 | tf_op jit(solution)/shard_map/ppermute | solution.py:26
  54.1 0.4 collective-permute-done.7
  54.5 1.0 %collective-permute-start.11 = (bf16[16,4096]{1,0:T(8,128)(2,1)S(1)}, bf16[16,4096]{1,0:T(8,128)(2,1)S(1)}, u32[]{:S(2)}, u32[]{:S(2)}) collective-permute-start(bf16[16,4096]{1,0:T(8,128)(2,1)S(1)} %add_convert_fusion.3), channel_id=1, source_target_pairs={{0,2},{2,0},{4,6},{6,4},{1,3},{3,1},{5,7},{7,5},{8,10},{10,8},{12,... | collective-permute-start | bytes 393224 | tf_op jit(solution)/shard_map/ppermute | solution.py:26
  55.6 1.6 %collective-permute-done.8 = bf16[16,4096]{1,0:T(8,128)(2,1)S(1)} collective-permute-done((bf16[16,4096]{1,0:T(8,128)(2,1)S(1)}, bf16[16,4096]{1,0:T(8,128)(2,1)S(1)}, u32[]{:S(2)}, u32[]{:S(2)}) %collective-permute-start.8) | collective-permute-done | bytes 131104 | tf_op jit(solution)/shard_map/ppermute | solution.py:26
  57.1 0.0 collective-permute-done.9.refs_1_
  57.1 0.0 copy-done
  57.1 0.0 copy-start.1
  57.1 0.1 collective-permute-start.13
  57.2 0.5 collective-permute-start.14
  57.8 0.8 %collective-permute-done.12 = bf16[16,4096]{1,0:T(8,128)(2,1)S(1)} collective-permute-done((bf16[16,4096]{1,0:T(8,128)(2,1)S(1)}, bf16[16,4096]{1,0:T(8,128)(2,1)S(1)}, u32[]{:S(2)}, u32[]{:S(2)}) %collective-permute-start.12) | collective-permute-done | bytes 131104 | tf_op jit(solution)/shard_map/ppermute | solution.py:26
  58.5 1.0 %collective-permute-start.10 = (bf16[16,4096]{1,0:T(8,128)(2,1)S(1)}, bf16[16,4096]{1,0:T(8,128)(2,1)S(1)}, u32[]{:S(2)}, u32[]{:S(2)}) collective-permute-start(bf16[16,4096]{1,0:T(8,128)(2,1)S(1)} %add_convert_fusion.2), channel_id=1, source_target_pairs={{0,2},{2,0},{4,6},{6,4},{1,3},{3,1},{5,7},{7,5},{8,10},{10,8},{12,... | collective-permute-start | bytes 393224 | tf_op jit(solution)/shard_map/ppermute | solution.py:26
  59.6 0.0 collective-permute-done.11
  59.6 0.0 collective-permute-done.13.refs_2_
  59.6 0.0 copy-start.2
  59.6 0.0 collective-permute-done.14.refs_3_
  59.6 0.0 copy-start.3
  59.6 0.1 add_convert_fusion.1
  59.7 2.9 %collective-permute-start.15 = (bf16[16,4096]{1,0:T(8,128)(2,1)S(1)}, bf16[16,4096]{1,0:T(8,128)(2,1)S(1)}, u32[]{:S(2)}, u32[]{:S(2)}) collective-permute-start(bf16[16,4096]{1,0:T(8,128)(2,1)S(1)} %add_convert_fusion.1), channel_id=1, source_target_pairs={{0,4},{2,6},{4,0},{6,2},{1,5},{3,7},{5,1},{7,3},{8,12},{10,14},{12... | collective-permute-start | bytes 393224 | tf_op jit(solution)/shard_map/ppermute | solution.py:26
  62.6 0.6 pad_add_fusion.base_ref
  63.2 0.0 copy-done.1
  63.2 0.0 copy-done.2
  63.2 0.0 copy-done.3
  63.2 3.6 %attention.1 = bf16[128,2048]{1,0:T(8,128)(2,1)} custom-call(s32[4]{0:T(128)} %pad_add_fusion.base_ref, bf16[128,2048]{1,0:T(8,128)(2,1)} %bitcast.27, bf16[128,512]{1,0:T(8,128)(2,1)} %copy-done, bf16[128,512]{1,0:T(8,128)(2,1)} %copy-done.1, bf16[128,512]{1,0:T(8,128)(2,1)} %copy-done.2, bf16[128,512]{1,0:T(8,128)(2,1)} %copy-done.3), custom_call_target="tpu_custom_call" | custom-call | flops 536870912 | bytes 1048576 | tf_op jit(solution)/shard_map/attention/pallas_call | solution.py:92
  66.8 0.0 collective-permute-done.16
  66.8 0.0 collective-permute-done.10
  66.8 1.8 %collective-permute-done.15 = bf16[16,4096]{1,0:T(8,128)(2,1)S(1)} collective-permute-done((bf16[16,4096]{1,0:T(8,128)(2,1)S(1)}, bf16[16,4096]{1,0:T(8,128)(2,1)S(1)}, u32[]{:S(2)}, u32[]{:S(2)}) %collective-permute-start.15) | collective-permute-done | bytes 131104 | tf_op jit(solution)/shard_map/ppermute | solution.py:26
  68.6 0.1 add_convert_fusion
  68.7 0.7 slice_bitcast_fusion
  (2 shorter events, 0.1 us)
Async XLA Ops:
  2.3 8.8 %collective-permute-start = (bf16[16,4224]{1,0:T(8,128)(2,1)}, bf16[16,4224]{1,0:T(8,128)(2,1)S(1)}, u32[]{:S(2)}, u32[]{:S(2)}) collective-permute-start(bf16[16,4224]{1,0:T(8,128)(2,1)} %get-tuple-element.56), channel_id=1, source_target_pairs={{0,2},{2,0},{4,6},{6,4},{1,3},{3,1},{5,7},{7,5},{8,10},{10,8},{12,... | collective-permute-start | bytes 405512 | tf_op jit(solution)/shard_map/ppermute | solution.py:26
  5.3 9.1 %collective-permute-start.1 = (bf16[16,4224]{1,0:T(8,128)(2,1)}, bf16[16,4224]{1,0:T(8,128)(2,1)S(1)}, u32[]{:S(2)}, u32[]{:S(2)}) collective-permute-start(bf16[16,4224]{1,0:T(8,128)(2,1)} %get-tuple-element.56), channel_id=1, source_target_pairs={{0,4},{2,6},{4,0},{6,2},{1,5},{3,7},{5,1},{7,3},{8,12},{10,14},{12... | collective-permute-start | bytes 405512 | tf_op jit(solution)/shard_map/ppermute | solution.py:26
  11.1 8.3 %collective-permute-start.3 = (bf16[16,4224]{1,0:T(8,128)(2,1)}, bf16[16,4224]{1,0:T(8,128)(2,1)S(1)}, u32[]{:S(2)}, u32[]{:S(2)}) collective-permute-start(bf16[16,4224]{1,0:T(8,128)(2,1)} %get-tuple-element.56), channel_id=1, source_target_pairs={{0,1},{1,0},{2,3},{3,2},{4,5},{5,4},{6,7},{7,6},{8,9},{9,8},{10,11... | collective-permute-start | bytes 405512 | tf_op jit(solution)/shard_map/ppermute | solution.py:26
  14.4 5.0 %collective-permute-start.2 = (bf16[16,4224]{1,0:T(8,128)(2,1)S(1)}, bf16[16,4224]{1,0:T(8,128)(2,1)S(1)}, u32[]{:S(2)}, u32[]{:S(2)}) collective-permute-start(bf16[16,4224]{1,0:T(8,128)(2,1)S(1)} %collective-permute-done.1.refs_2_), channel_id=1, source_target_pairs={{0,2},{2,0},{4,6},{6,4},{1,3},{3,1},{5,7},{7,5},{8,10},{10,8},{12,... | collective-permute-start | bytes 405512 | tf_op jit(solution)/shard_map/ppermute | solution.py:26
  14.9 5.8 %collective-permute-start.4 = (bf16[16,4224]{1,0:T(8,128)(2,1)S(1)}, bf16[16,4224]{1,0:T(8,128)(2,1)S(1)}, u32[]{:S(2)}, u32[]{:S(2)}) collective-permute-start(bf16[16,4224]{1,0:T(8,128)(2,1)S(1)} %collective-permute-done.refs_1_), channel_id=1, source_target_pairs={{0,1},{1,0},{2,3},{3,2},{4,5},{5,4},{6,7},{7,6},{8,9},{9,8},{10,11... | collective-permute-start | bytes 405512 | tf_op jit(solution)/shard_map/ppermute | solution.py:26
  16.4 7.2 %collective-permute-start.5 = (bf16[16,4224]{1,0:T(8,128)(2,1)S(1)}, bf16[16,4224]{1,0:T(8,128)(2,1)S(1)}, u32[]{:S(2)}, u32[]{:S(2)}) collective-permute-start(bf16[16,4224]{1,0:T(8,128)(2,1)S(1)} %collective-permute-done.1.refs_2_), channel_id=1, source_target_pairs={{0,1},{1,0},{2,3},{3,2},{4,5},{5,4},{6,7},{7,6},{8,9},{9,8},{10,11... | collective-permute-start | bytes 405512 | tf_op jit(solution)/shard_map/ppermute | solution.py:26
  20.7 5.0 %collective-permute-start.6 = (bf16[16,4224]{1,0:T(8,128)(2,1)S(1)}, bf16[16,4224]{1,0:T(8,128)(2,1)S(1)}, u32[]{:S(2)}, u32[]{:S(2)}) collective-permute-start(bf16[16,4224]{1,0:T(8,128)(2,1)S(1)} %collective-permute-done.2.refs_3_), channel_id=1, source_target_pairs={{0,1},{1,0},{2,3},{3,2},{4,5},{5,4},{6,7},{7,6},{8,9},{9,8},{10,11... | collective-permute-start | bytes 405512 | tf_op jit(solution)/shard_map/ppermute | solution.py:26
  23.5 33.6 %copy-start = (bf16[128,512]{1,0:T(8,128)(2,1)}, bf16[128,512]{1,0:T(8,128)(2,1)S(1)}, u32[]{:S(2)}) copy-start(bf16[128,512]{1,0:T(8,128)(2,1)S(1)} %pad_maximum_fusion.refs_0_) | copy-start | bytes 393220
  48.0 6.5 %collective-permute-start.7 = (bf16[16,4096]{1,0:T(8,128)(2,1)S(1)}, bf16[16,4096]{1,0:T(8,128)(2,1)S(1)}, u32[]{:S(2)}, u32[]{:S(2)}) collective-permute-start(bf16[16,4096]{1,0:T(8,128)(2,1)S(1)} %get-tuple-element.79), channel_id=1, source_target_pairs={{0,1},{1,0},{2,3},{3,2},{4,5},{5,4},{6,7},{7,6},{8,9},{9,8},{10,11... | collective-permute-start | bytes 393224 | tf_op jit(solution)/shard_map/ppermute | solution.py:26
  50.0 7.1 %collective-permute-start.8 = (bf16[16,4096]{1,0:T(8,128)(2,1)S(1)}, bf16[16,4096]{1,0:T(8,128)(2,1)S(1)}, u32[]{:S(2)}, u32[]{:S(2)}) collective-permute-start(bf16[16,4096]{1,0:T(8,128)(2,1)S(1)} %get-tuple-element.81), channel_id=1, source_target_pairs={{0,1},{1,0},{2,3},{3,2},{4,5},{5,4},{6,7},{7,6},{8,9},{9,8},{10,11... | collective-permute-start | bytes 393224 | tf_op jit(solution)/shard_map/ppermute | solution.py:26
  50.1 8.4 %collective-permute-start.12 = (bf16[16,4096]{1,0:T(8,128)(2,1)S(1)}, bf16[16,4096]{1,0:T(8,128)(2,1)S(1)}, u32[]{:S(2)}, u32[]{:S(2)}) collective-permute-start(bf16[16,4096]{1,0:T(8,128)(2,1)S(1)} %get-tuple-element.86), channel_id=1, source_target_pairs={{0,1},{1,0},{2,3},{3,2},{4,5},{5,4},{6,7},{7,6},{8,9},{9,8},{10,11... | collective-permute-start | bytes 393224 | tf_op jit(solution)/shard_map/ppermute | solution.py:26
  52.1 14.7 %collective-permute-start.16 = (bf16[16,4096]{1,0:T(8,128)(2,1)S(1)}, bf16[16,4096]{1,0:T(8,128)(2,1)S(1)}, u32[]{:S(2)}, u32[]{:S(2)}) collective-permute-start(bf16[16,4096]{1,0:T(8,128)(2,1)S(1)} %get-tuple-element.92), channel_id=1, source_target_pairs={{0,1},{1,0},{2,3},{3,2},{4,5},{5,4},{6,7},{7,6},{8,9},{9,8},{10,11... | collective-permute-start | bytes 393224 | tf_op jit(solution)/shard_map/ppermute | solution.py:26
  52.1 5.0 %collective-permute-start.9 = (bf16[128,512]{1,0:T(8,128)(2,1)S(1)}, bf16[128,512]{1,0:T(8,128)(2,1)S(1)}, u32[]{:S(2)}, u32[]{:S(2)}) collective-permute-start(bf16[128,512]{1,0:T(8,128)(2,1)S(1)} %pad_maximum_fusion.refs_0_), channel_id=1, source_target_pairs={{0,16},{8,24},{16,0},{24,8},{1,17},{9,25},{17,1},{25,9},{2,18},{10... | collective-permute-start | bytes 393224 | tf_op jit(solution)/shard_map/ppermute | solution.py:26
  54.5 5.0 %collective-permute-start.11 = (bf16[16,4096]{1,0:T(8,128)(2,1)S(1)}, bf16[16,4096]{1,0:T(8,128)(2,1)S(1)}, u32[]{:S(2)}, u32[]{:S(2)}) collective-permute-start(bf16[16,4096]{1,0:T(8,128)(2,1)S(1)} %add_convert_fusion.3), channel_id=1, source_target_pairs={{0,2},{2,0},{4,6},{6,4},{1,3},{3,1},{5,7},{7,5},{8,10},{10,8},{12,... | collective-permute-start | bytes 393224 | tf_op jit(solution)/shard_map/ppermute | solution.py:26
  57.1 6.1 %copy-start.1 = (bf16[128,512]{1,0:T(8,128)(2,1)}, bf16[128,512]{1,0:T(8,128)(2,1)S(1)}, u32[]{:S(2)}) copy-start(bf16[128,512]{1,0:T(8,128)(2,1)S(1)} %collective-permute-done.9.refs_1_) | copy-start | bytes 393220
  57.1 2.4 %collective-permute-start.13 = (bf16[128,512]{1,0:T(8,128)(2,1)S(1)}, bf16[128,512]{1,0:T(8,128)(2,1)S(1)}, u32[]{:S(2)}, u32[]{:S(2)}) collective-permute-start(bf16[128,512]{1,0:T(8,128)(2,1)S(1)} %pad_maximum_fusion.refs_0_), channel_id=1, source_target_pairs={{0,8},{8,0},{16,24},{24,16},{1,9},{9,1},{17,25},{25,17},{2,10},{10... | collective-permute-start | bytes 393224 | tf_op jit(solution)/shard_map/ppermute | solution.py:26
  57.2 2.4 %collective-permute-start.14 = (bf16[128,512]{1,0:T(8,128)(2,1)S(1)}, bf16[128,512]{1,0:T(8,128)(2,1)S(1)}, u32[]{:S(2)}, u32[]{:S(2)}) collective-permute-start(bf16[128,512]{1,0:T(8,128)(2,1)S(1)} %collective-permute-done.9.refs_1_), channel_id=1, source_target_pairs={{0,8},{8,0},{16,24},{24,16},{1,9},{9,1},{17,25},{25,17},{2,10},{10... | collective-permute-start | bytes 393224 | tf_op jit(solution)/shard_map/ppermute | solution.py:26
  58.5 8.2 %collective-permute-start.10 = (bf16[16,4096]{1,0:T(8,128)(2,1)S(1)}, bf16[16,4096]{1,0:T(8,128)(2,1)S(1)}, u32[]{:S(2)}, u32[]{:S(2)}) collective-permute-start(bf16[16,4096]{1,0:T(8,128)(2,1)S(1)} %add_convert_fusion.2), channel_id=1, source_target_pairs={{0,2},{2,0},{4,6},{6,4},{1,3},{3,1},{5,7},{7,5},{8,10},{10,8},{12,... | collective-permute-start | bytes 393224 | tf_op jit(solution)/shard_map/ppermute | solution.py:26
  59.6 3.6 %copy-start.2 = (bf16[128,512]{1,0:T(8,128)(2,1)}, bf16[128,512]{1,0:T(8,128)(2,1)S(1)}, u32[]{:S(2)}) copy-start(bf16[128,512]{1,0:T(8,128)(2,1)S(1)} %collective-permute-done.13.refs_2_) | copy-start | bytes 393220
  59.6 3.6 %copy-start.3 = (bf16[128,512]{1,0:T(8,128)(2,1)}, bf16[128,512]{1,0:T(8,128)(2,1)S(1)}, u32[]{:S(2)}) copy-start(bf16[128,512]{1,0:T(8,128)(2,1)S(1)} %collective-permute-done.14.refs_3_) | copy-start | bytes 393220
  59.7 9.0 %collective-permute-start.15 = (bf16[16,4096]{1,0:T(8,128)(2,1)S(1)}, bf16[16,4096]{1,0:T(8,128)(2,1)S(1)}, u32[]{:S(2)}, u32[]{:S(2)}) collective-permute-start(bf16[16,4096]{1,0:T(8,128)(2,1)S(1)} %add_convert_fusion.1), channel_id=1, source_target_pairs={{0,4},{2,6},{4,0},{6,2},{1,5},{3,7},{5,1},{7,3},{8,12},{10,14},{12... | collective-permute-start | bytes 393224 | tf_op jit(solution)/shard_map/ppermute | solution.py:26

commit v6 on v5

--- a/solution.py
+++ b/solution.py
@@ -54,6 +54,24 @@
         ],
         name="pack_rows",
     )(ids, gates, x, grad)
+
+
+def join_kernel(key_ref, value_ref, out_ref):
+    half = key_ref.shape[1]
+    out_ref[:, :half] = key_ref[...]
+    out_ref[:, half:] = value_ref[...]
+
+
+def join(keys, values):
+    rows, half = keys.shape
+    return pl.pallas_call(
+        join_kernel,
+        in_specs=[VMEM] * 2,
+        out_specs=VMEM,
+        out_shape=jax.ShapeDtypeStruct((rows, 2 * half), BF16),
+        cost_estimate=pl.CostEstimate(flops=0, bytes_accessed=10**7, transcendentals=0),
+        name="join",
+    )(keys, values)
 
 
 def attention_kernel(base_ref, q_ref, *refs):
@@ -251,20 +269,27 @@
     return [swap(block, "tp", t) for t in range(1, lax.axis_size("tp"))]
 
 
-def spread(rows):
+def spread(rows, beside):
     near, far = [rows], []
     for d in range(1, lax.axis_size("seq")):
         block = swap(near[parent(d)], "seq", d - parent(d))
         if d == 1:
-            block, rows = lax.optimization_barrier((block, rows))
+            rows, beside = lax.optimization_barrier((rows, beside))
             far.append(over_tp(rows))
+        elif d == 2:
+            far[0], near[1] = lax.optimization_barrier((far[0], near[1]))
+            far.append([swap(a, "seq", 1) for a in far[0]])
         else:
             far.append(over_tp(near[d - 1]))
-        if d > 2:
-            block, far[: d - 1] = lax.optimization_barrier((block, far[: d - 1]))
+            block, far[: d - 2] = lax.optimization_barrier((block, far[: d - 2]))
         near.append(block)
-    far.append(over_tp(near[-1]))
-    return near + [a for blocks in zip(*far) for a in blocks]
+    if len(near) == 2:
+        far.append([swap(a, "seq", 1) for a in far[0]])
+    elif len(near) > 2:
+        far.append(over_tp(near[-1]))
+    else:
+        far.append(over_tp(rows))
+    return near + [a for blocks in zip(*far) for a in blocks], beside
 
 
 def collect(pieces, kv, beside):
@@ -299,10 +324,7 @@
     group = lax.axis_index("group")
     shard = (lax.axis_index("seq") * lax.axis_size("tp") + lax.axis_index("tp")).reshape(1)
     rows, own = pack_rows(expert_ids[0].T, gates[0].T, moe_x[0], grad_out[0])
-    pieces = spread(rows)
-    _, *kv = lax.optimization_barrier((pieces[1], keys[0], values[0]))
-    kv = jnp.concatenate(kv, axis=1)
-    pieces[2:], kv = lax.optimization_barrier((pieces[2:], kv))
+    pieces, kv = spread(rows, join(keys[0], values[0]))
     partial = experts(shard, [own] + pieces[1:], w_gate, w_up, w_down)
     partial, kv = lax.optimization_barrier((partial, kv))
 

time: 69.6 us -> 68.4 us (0.983)
  starting transfers between devices: 23.5 us -> 21.7 us
  Pallas kernels: 27.5 us -> 29.1 us
  other arithmetic: 1.68 us -> 0.8 us
    ppermute x17, starting transfers between devices: 23.5 us -> 21.7 us  [swap(): return lax.ppermute(array, axis, [(i, i ^ offset) for i in range(count)])]
    pallas_call x0 -> x1, Pallas kernels: none -> 1.53 us  [join(): pl.pallas_call(join_kernel, in_specs=[VMEM] * 2, out_specs=VMEM, out_shap...]
    concatenate x1 -> x0, other arithmetic: 0.88 us -> none  [shards(): kv = jnp.concatenate(kv, axis=1)]
  transfers between devices with their start and end apart: 17 -> 17, of which waited for: 9 -> 9; matrix products, arithmetic and copies ran while one was open for 2% -> 1% of each run, Pallas kernels for 5% -> 7%
where the time goes in v6:
time: 68.4 us; the launch traced here: 68.1 us
  Pallas kernels  29.1 us (43%)
  starting transfers between devices  21.7 us (32%)
  waiting for transfers between devices  15.2 us (22%)
  other arithmetic  0.8 us (1%)
  between operations  0.7 us (1%)
    pallas_call x1, Pallas kernels, experts(): pl.pallas_call(functools.partial(experts_kernel, count=count, slots=slots...  22.3 us
    ppermute x17, starting transfers between devices, swap(): return lax.ppermute(array, axis, [(i, i ^ offset) for i in range(count)])  21.7 us
    ppermute x17, waiting for transfers between devices, swap(): return lax.ppermute(array, axis, [(i, i ^ offset) for i in range(count)])  15.2 us
    pallas_call x1, Pallas kernels, attend(): pl.pallas_call(attention_kernel, in_specs=[SMEM] + [VMEM] * (1 + len(kv))...  3.55 us
    pallas_call x1, Pallas kernels, pack_rows(): pl.pallas_call(pack_kernel, in_specs=[VMEM] * 4, out_specs=[VMEM] * 2, ou...  1.66 us
    pallas_call x1, Pallas kernels, join(): pl.pallas_call(join_kernel, in_specs=[VMEM] * 2, out_specs=VMEM, out_shap...  1.53 us
  transfers between devices with their start and end apart: 17, of which 9 were waited for; matrix products, arithmetic and copies ran while one was open for 1% of the time, Pallas kernels for 7%

profile of v6, /device:TPU:0, one launch (start us, length us, event | category | flops | bytes accessed | tf_op | source)
XLA Modules:
  0.0 68.1 jit_solution(887509435052772722)
XLA Ops:
  0.6 1.7 %pack_rows.1 = (bf16[16,4224]{1,0:T(8,128)(2,1)}, bf16[16,4224]{1,0:T(8,128)(2,1)S(1)}) custom-call(s32[8,16]{1,0:T(8,128)} %bitcast.25, f32[8,16]{1,0:T(8,128)} %bitcast.26, bf16[16,2048]{1,0:T(8,128)(2,1)} %bitcast.21, bf16[16,2048]{1,0:T(8,128)(2,1)} %bitcast.22), custom_call_target="tpu_custom_call" | custom-call | tf_op jit(solution)/shard_map/pack_rows/pallas_call | solution.py:47
  2.3 4.0 %collective-permute-start.2 = (bf16[16,4224]{1,0:T(8,128)(2,1)}, bf16[16,4224]{1,0:T(8,128)(2,1)S(1)}, u32[]{:S(2)}, u32[]{:S(2)}) collective-permute-start(bf16[16,4224]{1,0:T(8,128)(2,1)} %get-tuple-element.47), channel_id=1, source_target_pairs={{0,4},{2,6},{4,0},{6,2},{1,5},{3,7},{5,1},{7,3},{8,12},{10,14},{12... | collective-permute-start | bytes 405512 | tf_op jit(solution)/shard_map/ppermute | solution.py:26
  6.3 1.5 %join.1.refs_0_ = bf16[128,512]{1,0:T(8,128)(2,1)} custom-call(bf16[128,256]{1,0:T(8,128)(2,1)} %bitcast.23, bf16[128,256]{1,0:T(8,128)(2,1)} %bitcast.24), custom_call_target="tpu_custom_call" | custom-call | bytes 10000000 | tf_op jit(solution)/shard_map/join/pallas_call | solution.py:67
  7.9 1.5 %collective-permute-start = (bf16[16,4224]{1,0:T(8,128)(2,1)}, bf16[16,4224]{1,0:T(8,128)(2,1)S(1)}, u32[]{:S(2)}, u32[]{:S(2)}) collective-permute-start(bf16[16,4224]{1,0:T(8,128)(2,1)} %get-tuple-element.47), channel_id=1, source_target_pairs={{0,1},{1,0},{2,3},{3,2},{4,5},{5,4},{6,7},{7,6},{8,9},{9,8},{10,11... | collective-permute-start | bytes 405512 | tf_op jit(solution)/shard_map/ppermute | solution.py:26
  9.4 1.6 %collective-permute-start.1 = (bf16[16,4224]{1,0:T(8,128)(2,1)}, bf16[16,4224]{1,0:T(8,128)(2,1)S(1)}, u32[]{:S(2)}, u32[]{:S(2)}) collective-permute-start(bf16[16,4224]{1,0:T(8,128)(2,1)} %get-tuple-element.47), channel_id=1, source_target_pairs={{0,2},{2,0},{4,6},{6,4},{1,3},{3,1},{5,7},{7,5},{8,10},{10,8},{12,... | collective-permute-start | bytes 405512 | tf_op jit(solution)/shard_map/ppermute | solution.py:26
  11.0 2.2 %collective-permute-done.2.refs_2_ = bf16[16,4224]{1,0:T(8,128)(2,1)S(1)} collective-permute-done((bf16[16,4224]{1,0:T(8,128)(2,1)}, bf16[16,4224]{1,0:T(8,128)(2,1)S(1)}, u32[]{:S(2)}, u32[]{:S(2)}) %collective-permute-start.2) | collective-permute-done | bytes 135200 | tf_op jit(solution)/shard_map/ppermute | solution.py:26
  13.1 0.8 %collective-permute-start.3 = (bf16[16,4224]{1,0:T(8,128)(2,1)S(1)}, bf16[16,4224]{1,0:T(8,128)(2,1)S(1)}, u32[]{:S(2)}, u32[]{:S(2)}) collective-permute-start(bf16[16,4224]{1,0:T(8,128)(2,1)S(1)} %collective-permute-done.2.refs_2_), channel_id=1, source_target_pairs={{0,2},{2,0},{4,6},{6,4},{1,3},{3,1},{5,7},{7,5},{8,10},{10,8},{12,... | collective-permute-start | bytes 405512 | tf_op jit(solution)/shard_map/ppermute | solution.py:26
  13.9 0.0 collective-permute-done.refs_4_
  13.9 2.1 %collective-permute-done.1.refs_1_ = bf16[16,4224]{1,0:T(8,128)(2,1)S(1)} collective-permute-done((bf16[16,4224]{1,0:T(8,128)(2,1)}, bf16[16,4224]{1,0:T(8,128)(2,1)S(1)}, u32[]{:S(2)}, u32[]{:S(2)}) %collective-permute-start.1) | collective-permute-done | bytes 135200 | tf_op jit(solution)/shard_map/ppermute | solution.py:26
  16.0 0.1 collective-permute-start.4
  16.2 0.6 collective-permute-start.5
  16.7 2.3 %collective-permute-done.3.refs_3_ = bf16[16,4224]{1,0:T(8,128)(2,1)S(1)} collective-permute-done((bf16[16,4224]{1,0:T(8,128)(2,1)S(1)}, bf16[16,4224]{1,0:T(8,128)(2,1)S(1)}, u32[]{:S(2)}, u32[]{:S(2)}) %collective-permute-start.3) | collective-permute-done | bytes 135200 | tf_op jit(solution)/shard_map/ppermute | solution.py:26
  19.1 2.0 %collective-permute-start.6 = (bf16[16,4224]{1,0:T(8,128)(2,1)S(1)}, bf16[16,4224]{1,0:T(8,128)(2,1)S(1)}, u32[]{:S(2)}, u32[]{:S(2)}) collective-permute-start(bf16[16,4224]{1,0:T(8,128)(2,1)S(1)} %collective-permute-done.3.refs_3_), channel_id=1, source_target_pairs={{0,1},{1,0},{2,3},{3,2},{4,5},{5,4},{6,7},{7,6},{8,9},{9,8},{10,11... | collective-permute-start | bytes 405512 | tf_op jit(solution)/shard_map/ppermute | solution.py:26
  21.1 1.0 %collective-permute-done.5.refs_6_ = bf16[16,4224]{1,0:T(8,128)(2,1)S(1)} collective-permute-done((bf16[16,4224]{1,0:T(8,128)(2,1)S(1)}, bf16[16,4224]{1,0:T(8,128)(2,1)S(1)}, u32[]{:S(2)}, u32[]{:S(2)}) %collective-permute-start.5) | collective-permute-done | bytes 135200 | tf_op jit(solution)/shard_map/ppermute | solution.py:26
  22.1 0.0 collective-permute-done.4.refs_5_
  22.1 2.2 %collective-permute-done.6.refs_7_ = bf16[16,4224]{1,0:T(8,128)(2,1)S(1)} collective-permute-done((bf16[16,4224]{1,0:T(8,128)(2,1)S(1)}, bf16[16,4224]{1,0:T(8,128)(2,1)S(1)}, u32[]{:S(2)}, u32[]{:S(2)}) %collective-permute-start.6) | collective-permute-done | bytes 135200 | tf_op jit(solution)/shard_map/ppermute | solution.py:26
  24.3 0.0 copy-start
  24.3 22.3 %experts.1 = (bf16[16,4096]{1,0:T(8,128)(2,1)S(1)}, bf16[16,4096]{1,0:T(8,128)(2,1)S(1)}, bf16[16,4096]{1,0:T(8,128)(2,1)S(1)}, bf16[16,4096]{1,0:T(8,128)(2,1)S...) custom-call(s32[1]{0:T(128)} %bitcast.shard_ref, ...), custom_call_target="tpu_custom_call" | custom-call | flops 2415919104 | bytes 37748736 | tf_op jit(solution)/shard_map/experts/pallas_call | solution.py:248
  46.6 1.9 %collective-permute-start.7 = (bf16[16,4096]{1,0:T(8,128)(2,1)S(1)}, bf16[16,4096]{1,0:T(8,128)(2,1)S(1)}, u32[]{:S(2)}, u32[]{:S(2)}) collective-permute-start(bf16[16,4096]{1,0:T(8,128)(2,1)S(1)} %get-tuple-element.63), channel_id=1, source_target_pairs={{0,1},{1,0},{2,3},{3,2},{4,5},{5,4},{6,7},{7,6},{8,9},{9,8},{10,11... | collective-permute-start | bytes 393224 | tf_op jit(solution)/shard_map/ppermute | solution.py:26
  48.5 0.2 collective-permute-start.8
  48.7 1.8 %collective-permute-start.12 = (bf16[16,4096]{1,0:T(8,128)(2,1)S(1)}, bf16[16,4096]{1,0:T(8,128)(2,1)S(1)}, u32[]{:S(2)}, u32[]{:S(2)}) collective-permute-start(bf16[16,4096]{1,0:T(8,128)(2,1)S(1)} %get-tuple-element.70), channel_id=1, source_target_pairs={{0,1},{1,0},{2,3},{3,2},{4,5},{5,4},{6,7},{7,6},{8,9},{9,8},{10,11... | collective-permute-start | bytes 393224 | tf_op jit(solution)/shard_map/ppermute | solution.py:26
  50.5 0.2 collective-permute-start.16
  50.7 0.0 copy-done
  50.7 1.6 %collective-permute-start.9 = (bf16[128,512]{1,0:T(8,128)(2,1)S(1)}, bf16[128,512]{1,0:T(8,128)(2,1)S(1)}, u32[]{:S(2)}, u32[]{:S(2)}) collective-permute-start(bf16[128,512]{1,0:T(8,128)(2,1)S(1)} %copy-done), channel_id=1, source_target_pairs={{0,16},{8,24},{16,0},{24,8},{1,17},{9,25},{17,1},{25,9},{2,18},{10... | collective-permute-start | bytes 393224 | tf_op jit(solution)/shard_map/ppermute | solution.py:26
  52.3 0.8 %collective-permute-done.7 = bf16[16,4096]{1,0:T(8,128)(2,1)S(1)} collective-permute-done((bf16[16,4096]{1,0:T(8,128)(2,1)S(1)}, bf16[16,4096]{1,0:T(8,128)(2,1)S(1)}, u32[]{:S(2)}, u32[]{:S(2)}) %collective-permute-start.7) | collective-permute-done | bytes 131104 | tf_op jit(solution)/shard_map/ppermute | solution.py:26
  53.1 1.8 %collective-permute-start.11 = (bf16[16,4096]{1,0:T(8,128)(2,1)S(1)}, bf16[16,4096]{1,0:T(8,128)(2,1)S(1)}, u32[]{:S(2)}, u32[]{:S(2)}) collective-permute-start(bf16[16,4096]{1,0:T(8,128)(2,1)S(1)} %add_convert_fusion.3), channel_id=1, source_target_pairs={{0,2},{2,0},{4,6},{6,4},{1,3},{3,1},{5,7},{7,5},{8,10},{10,8},{12,... | collective-permute-start | bytes 393224 | tf_op jit(solution)/shard_map/ppermute | solution.py:26
  55.0 1.0 %collective-permute-done.8 = bf16[16,4096]{1,0:T(8,128)(2,1)S(1)} collective-permute-done((bf16[16,4096]{1,0:T(8,128)(2,1)S(1)}, bf16[16,4096]{1,0:T(8,128)(2,1)S(1)}, u32[]{:S(2)}, u32[]{:S(2)}) %collective-permute-start.8) | collective-permute-done | bytes 131104 | tf_op jit(solution)/shard_map/ppermute | solution.py:26
  55.9 0.0 collective-permute-done.9.refs_1_
  55.9 0.0 copy-start.1
  55.9 0.0 collective-permute-start.13
  55.9 0.5 collective-permute-start.14
  56.5 1.4 %collective-permute-done.12 = bf16[16,4096]{1,0:T(8,128)(2,1)S(1)} collective-permute-done((bf16[16,4096]{1,0:T(8,128)(2,1)S(1)}, bf16[16,4096]{1,0:T(8,128)(2,1)S(1)}, u32[]{:S(2)}, u32[]{:S(2)}) %collective-permute-start.12) | collective-permute-done | bytes 131104 | tf_op jit(solution)/shard_map/ppermute | solution.py:26
  57.9 1.6 %collective-permute-start.10 = (bf16[16,4096]{1,0:T(8,128)(2,1)S(1)}, bf16[16,4096]{1,0:T(8,128)(2,1)S(1)}, u32[]{:S(2)}, u32[]{:S(2)}) collective-permute-start(bf16[16,4096]{1,0:T(8,128)(2,1)S(1)} %add_convert_fusion.2), channel_id=1, source_target_pairs={{0,2},{2,0},{4,6},{6,4},{1,3},{3,1},{5,7},{7,5},{8,10},{10,8},{12,... | collective-permute-start | bytes 393224 | tf_op jit(solution)/shard_map/ppermute | solution.py:26
  59.5 0.0 collective-permute-done.11
  59.5 0.0 collective-permute-done.13.refs_2_
  59.5 0.0 copy-start.2
  59.5 0.0 collective-permute-done.14.refs_3_
  59.5 0.0 copy-start.3
  59.5 0.1 add_convert_fusion.1
  59.6 1.4 %collective-permute-start.15 = (bf16[16,4096]{1,0:T(8,128)(2,1)S(1)}, bf16[16,4096]{1,0:T(8,128)(2,1)S(1)}, u32[]{:S(2)}, u32[]{:S(2)}) collective-permute-start(bf16[16,4096]{1,0:T(8,128)(2,1)S(1)} %add_convert_fusion.1), channel_id=1, source_target_pairs={{0,4},{2,6},{4,0},{6,2},{1,5},{3,7},{5,1},{7,3},{8,12},{10,14},{12... | collective-permute-start | bytes 393224 | tf_op jit(solution)/shard_map/ppermute | solution.py:26
  61.0 0.6 pad_add_fusion.base_ref
  61.6 0.0 copy-done.1
  61.6 0.0 copy-done.2
  61.6 0.0 copy-done.3
  61.6 3.6 %attention.1 = bf16[128,2048]{1,0:T(8,128)(2,1)} custom-call(s32[4]{0:T(128)} %pad_add_fusion.base_ref, bf16[128,2048]{1,0:T(8,128)(2,1)} %bitcast.27, bf16[128,512]{1,0:T(8,128)(2,1)} %join.1.refs_0_, bf16[128,512]{1,0:T(8,128)(2,1)} %copy-done.1, bf16[128,512]{1,0:T(8,128)(2,1)} %copy-done.2, bf16[128,512]{1,0:T(8,128)(2,1)} %copy-done.3), custom_call_target="tpu_custom_call" | custom-call | flops 536870912 | bytes 1048576 | tf_op jit(solution)/shard_map/attention/pallas_call | solution.py:110
  65.2 0.0 collective-permute-done.16
  65.2 0.0 collective-permute-done.10
  65.2 2.2 %collective-permute-done.15 = bf16[16,4096]{1,0:T(8,128)(2,1)S(1)} collective-permute-done((bf16[16,4096]{1,0:T(8,128)(2,1)S(1)}, bf16[16,4096]{1,0:T(8,128)(2,1)S(1)}, u32[]{:S(2)}, u32[]{:S(2)}) %collective-permute-start.15) | collective-permute-done | bytes 131104 | tf_op jit(solution)/shard_map/ppermute | solution.py:26
  67.4 0.1 add_convert_fusion
  67.5 0.7 slice_bitcast_fusion
  (2 shorter events, 0.1 us)
Async XLA Ops:
  2.3 10.8 %collective-permute-start.2 = (bf16[16,4224]{1,0:T(8,128)(2,1)}, bf16[16,4224]{1,0:T(8,128)(2,1)S(1)}, u32[]{:S(2)}, u32[]{:S(2)}) collective-permute-start(bf16[16,4224]{1,0:T(8,128)(2,1)} %get-tuple-element.47), channel_id=1, source_target_pairs={{0,4},{2,6},{4,0},{6,2},{1,5},{3,7},{5,1},{7,3},{8,12},{10,14},{12... | collective-permute-start | bytes 405512 | tf_op jit(solution)/shard_map/ppermute | solution.py:26
  7.9 6.0 %collective-permute-start = (bf16[16,4224]{1,0:T(8,128)(2,1)}, bf16[16,4224]{1,0:T(8,128)(2,1)S(1)}, u32[]{:S(2)}, u32[]{:S(2)}) collective-permute-start(bf16[16,4224]{1,0:T(8,128)(2,1)} %get-tuple-element.47), channel_id=1, source_target_pairs={{0,1},{1,0},{2,3},{3,2},{4,5},{5,4},{6,7},{7,6},{8,9},{9,8},{10,11... | collective-permute-start | bytes 405512 | tf_op jit(solution)/shard_map/ppermute | solution.py:26
  9.4 6.7 %collective-permute-start.1 = (bf16[16,4224]{1,0:T(8,128)(2,1)}, bf16[16,4224]{1,0:T(8,128)(2,1)S(1)}, u32[]{:S(2)}, u32[]{:S(2)}) collective-permute-start(bf16[16,4224]{1,0:T(8,128)(2,1)} %get-tuple-element.47), channel_id=1, source_target_pairs={{0,2},{2,0},{4,6},{6,4},{1,3},{3,1},{5,7},{7,5},{8,10},{10,8},{12,... | collective-permute-start | bytes 405512 | tf_op jit(solution)/shard_map/ppermute | solution.py:26
  13.1 5.9 %collective-permute-start.3 = (bf16[16,4224]{1,0:T(8,128)(2,1)S(1)}, bf16[16,4224]{1,0:T(8,128)(2,1)S(1)}, u32[]{:S(2)}, u32[]{:S(2)}) collective-permute-start(bf16[16,4224]{1,0:T(8,128)(2,1)S(1)} %collective-permute-done.2.refs_2_), channel_id=1, source_target_pairs={{0,2},{2,0},{4,6},{6,4},{1,3},{3,1},{5,7},{7,5},{8,10},{10,8},{12,... | collective-permute-start | bytes 405512 | tf_op jit(solution)/shard_map/ppermute | solution.py:26
  16.0 6.1 %collective-permute-start.4 = (bf16[16,4224]{1,0:T(8,128)(2,1)S(1)}, bf16[16,4224]{1,0:T(8,128)(2,1)S(1)}, u32[]{:S(2)}, u32[]{:S(2)}) collective-permute-start(bf16[16,4224]{1,0:T(8,128)(2,1)S(1)} %collective-permute-done.refs_4_), channel_id=1, source_target_pairs={{0,2},{2,0},{4,6},{6,4},{1,3},{3,1},{5,7},{7,5},{8,10},{10,8},{12,... | collective-permute-start | bytes 405512 | tf_op jit(solution)/shard_map/ppermute | solution.py:26
  16.2 5.9 %collective-permute-start.5 = (bf16[16,4224]{1,0:T(8,128)(2,1)S(1)}, bf16[16,4224]{1,0:T(8,128)(2,1)S(1)}, u32[]{:S(2)}, u32[]{:S(2)}) collective-permute-start(bf16[16,4224]{1,0:T(8,128)(2,1)S(1)} %collective-permute-done.2.refs_2_), channel_id=1, source_target_pairs={{0,1},{1,0},{2,3},{3,2},{4,5},{5,4},{6,7},{7,6},{8,9},{9,8},{10,11... | collective-permute-start | bytes 405512 | tf_op jit(solution)/shard_map/ppermute | solution.py:26
  19.1 5.2 %collective-permute-start.6 = (bf16[16,4224]{1,0:T(8,128)(2,1)S(1)}, bf16[16,4224]{1,0:T(8,128)(2,1)S(1)}, u32[]{:S(2)}, u32[]{:S(2)}) collective-permute-start(bf16[16,4224]{1,0:T(8,128)(2,1)S(1)} %collective-permute-done.3.refs_3_), channel_id=1, source_target_pairs={{0,1},{1,0},{2,3},{3,2},{4,5},{5,4},{6,7},{7,6},{8,9},{9,8},{10,11... | collective-permute-start | bytes 405512 | tf_op jit(solution)/shard_map/ppermute | solution.py:26
  24.3 26.4 %copy-start = (bf16[128,512]{1,0:T(8,128)(2,1)S(1)}, bf16[128,512]{1,0:T(8,128)(2,1)}, u32[]{:S(2)}) copy-start(bf16[128,512]{1,0:T(8,128)(2,1)} %join.1.refs_0_) | copy-start | bytes 393220
  46.6 6.5 %collective-permute-start.7 = (bf16[16,4096]{1,0:T(8,128)(2,1)S(1)}, bf16[16,4096]{1,0:T(8,128)(2,1)S(1)}, u32[]{:S(2)}, u32[]{:S(2)}) collective-permute-start(bf16[16,4096]{1,0:T(8,128)(2,1)S(1)} %get-tuple-element.63), channel_id=1, source_target_pairs={{0,1},{1,0},{2,3},{3,2},{4,5},{5,4},{6,7},{7,6},{8,9},{9,8},{10,11... | collective-permute-start | bytes 393224 | tf_op jit(solution)/shard_map/ppermute | solution.py:26
  48.5 7.4 %collective-permute-start.8 = (bf16[16,4096]{1,0:T(8,128)(2,1)S(1)}, bf16[16,4096]{1,0:T(8,128)(2,1)S(1)}, u32[]{:S(2)}, u32[]{:S(2)}) collective-permute-start(bf16[16,4096]{1,0:T(8,128)(2,1)S(1)} %get-tuple-element.65), channel_id=1, source_target_pairs={{0,1},{1,0},{2,3},{3,2},{4,5},{5,4},{6,7},{7,6},{8,9},{9,8},{10,11... | collective-permute-start | bytes 393224 | tf_op jit(solution)/shard_map/ppermute | solution.py:26
  48.7 9.2 %collective-permute-start.12 = (bf16[16,4096]{1,0:T(8,128)(2,1)S(1)}, bf16[16,4096]{1,0:T(8,128)(2,1)S(1)}, u32[]{:S(2)}, u32[]{:S(2)}) collective-permute-start(bf16[16,4096]{1,0:T(8,128)(2,1)S(1)} %get-tuple-element.70), channel_id=1, source_target_pairs={{0,1},{1,0},{2,3},{3,2},{4,5},{5,4},{6,7},{7,6},{8,9},{9,8},{10,11... | collective-permute-start | bytes 393224 | tf_op jit(solution)/shard_map/ppermute | solution.py:26
  50.5 14.7 %collective-permute-start.16 = (bf16[16,4096]{1,0:T(8,128)(2,1)S(1)}, bf16[16,4096]{1,0:T(8,128)(2,1)S(1)}, u32[]{:S(2)}, u32[]{:S(2)}) collective-permute-start(bf16[16,4096]{1,0:T(8,128)(2,1)S(1)} %get-tuple-element.76), channel_id=1, source_target_pairs={{0,1},{1,0},{2,3},{3,2},{4,5},{5,4},{6,7},{7,6},{8,9},{9,8},{10,11... | collective-permute-start | bytes 393224 | tf_op jit(solution)/shard_map/ppermute | solution.py:26
  50.7 5.2 %collective-permute-start.9 = (bf16[128,512]{1,0:T(8,128)(2,1)S(1)}, bf16[128,512]{1,0:T(8,128)(2,1)S(1)}, u32[]{:S(2)}, u32[]{:S(2)}) collective-permute-start(bf16[128,512]{1,0:T(8,128)(2,1)S(1)} %copy-done), channel_id=1, source_target_pairs={{0,16},{8,24},{16,0},{24,8},{1,17},{9,25},{17,1},{25,9},{2,18},{10... | collective-permute-start | bytes 393224 | tf_op jit(solution)/shard_map/ppermute | solution.py:26
  53.1 6.4 %collective-permute-start.11 = (bf16[16,4096]{1,0:T(8,128)(2,1)S(1)}, bf16[16,4096]{1,0:T(8,128)(2,1)S(1)}, u32[]{:S(2)}, u32[]{:S(2)}) collective-permute-start(bf16[16,4096]{1,0:T(8,128)(2,1)S(1)} %add_convert_fusion.3), channel_id=1, source_target_pairs={{0,2},{2,0},{4,6},{6,4},{1,3},{3,1},{5,7},{7,5},{8,10},{10,8},{12,... | collective-permute-start | bytes 393224 | tf_op jit(solution)/shard_map/ppermute | solution.py:26
  55.9 5.7 %copy-start.1 = (bf16[128,512]{1,0:T(8,128)(2,1)}, bf16[128,512]{1,0:T(8,128)(2,1)S(1)}, u32[]{:S(2)}) copy-start(bf16[128,512]{1,0:T(8,128)(2,1)S(1)} %collective-permute-done.9.refs_1_) | copy-start | bytes 393220
  55.9 3.6 %collective-permute-start.13 = (bf16[128,512]{1,0:T(8,128)(2,1)S(1)}, bf16[128,512]{1,0:T(8,128)(2,1)S(1)}, u32[]{:S(2)}, u32[]{:S(2)}) collective-permute-start(bf16[128,512]{1,0:T(8,128)(2,1)S(1)} %copy-done), channel_id=1, source_target_pairs={{0,8},{8,0},{16,24},{24,16},{1,9},{9,1},{17,25},{25,17},{2,10},{10... | collective-permute-start | bytes 393224 | tf_op jit(solution)/shard_map/ppermute | solution.py:26
  55.9 3.6 %collective-permute-start.14 = (bf16[128,512]{1,0:T(8,128)(2,1)S(1)}, bf16[128,512]{1,0:T(8,128)(2,1)S(1)}, u32[]{:S(2)}, u32[]{:S(2)}) collective-permute-start(bf16[128,512]{1,0:T(8,128)(2,1)S(1)} %collective-permute-done.9.refs_1_), channel_id=1, source_target_pairs={{0,8},{8,0},{16,24},{24,16},{1,9},{9,1},{17,25},{25,17},{2,10},{10... | collective-permute-start | bytes 393224 | tf_op jit(solution)/shard_map/ppermute | solution.py:26
  57.9 7.3 %collective-permute-start.10 = (bf16[16,4096]{1,0:T(8,128)(2,1)S(1)}, bf16[16,4096]{1,0:T(8,128)(2,1)S(1)}, u32[]{:S(2)}, u32[]{:S(2)}) collective-permute-start(bf16[16,4096]{1,0:T(8,128)(2,1)S(1)} %add_convert_fusion.2), channel_id=1, source_target_pairs={{0,2},{2,0},{4,6},{6,4},{1,3},{3,1},{5,7},{7,5},{8,10},{10,8},{12,... | collective-permute-start | bytes 393224 | tf_op jit(solution)/shard_map/ppermute | solution.py:26
  59.5 2.1 %copy-start.2 = (bf16[128,512]{1,0:T(8,128)(2,1)}, bf16[128,512]{1,0:T(8,128)(2,1)S(1)}, u32[]{:S(2)}) copy-start(bf16[128,512]{1,0:T(8,128)(2,1)S(1)} %collective-permute-done.13.refs_2_) | copy-start | bytes 393220
  59.5 2.1 %copy-start.3 = (bf16[128,512]{1,0:T(8,128)(2,1)}, bf16[128,512]{1,0:T(8,128)(2,1)S(1)}, u32[]{:S(2)}) copy-start(bf16[128,512]{1,0:T(8,128)(2,1)S(1)} %collective-permute-done.14.refs_3_) | copy-start | bytes 393220
  59.6 7.8 %collective-permute-start.15 = (bf16[16,4096]{1,0:T(8,128)(2,1)S(1)}, bf16[16,4096]{1,0:T(8,128)(2,1)S(1)}, u32[]{:S(2)}, u32[]{:S(2)}) collective-permute-start(bf16[16,4096]{1,0:T(8,128)(2,1)S(1)} %add_convert_fusion.1), channel_id=1, source_target_pairs={{0,4},{2,6},{4,0},{6,2},{1,5},{3,7},{5,1},{7,3},{8,12},{10,14},{12... | collective-permute-start | bytes 393224 | tf_op jit(solution)/shard_map/ppermute | solution.py:26

commit v7 on v6

--- a/solution.py
+++ b/solution.py
@@ -49,7 +49,7 @@
         in_specs=[VMEM] * 4,
         out_specs=[VMEM] * 2,
         out_shape=[
-            jax.ShapeDtypeStruct((rows, 2 * (width + EXPERTS)), BF16),
+            pltpu.VMEM((rows, 2 * (width + EXPERTS)), BF16),
             pltpu.VMEM((rows, 2 * (width + EXPERTS)), BF16),
         ],
         name="pack_rows",
@@ -142,7 +142,7 @@
     pieces = refs[:count]
     weights = refs[count : count + 3]
     outs = refs[count + 3 : 2 * count + 3]
-    held, sems, tokens_scr, gates_scr, rows_scr, back_scr, scale_scr, pick_scr = refs[
+    held, sems, rows_scr, back_scr, scale_scr, pick_scr = refs[
         2 * count + 3 :
     ]
     gate_scr, up_scr, down_scr = held
@@ -159,10 +159,8 @@
         for which in range(3):
             copy(which, e).start()
 
-    for p in range(count):
-        tokens_scr[p * piece : (p + 1) * piece] = pieces[p][:, :both]
-        gates_scr[p * piece : (p + 1) * piece] = pieces[p][:, both:]
-    picks, scales = routing_rows(shard_ref[0], gates_scr[...], local, slots)
+    gates = jnp.concatenate([r[:, both:] for r in pieces], axis=0)
+    picks, scales = routing_rows(shard_ref[0], gates, local, slots)
     scale_scr[...] = jnp.broadcast_to(scales, scale_scr.shape)
     high = scales.astype(BF16).astype(F32)
     for i, part in enumerate((picks, picks * high, picks * (scales - high))):
@@ -171,7 +169,9 @@
     chunk = 512
     for c in range(0, both, chunk):
         rows_scr[:, c : c + chunk] = jnp.dot(
-            picks, tokens_scr[:, c : c + chunk], preferred_element_type=F32
+            picks,
+            jnp.concatenate([r[:, c : c + chunk] for r in pieces], axis=0),
+            preferred_element_type=F32,
         ).astype(BF16)
 
     unroll = 2 if local % 2 == 0 else 1
@@ -237,8 +237,6 @@
     scratch = [
         tuple(pltpu.VMEM(w.shape, BF16) for w in (w_gate, w_up, w_down)),
         pltpu.SemaphoreType.DMA((3, local)),
-        pltpu.VMEM((tokens, 2 * width), BF16),
-        pltpu.VMEM((tokens, pieces[0].shape[1] - 2 * width), BF16),
         pltpu.VMEM((local * slots, 2 * width), BF16),
         pltpu.VMEM((local * slots, 2 * width), BF16),
         pltpu.VMEM((local * slots, 128), F32),

time: 68.4 us -> 67.5 us (0.987)
  Pallas kernels: 29.1 us -> 28.4 us
  transfers between devices with their start and end apart: 17 -> 17, of which waited for: 9 -> 9; matrix products, arithmetic and copies ran while one was open for 1% -> 1% of each run, Pallas kernels for 7% -> 8%
where the time goes in v7:
time: 67.5 us; the launch traced here: 67.3 us
  Pallas kernels  28.4 us (42%)
  starting transfers between devices  21.7 us (32%)
  waiting for transfers between devices  15 us (22%)
  other arithmetic  0.8 us (1%)
  between operations  0.7 us (1%)
  local copies, waits for them, and re-layouts  0.68 us (1%)
    pallas_call x1, Pallas kernels, experts(): pl.pallas_call(functools.partial(experts_kernel, count=count, slots=slots...  22.3 us
    ppermute x17, starting transfers between devices, swap(): return lax.ppermute(array, axis, [(i, i ^ offset) for i in range(count)])  21.7 us
    ppermute x17, waiting for transfers between devices, swap(): return lax.ppermute(array, axis, [(i, i ^ offset) for i in range(count)])  15 us
    pallas_call x1, Pallas kernels, attend(): pl.pallas_call(attention_kernel, in_specs=[SMEM] + [VMEM] * (1 + len(kv))...  3.55 us
    pallas_call x1, Pallas kernels, join(): pl.pallas_call(join_kernel, in_specs=[VMEM] * 2, out_specs=VMEM, out_shap...  1.53 us
  transfers between devices with their start and end apart: 17, of which 9 were waited for; matrix products, arithmetic and copies ran while one was open for 1% of the time, Pallas kernels for 8%

profile of v7, /device:TPU:0, one launch (start us, length us, event | category | flops | bytes accessed | tf_op | source)
XLA Modules:
  0.0 67.3 jit_solution(5222225844395626154)
XLA Ops:
  0.6 1.0 %pack_rows.1 = (bf16[16,4224]{1,0:T(8,128)(2,1)S(1)}, bf16[16,4224]{1,0:T(8,128)(2,1)S(1)}) custom-call(s32[8,16]{1,0:T(8,128)} %bitcast.25, f32[8,16]{1,0:T(8,128)} %bitcast.26, bf16[16,2048]{1,0:T(8,128)(2,1)} %bitcast.21, bf16[16,2048]{1,0:T(8,128)(2,1)} %bitcast.22), custom_call_target="tpu_custom_call" | custom-call | tf_op jit(solution)/shard_map/pack_rows/pallas_call | solution.py:47
  1.6 4.1 %collective-permute-start.2 = (bf16[16,4224]{1,0:T(8,128)(2,1)S(1)}, bf16[16,4224]{1,0:T(8,128)(2,1)S(1)}, u32[]{:S(2)}, u32[]{:S(2)}) collective-permute-start(bf16[16,4224]{1,0:T(8,128)(2,1)S(1)} %get-tuple-element.47), channel_id=1, source_target_pairs={{0,4},{2,6},{4,0},{6,2},{1,5},{3,7},{5,1},{7,3},{8,12},{10,14},{12... | collective-permute-start | bytes 405512 | tf_op jit(solution)/shard_map/ppermute | solution.py:26
  5.7 1.5 %join.1.refs_0_ = bf16[128,512]{1,0:T(8,128)(2,1)} custom-call(bf16[128,256]{1,0:T(8,128)(2,1)} %bitcast.23, bf16[128,256]{1,0:T(8,128)(2,1)} %bitcast.24), custom_call_target="tpu_custom_call" | custom-call | bytes 10000000 | tf_op jit(solution)/shard_map/join/pallas_call | solution.py:67
  7.2 1.5 %collective-permute-start = (bf16[16,4224]{1,0:T(8,128)(2,1)S(1)}, bf16[16,4224]{1,0:T(8,128)(2,1)S(1)}, u32[]{:S(2)}, u32[]{:S(2)}) collective-permute-start(bf16[16,4224]{1,0:T(8,128)(2,1)S(1)} %get-tuple-element.47), channel_id=1, source_target_pairs={{0,1},{1,0},{2,3},{3,2},{4,5},{5,4},{6,7},{7,6},{8,9},{9,8},{10,11... | collective-permute-start | bytes 405512 | tf_op jit(solution)/shard_map/ppermute | solution.py:26
  8.7 1.6 %collective-permute-start.1 = (bf16[16,4224]{1,0:T(8,128)(2,1)S(1)}, bf16[16,4224]{1,0:T(8,128)(2,1)S(1)}, u32[]{:S(2)}, u32[]{:S(2)}) collective-permute-start(bf16[16,4224]{1,0:T(8,128)(2,1)S(1)} %get-tuple-element.47), channel_id=1, source_target_pairs={{0,2},{2,0},{4,6},{6,4},{1,3},{3,1},{5,7},{7,5},{8,10},{10,8},{12,... | collective-permute-start | bytes 405512 | tf_op jit(solution)/shard_map/ppermute | solution.py:26
  10.3 2.0 %collective-permute-done.2.refs_2_ = bf16[16,4224]{1,0:T(8,128)(2,1)S(1)} collective-permute-done((bf16[16,4224]{1,0:T(8,128)(2,1)S(1)}, bf16[16,4224]{1,0:T(8,128)(2,1)S(1)}, u32[]{:S(2)}, u32[]{:S(2)}) %collective-permute-start.2) | collective-permute-done | bytes 135200 | tf_op jit(solution)/shard_map/ppermute | solution.py:26
  12.3 0.7 collective-permute-start.3
  12.9 0.0 collective-permute-done.refs_4_
  12.9 2.3 %collective-permute-done.1.refs_1_ = bf16[16,4224]{1,0:T(8,128)(2,1)S(1)} collective-permute-done((bf16[16,4224]{1,0:T(8,128)(2,1)S(1)}, bf16[16,4224]{1,0:T(8,128)(2,1)S(1)}, u32[]{:S(2)}, u32[]{:S(2)}) %collective-permute-start.1) | collective-permute-done | bytes 135200 | tf_op jit(solution)/shard_map/ppermute | solution.py:26
  15.2 0.1 collective-permute-start.4
  15.3 0.7 collective-permute-start.5
  16.0 2.2 %collective-permute-done.3.refs_3_ = bf16[16,4224]{1,0:T(8,128)(2,1)S(1)} collective-permute-done((bf16[16,4224]{1,0:T(8,128)(2,1)S(1)}, bf16[16,4224]{1,0:T(8,128)(2,1)S(1)}, u32[]{:S(2)}, u32[]{:S(2)}) %collective-permute-start.3) | collective-permute-done | bytes 135200 | tf_op jit(solution)/shard_map/ppermute | solution.py:26
  18.2 2.0 %collective-permute-start.6 = (bf16[16,4224]{1,0:T(8,128)(2,1)S(1)}, bf16[16,4224]{1,0:T(8,128)(2,1)S(1)}, u32[]{:S(2)}, u32[]{:S(2)}) collective-permute-start(bf16[16,4224]{1,0:T(8,128)(2,1)S(1)} %collective-permute-done.3.refs_3_), channel_id=1, source_target_pairs={{0,1},{1,0},{2,3},{3,2},{4,5},{5,4},{6,7},{7,6},{8,9},{9,8},{10,11... | collective-permute-start | bytes 405512 | tf_op jit(solution)/shard_map/ppermute | solution.py:26
  20.2 1.0 %collective-permute-done.5.refs_6_ = bf16[16,4224]{1,0:T(8,128)(2,1)S(1)} collective-permute-done((bf16[16,4224]{1,0:T(8,128)(2,1)S(1)}, bf16[16,4224]{1,0:T(8,128)(2,1)S(1)}, u32[]{:S(2)}, u32[]{:S(2)}) %collective-permute-start.5) | collective-permute-done | bytes 135200 | tf_op jit(solution)/shard_map/ppermute | solution.py:26
  21.3 0.0 collective-permute-done.4.refs_5_
  21.3 2.2 %collective-permute-done.6.refs_7_ = bf16[16,4224]{1,0:T(8,128)(2,1)S(1)} collective-permute-done((bf16[16,4224]{1,0:T(8,128)(2,1)S(1)}, bf16[16,4224]{1,0:T(8,128)(2,1)S(1)}, u32[]{:S(2)}, u32[]{:S(2)}) %collective-permute-start.6) | collective-permute-done | bytes 135200 | tf_op jit(solution)/shard_map/ppermute | solution.py:26
  23.4 0.0 copy-start
  23.4 22.3 %experts.1 = (bf16[16,4096]{1,0:T(8,128)(2,1)S(1)}, bf16[16,4096]{1,0:T(8,128)(2,1)S(1)}, bf16[16,4096]{1,0:T(8,128)(2,1)S(1)}, bf16[16,4096]{1,0:T(8,128)(2,1)S...) custom-call(s32[1]{0:T(128)} %bitcast.shard_ref, ...), custom_call_target="tpu_custom_call" | custom-call | flops 2415919104 | bytes 37748736 | tf_op jit(solution)/shard_map/experts/pallas_call | solution.py:246
  45.8 1.9 %collective-permute-start.7 = (bf16[16,4096]{1,0:T(8,128)(2,1)S(1)}, bf16[16,4096]{1,0:T(8,128)(2,1)S(1)}, u32[]{:S(2)}, u32[]{:S(2)}) collective-permute-start(bf16[16,4096]{1,0:T(8,128)(2,1)S(1)} %get-tuple-element.63), channel_id=1, source_target_pairs={{0,1},{1,0},{2,3},{3,2},{4,5},{5,4},{6,7},{7,6},{8,9},{9,8},{10,11... | collective-permute-start | bytes 393224 | tf_op jit(solution)/shard_map/ppermute | solution.py:26
  47.6 0.2 collective-permute-start.8
  47.9 1.8 %collective-permute-start.12 = (bf16[16,4096]{1,0:T(8,128)(2,1)S(1)}, bf16[16,4096]{1,0:T(8,128)(2,1)S(1)}, u32[]{:S(2)}, u32[]{:S(2)}) collective-permute-start(bf16[16,4096]{1,0:T(8,128)(2,1)S(1)} %get-tuple-element.70), channel_id=1, source_target_pairs={{0,1},{1,0},{2,3},{3,2},{4,5},{5,4},{6,7},{7,6},{8,9},{9,8},{10,11... | collective-permute-start | bytes 393224 | tf_op jit(solution)/shard_map/ppermute | solution.py:26
  49.7 0.2 collective-permute-start.16
  49.9 0.0 copy-done
  49.9 1.6 %collective-permute-start.9 = (bf16[128,512]{1,0:T(8,128)(2,1)S(1)}, bf16[128,512]{1,0:T(8,128)(2,1)S(1)}, u32[]{:S(2)}, u32[]{:S(2)}) collective-permute-start(bf16[128,512]{1,0:T(8,128)(2,1)S(1)} %copy-done), channel_id=1, source_target_pairs={{0,16},{8,24},{16,0},{24,8},{1,17},{9,25},{17,1},{25,9},{2,18},{10... | collective-permute-start | bytes 393224 | tf_op jit(solution)/shard_map/ppermute | solution.py:26
  51.5 0.8 %collective-permute-done.7 = bf16[16,4096]{1,0:T(8,128)(2,1)S(1)} collective-permute-done((bf16[16,4096]{1,0:T(8,128)(2,1)S(1)}, bf16[16,4096]{1,0:T(8,128)(2,1)S(1)}, u32[]{:S(2)}, u32[]{:S(2)}) %collective-permute-start.7) | collective-permute-done | bytes 131104 | tf_op jit(solution)/shard_map/ppermute | solution.py:26
  52.3 1.8 %collective-permute-start.11 = (bf16[16,4096]{1,0:T(8,128)(2,1)S(1)}, bf16[16,4096]{1,0:T(8,128)(2,1)S(1)}, u32[]{:S(2)}, u32[]{:S(2)}) collective-permute-start(bf16[16,4096]{1,0:T(8,128)(2,1)S(1)} %add_convert_fusion.3), channel_id=1, source_target_pairs={{0,2},{2,0},{4,6},{6,4},{1,3},{3,1},{5,7},{7,5},{8,10},{10,8},{12,... | collective-permute-start | bytes 393224 | tf_op jit(solution)/shard_map/ppermute | solution.py:26
  54.1 1.0 %collective-permute-done.8 = bf16[16,4096]{1,0:T(8,128)(2,1)S(1)} collective-permute-done((bf16[16,4096]{1,0:T(8,128)(2,1)S(1)}, bf16[16,4096]{1,0:T(8,128)(2,1)S(1)}, u32[]{:S(2)}, u32[]{:S(2)}) %collective-permute-start.8) | collective-permute-done | bytes 131104 | tf_op jit(solution)/shard_map/ppermute | solution.py:26
  55.1 0.0 collective-permute-done.9.refs_1_
  55.1 0.0 copy-start.1
  55.1 0.0 collective-permute-start.13
  55.1 0.5 collective-permute-start.14
  55.6 1.4 %collective-permute-done.12 = bf16[16,4096]{1,0:T(8,128)(2,1)S(1)} collective-permute-done((bf16[16,4096]{1,0:T(8,128)(2,1)S(1)}, bf16[16,4096]{1,0:T(8,128)(2,1)S(1)}, u32[]{:S(2)}, u32[]{:S(2)}) %collective-permute-start.12) | collective-permute-done | bytes 131104 | tf_op jit(solution)/shard_map/ppermute | solution.py:26
  57.1 1.6 %collective-permute-start.10 = (bf16[16,4096]{1,0:T(8,128)(2,1)S(1)}, bf16[16,4096]{1,0:T(8,128)(2,1)S(1)}, u32[]{:S(2)}, u32[]{:S(2)}) collective-permute-start(bf16[16,4096]{1,0:T(8,128)(2,1)S(1)} %add_convert_fusion.2), channel_id=1, source_target_pairs={{0,2},{2,0},{4,6},{6,4},{1,3},{3,1},{5,7},{7,5},{8,10},{10,8},{12,... | collective-permute-start | bytes 393224 | tf_op jit(solution)/shard_map/ppermute | solution.py:26
  58.6 0.0 collective-permute-done.11
  58.6 0.0 collective-permute-done.13.refs_2_
  58.6 0.0 copy-start.2
  58.6 0.0 collective-permute-done.14.refs_3_
  58.6 0.0 copy-start.3
  58.6 0.1 add_convert_fusion.1
  58.7 1.5 %collective-permute-start.15 = (bf16[16,4096]{1,0:T(8,128)(2,1)S(1)}, bf16[16,4096]{1,0:T(8,128)(2,1)S(1)}, u32[]{:S(2)}, u32[]{:S(2)}) collective-permute-start(bf16[16,4096]{1,0:T(8,128)(2,1)S(1)} %add_convert_fusion.1), channel_id=1, source_target_pairs={{0,4},{2,6},{4,0},{6,2},{1,5},{3,7},{5,1},{7,3},{8,12},{10,14},{12... | collective-permute-start | bytes 393224 | tf_op jit(solution)/shard_map/ppermute | solution.py:26
  60.2 0.6 pad_add_fusion.base_ref
  60.8 0.0 copy-done.1
  60.8 0.0 copy-done.2
  60.8 0.0 copy-done.3
  60.8 3.6 %attention.1 = bf16[128,2048]{1,0:T(8,128)(2,1)} custom-call(s32[4]{0:T(128)} %pad_add_fusion.base_ref, bf16[128,2048]{1,0:T(8,128)(2,1)} %bitcast.27, bf16[128,512]{1,0:T(8,128)(2,1)} %join.1.refs_0_, bf16[128,512]{1,0:T(8,128)(2,1)} %copy-done.1, bf16[128,512]{1,0:T(8,128)(2,1)} %copy-done.2, bf16[128,512]{1,0:T(8,128)(2,1)} %copy-done.3), custom_call_target="tpu_custom_call" | custom-call | flops 536870912 | bytes 1048576 | tf_op jit(solution)/shard_map/attention/pallas_call | solution.py:110
  64.3 0.0 collective-permute-done.16
  64.3 0.0 collective-permute-done.10
  64.4 2.2 %collective-permute-done.15 = bf16[16,4096]{1,0:T(8,128)(2,1)S(1)} collective-permute-done((bf16[16,4096]{1,0:T(8,128)(2,1)S(1)}, bf16[16,4096]{1,0:T(8,128)(2,1)S(1)}, u32[]{:S(2)}, u32[]{:S(2)}) %collective-permute-start.15) | collective-permute-done | bytes 131104 | tf_op jit(solution)/shard_map/ppermute | solution.py:26
  66.5 0.1 add_convert_fusion
  66.6 0.7 slice_bitcast_fusion
  (2 shorter events, 0.1 us)
Async XLA Ops:
  1.6 10.7 %collective-permute-start.2 = (bf16[16,4224]{1,0:T(8,128)(2,1)S(1)}, bf16[16,4224]{1,0:T(8,128)(2,1)S(1)}, u32[]{:S(2)}, u32[]{:S(2)}) collective-permute-start(bf16[16,4224]{1,0:T(8,128)(2,1)S(1)} %get-tuple-element.47), channel_id=1, source_target_pairs={{0,4},{2,6},{4,0},{6,2},{1,5},{3,7},{5,1},{7,3},{8,12},{10,14},{12... | collective-permute-start | bytes 405512 | tf_op jit(solution)/shard_map/ppermute | solution.py:26
  7.2 5.7 %collective-permute-start = (bf16[16,4224]{1,0:T(8,128)(2,1)S(1)}, bf16[16,4224]{1,0:T(8,128)(2,1)S(1)}, u32[]{:S(2)}, u32[]{:S(2)}) collective-permute-start(bf16[16,4224]{1,0:T(8,128)(2,1)S(1)} %get-tuple-element.47), channel_id=1, source_target_pairs={{0,1},{1,0},{2,3},{3,2},{4,5},{5,4},{6,7},{7,6},{8,9},{9,8},{10,11... | collective-permute-start | bytes 405512 | tf_op jit(solution)/shard_map/ppermute | solution.py:26
  8.7 6.5 %collective-permute-start.1 = (bf16[16,4224]{1,0:T(8,128)(2,1)S(1)}, bf16[16,4224]{1,0:T(8,128)(2,1)S(1)}, u32[]{:S(2)}, u32[]{:S(2)}) collective-permute-start(bf16[16,4224]{1,0:T(8,128)(2,1)S(1)} %get-tuple-element.47), channel_id=1, source_target_pairs={{0,2},{2,0},{4,6},{6,4},{1,3},{3,1},{5,7},{7,5},{8,10},{10,8},{12,... | collective-permute-start | bytes 405512 | tf_op jit(solution)/shard_map/ppermute | solution.py:26
  12.3 5.9 %collective-permute-start.3 = (bf16[16,4224]{1,0:T(8,128)(2,1)S(1)}, bf16[16,4224]{1,0:T(8,128)(2,1)S(1)}, u32[]{:S(2)}, u32[]{:S(2)}) collective-permute-start(bf16[16,4224]{1,0:T(8,128)(2,1)S(1)} %collective-permute-done.2.refs_2_), channel_id=1, source_target_pairs={{0,2},{2,0},{4,6},{6,4},{1,3},{3,1},{5,7},{7,5},{8,10},{10,8},{12,... | collective-permute-start | bytes 405512 | tf_op jit(solution)/shard_map/ppermute | solution.py:26
  15.2 6.1 %collective-permute-start.4 = (bf16[16,4224]{1,0:T(8,128)(2,1)S(1)}, bf16[16,4224]{1,0:T(8,128)(2,1)S(1)}, u32[]{:S(2)}, u32[]{:S(2)}) collective-permute-start(bf16[16,4224]{1,0:T(8,128)(2,1)S(1)} %collective-permute-done.refs_4_), channel_id=1, source_target_pairs={{0,2},{2,0},{4,6},{6,4},{1,3},{3,1},{5,7},{7,5},{8,10},{10,8},{12,... | collective-permute-start | bytes 405512 | tf_op jit(solution)/shard_map/ppermute | solution.py:26
  15.3 5.9 %collective-permute-start.5 = (bf16[16,4224]{1,0:T(8,128)(2,1)S(1)}, bf16[16,4224]{1,0:T(8,128)(2,1)S(1)}, u32[]{:S(2)}, u32[]{:S(2)}) collective-permute-start(bf16[16,4224]{1,0:T(8,128)(2,1)S(1)} %collective-permute-done.2.refs_2_), channel_id=1, source_target_pairs={{0,1},{1,0},{2,3},{3,2},{4,5},{5,4},{6,7},{7,6},{8,9},{9,8},{10,11... | collective-permute-start | bytes 405512 | tf_op jit(solution)/shard_map/ppermute | solution.py:26
  18.2 5.2 %collective-permute-start.6 = (bf16[16,4224]{1,0:T(8,128)(2,1)S(1)}, bf16[16,4224]{1,0:T(8,128)(2,1)S(1)}, u32[]{:S(2)}, u32[]{:S(2)}) collective-permute-start(bf16[16,4224]{1,0:T(8,128)(2,1)S(1)} %collective-permute-done.3.refs_3_), channel_id=1, source_target_pairs={{0,1},{1,0},{2,3},{3,2},{4,5},{5,4},{6,7},{7,6},{8,9},{9,8},{10,11... | collective-permute-start | bytes 405512 | tf_op jit(solution)/shard_map/ppermute | solution.py:26
  23.4 26.5 %copy-start = (bf16[128,512]{1,0:T(8,128)(2,1)S(1)}, bf16[128,512]{1,0:T(8,128)(2,1)}, u32[]{:S(2)}) copy-start(bf16[128,512]{1,0:T(8,128)(2,1)} %join.1.refs_0_) | copy-start | bytes 393220
  45.8 6.5 %collective-permute-start.7 = (bf16[16,4096]{1,0:T(8,128)(2,1)S(1)}, bf16[16,4096]{1,0:T(8,128)(2,1)S(1)}, u32[]{:S(2)}, u32[]{:S(2)}) collective-permute-start(bf16[16,4096]{1,0:T(8,128)(2,1)S(1)} %get-tuple-element.63), channel_id=1, source_target_pairs={{0,1},{1,0},{2,3},{3,2},{4,5},{5,4},{6,7},{7,6},{8,9},{9,8},{10,11... | collective-permute-start | bytes 393224 | tf_op jit(solution)/shard_map/ppermute | solution.py:26
  47.6 7.5 %collective-permute-start.8 = (bf16[16,4096]{1,0:T(8,128)(2,1)S(1)}, bf16[16,4096]{1,0:T(8,128)(2,1)S(1)}, u32[]{:S(2)}, u32[]{:S(2)}) collective-permute-start(bf16[16,4096]{1,0:T(8,128)(2,1)S(1)} %get-tuple-element.65), channel_id=1, source_target_pairs={{0,1},{1,0},{2,3},{3,2},{4,5},{5,4},{6,7},{7,6},{8,9},{9,8},{10,11... | collective-permute-start | bytes 393224 | tf_op jit(solution)/shard_map/ppermute | solution.py:26
  47.9 9.2 %collective-permute-start.12 = (bf16[16,4096]{1,0:T(8,128)(2,1)S(1)}, bf16[16,4096]{1,0:T(8,128)(2,1)S(1)}, u32[]{:S(2)}, u32[]{:S(2)}) collective-permute-start(bf16[16,4096]{1,0:T(8,128)(2,1)S(1)} %get-tuple-element.70), channel_id=1, source_target_pairs={{0,1},{1,0},{2,3},{3,2},{4,5},{5,4},{6,7},{7,6},{8,9},{9,8},{10,11... | collective-permute-start | bytes 393224 | tf_op jit(solution)/shard_map/ppermute | solution.py:26
  49.7 14.7 %collective-permute-start.16 = (bf16[16,4096]{1,0:T(8,128)(2,1)S(1)}, bf16[16,4096]{1,0:T(8,128)(2,1)S(1)}, u32[]{:S(2)}, u32[]{:S(2)}) collective-permute-start(bf16[16,4096]{1,0:T(8,128)(2,1)S(1)} %get-tuple-element.76), channel_id=1, source_target_pairs={{0,1},{1,0},{2,3},{3,2},{4,5},{5,4},{6,7},{7,6},{8,9},{9,8},{10,11... | collective-permute-start | bytes 393224 | tf_op jit(solution)/shard_map/ppermute | solution.py:26
  49.9 5.2 %collective-permute-start.9 = (bf16[128,512]{1,0:T(8,128)(2,1)S(1)}, bf16[128,512]{1,0:T(8,128)(2,1)S(1)}, u32[]{:S(2)}, u32[]{:S(2)}) collective-permute-start(bf16[128,512]{1,0:T(8,128)(2,1)S(1)} %copy-done), channel_id=1, source_target_pairs={{0,16},{8,24},{16,0},{24,8},{1,17},{9,25},{17,1},{25,9},{2,18},{10... | collective-permute-start | bytes 393224 | tf_op jit(solution)/shard_map/ppermute | solution.py:26
  52.3 6.3 %collective-permute-start.11 = (bf16[16,4096]{1,0:T(8,128)(2,1)S(1)}, bf16[16,4096]{1,0:T(8,128)(2,1)S(1)}, u32[]{:S(2)}, u32[]{:S(2)}) collective-permute-start(bf16[16,4096]{1,0:T(8,128)(2,1)S(1)} %add_convert_fusion.3), channel_id=1, source_target_pairs={{0,2},{2,0},{4,6},{6,4},{1,3},{3,1},{5,7},{7,5},{8,10},{10,8},{12,... | collective-permute-start | bytes 393224 | tf_op jit(solution)/shard_map/ppermute | solution.py:26
  55.1 5.7 %copy-start.1 = (bf16[128,512]{1,0:T(8,128)(2,1)}, bf16[128,512]{1,0:T(8,128)(2,1)S(1)}, u32[]{:S(2)}) copy-start(bf16[128,512]{1,0:T(8,128)(2,1)S(1)} %collective-permute-done.9.refs_1_) | copy-start | bytes 393220
  55.1 3.5 %collective-permute-start.13 = (bf16[128,512]{1,0:T(8,128)(2,1)S(1)}, bf16[128,512]{1,0:T(8,128)(2,1)S(1)}, u32[]{:S(2)}, u32[]{:S(2)}) collective-permute-start(bf16[128,512]{1,0:T(8,128)(2,1)S(1)} %copy-done), channel_id=1, source_target_pairs={{0,8},{8,0},{16,24},{24,16},{1,9},{9,1},{17,25},{25,17},{2,10},{10... | collective-permute-start | bytes 393224 | tf_op jit(solution)/shard_map/ppermute | solution.py:26
  55.1 3.5 %collective-permute-start.14 = (bf16[128,512]{1,0:T(8,128)(2,1)S(1)}, bf16[128,512]{1,0:T(8,128)(2,1)S(1)}, u32[]{:S(2)}, u32[]{:S(2)}) collective-permute-start(bf16[128,512]{1,0:T(8,128)(2,1)S(1)} %collective-permute-done.9.refs_1_), channel_id=1, source_target_pairs={{0,8},{8,0},{16,24},{24,16},{1,9},{9,1},{17,25},{25,17},{2,10},{10... | collective-permute-start | bytes 393224 | tf_op jit(solution)/shard_map/ppermute | solution.py:26
  57.1 7.3 %collective-permute-start.10 = (bf16[16,4096]{1,0:T(8,128)(2,1)S(1)}, bf16[16,4096]{1,0:T(8,128)(2,1)S(1)}, u32[]{:S(2)}, u32[]{:S(2)}) collective-permute-start(bf16[16,4096]{1,0:T(8,128)(2,1)S(1)} %add_convert_fusion.2), channel_id=1, source_target_pairs={{0,2},{2,0},{4,6},{6,4},{1,3},{3,1},{5,7},{7,5},{8,10},{10,8},{12,... | collective-permute-start | bytes 393224 | tf_op jit(solution)/shard_map/ppermute | solution.py:26
  58.6 2.2 %copy-start.2 = (bf16[128,512]{1,0:T(8,128)(2,1)}, bf16[128,512]{1,0:T(8,128)(2,1)S(1)}, u32[]{:S(2)}) copy-start(bf16[128,512]{1,0:T(8,128)(2,1)S(1)} %collective-permute-done.13.refs_2_) | copy-start | bytes 393220
  58.6 2.2 %copy-start.3 = (bf16[128,512]{1,0:T(8,128)(2,1)}, bf16[128,512]{1,0:T(8,128)(2,1)S(1)}, u32[]{:S(2)}) copy-start(bf16[128,512]{1,0:T(8,128)(2,1)S(1)} %collective-permute-done.14.refs_3_) | copy-start | bytes 393220
  58.7 7.8 %collective-permute-start.15 = (bf16[16,4096]{1,0:T(8,128)(2,1)S(1)}, bf16[16,4096]{1,0:T(8,128)(2,1)S(1)}, u32[]{:S(2)}, u32[]{:S(2)}) collective-permute-start(bf16[16,4096]{1,0:T(8,128)(2,1)S(1)} %add_convert_fusion.1), channel_id=1, source_target_pairs={{0,4},{2,6},{4,0},{6,2},{1,5},{3,7},{5,1},{7,3},{8,12},{10,14},{12... | collective-permute-start | bytes 393224 | tf_op jit(solution)/shard_map/ppermute | solution.py:26

commit v8 on v7

--- a/solution.py
+++ b/solution.py
@@ -68,8 +68,8 @@
         join_kernel,
         in_specs=[VMEM] * 2,
         out_specs=VMEM,
-        out_shape=jax.ShapeDtypeStruct((rows, 2 * half), BF16),
-        cost_estimate=pl.CostEstimate(flops=0, bytes_accessed=10**7, transcendentals=0),
+        out_shape=pltpu.VMEM((rows, 2 * half), BF16),
+        cost_estimate=pl.CostEstimate(flops=0, bytes_accessed=8 * rows * half, transcendentals=0),
         name="join",
     )(keys, values)
 
@@ -269,11 +269,11 @@
 
 def spread(rows, beside):
     near, far = [rows], []
+    later, beside = lax.optimization_barrier((rows, beside))
     for d in range(1, lax.axis_size("seq")):
-        block = swap(near[parent(d)], "seq", d - parent(d))
+        block = swap(near[parent(d)] if d > 1 else later, "seq", d - parent(d))
         if d == 1:
-            rows, beside = lax.optimization_barrier((rows, beside))
-            far.append(over_tp(rows))
+            far.append(over_tp(later))
         elif d == 2:
             far[0], near[1] = lax.optimization_barrier((far[0], near[1]))
             far.append([swap(a, "seq", 1) for a in far[0]])
@@ -281,12 +281,12 @@
             far.append(over_tp(near[d - 1]))
             block, far[: d - 2] = lax.optimization_barrier((block, far[: d - 2]))
         near.append(block)
-    if len(near) == 2:
+    if len(near) == 1:
+        far.append(over_tp(later))
+    elif len(near) == 2:
         far.append([swap(a, "seq", 1) for a in far[0]])
-    elif len(near) > 2:
+    else:
         far.append(over_tp(near[-1]))
-    else:
-        far.append(over_tp(rows))
     return near + [a for blocks in zip(*far) for a in blocks], beside
 
 

time: 67.5 us -> 67.3 us (level)
  starting transfers between devices: 21.7 us -> 23 us
  waiting for transfers between devices: 15 us -> 14.2 us
  Pallas kernels: 28.4 us -> 27.7 us
    ppermute x17, starting transfers between devices: 21.7 us -> 23 us  [swap(): return lax.ppermute(array, axis, [(i, i ^ offset) for i in range(count)])]
    ppermute x17, waiting for transfers between devices: 15 us -> 14.2 us  [swap(): return lax.ppermute(array, axis, [(i, i ^ offset) for i in range(count)])]
  transfers between devices with their start and end apart: 17 -> 17, of which waited for: 9 -> 11; matrix products, arithmetic and copies ran while one was open for 1% -> 1% of each run, Pallas kernels for 8% -> 7%
where the time goes in v8:
time: 67.3 us; the launch traced here: 67.1 us
  Pallas kernels  27.7 us (41%)
  starting transfers between devices  23 us (34%)
  waiting for transfers between devices  14.2 us (21%)
  other arithmetic  0.8 us (1%)
  between operations  0.71 us (1%)
  local copies, waits for them, and re-layouts  0.68 us (1%)
    ppermute x17, starting transfers between devices, swap(): return lax.ppermute(array, axis, [(i, i ^ offset) for i in range(count)])  23 us
    pallas_call x1, Pallas kernels, experts(): pl.pallas_call(functools.partial(experts_kernel, count=count, slots=slots...  22.3 us
    ppermute x17, waiting for transfers between devices, swap(): return lax.ppermute(array, axis, [(i, i ^ offset) for i in range(count)])  14.2 us
    pallas_call x1, Pallas kernels, attend(): pl.pallas_call(attention_kernel, in_specs=[SMEM] + [VMEM] * (1 + len(kv))...  3.55 us
  transfers between devices with their start and end apart: 17, of which 11 were waited for; matrix products, arithmetic and copies ran while one was open for 1% of the time, Pallas kernels for 7%

profile of v8, /device:TPU:0, one launch (start us, length us, event | category | flops | bytes accessed | tf_op | source)
XLA Modules:
  0.0 67.1 jit_solution(11328655876389522262)
XLA Ops:
  0.6 1.0 %pack_rows.1 = (bf16[16,4224]{1,0:T(8,128)(2,1)S(1)}, bf16[16,4224]{1,0:T(8,128)(2,1)S(1)}) custom-call(s32[8,16]{1,0:T(8,128)} %bitcast.25, f32[8,16]{1,0:T(8,128)} %bitcast.26, bf16[16,2048]{1,0:T(8,128)(2,1)} %bitcast.21, bf16[16,2048]{1,0:T(8,128)(2,1)} %bitcast.22), custom_call_target="tpu_custom_call" | custom-call | tf_op jit(solution)/shard_map/pack_rows/pallas_call | solution.py:47
  1.6 4.1 %collective-permute-start.2 = (bf16[16,4224]{1,0:T(8,128)(2,1)S(1)}, bf16[16,4224]{1,0:T(8,128)(2,1)S(1)}, u32[]{:S(2)}, u32[]{:S(2)}) collective-permute-start(bf16[16,4224]{1,0:T(8,128)(2,1)S(1)} %get-tuple-element.47), channel_id=1, source_target_pairs={{0,4},{2,6},{4,0},{6,2},{1,5},{3,7},{5,1},{7,3},{8,12},{10,14},{12... | collective-permute-start | bytes 405512 | tf_op jit(solution)/shard_map/ppermute | solution.py:26
  5.7 0.9 %join.1.refs_0_ = bf16[128,512]{1,0:T(8,128)(2,1)S(1)} custom-call(bf16[128,256]{1,0:T(8,128)(2,1)} %bitcast.23, bf16[128,256]{1,0:T(8,128)(2,1)} %bitcast.24), custom_call_target="tpu_custom_call" | custom-call | bytes 262144 | tf_op jit(solution)/shard_map/join/pallas_call | solution.py:67
  6.6 0.0 copy-start
  6.6 1.6 %collective-permute-start.1 = (bf16[16,4224]{1,0:T(8,128)(2,1)S(1)}, bf16[16,4224]{1,0:T(8,128)(2,1)S(1)}, u32[]{:S(2)}, u32[]{:S(2)}) collective-permute-start(bf16[16,4224]{1,0:T(8,128)(2,1)S(1)} %get-tuple-element.47), channel_id=1, source_target_pairs={{0,2},{2,0},{4,6},{6,4},{1,3},{3,1},{5,7},{7,5},{8,10},{10,8},{12,... | collective-permute-start | bytes 405512 | tf_op jit(solution)/shard_map/ppermute | solution.py:26
  8.2 1.5 %collective-permute-start = (bf16[16,4224]{1,0:T(8,128)(2,1)S(1)}, bf16[16,4224]{1,0:T(8,128)(2,1)S(1)}, u32[]{:S(2)}, u32[]{:S(2)}) collective-permute-start(bf16[16,4224]{1,0:T(8,128)(2,1)S(1)} %get-tuple-element.47), channel_id=1, source_target_pairs={{0,1},{1,0},{2,3},{3,2},{4,5},{5,4},{6,7},{7,6},{8,9},{9,8},{10,11... | collective-permute-start | bytes 405512 | tf_op jit(solution)/shard_map/ppermute | solution.py:26
  9.7 2.5 %collective-permute-done.2.refs_2_ = bf16[16,4224]{1,0:T(8,128)(2,1)S(1)} collective-permute-done((bf16[16,4224]{1,0:T(8,128)(2,1)S(1)}, bf16[16,4224]{1,0:T(8,128)(2,1)S(1)}, u32[]{:S(2)}, u32[]{:S(2)}) %collective-permute-start.2) | collective-permute-done | bytes 135200 | tf_op jit(solution)/shard_map/ppermute | solution.py:26
  12.3 0.7 collective-permute-start.3
  12.9 0.5 collective-permute-done.1.refs_1_
  13.4 0.0 collective-permute-done.refs_4_
  13.4 0.9 %collective-permute-start.4 = (bf16[16,4224]{1,0:T(8,128)(2,1)S(1)}, bf16[16,4224]{1,0:T(8,128)(2,1)S(1)}, u32[]{:S(2)}, u32[]{:S(2)}) collective-permute-start(bf16[16,4224]{1,0:T(8,128)(2,1)S(1)} %collective-permute-done.refs_4_), channel_id=1, source_target_pairs={{0,2},{2,0},{4,6},{6,4},{1,3},{3,1},{5,7},{7,5},{8,10},{10,8},{12,... | collective-permute-start | bytes 405512 | tf_op jit(solution)/shard_map/ppermute | solution.py:26
  14.3 1.6 %collective-permute-start.5 = (bf16[16,4224]{1,0:T(8,128)(2,1)S(1)}, bf16[16,4224]{1,0:T(8,128)(2,1)S(1)}, u32[]{:S(2)}, u32[]{:S(2)}) collective-permute-start(bf16[16,4224]{1,0:T(8,128)(2,1)S(1)} %collective-permute-done.2.refs_2_), channel_id=1, source_target_pairs={{0,1},{1,0},{2,3},{3,2},{4,5},{5,4},{6,7},{7,6},{8,9},{9,8},{10,11... | collective-permute-start | bytes 405512 | tf_op jit(solution)/shard_map/ppermute | solution.py:26
  15.9 2.4 %collective-permute-done.3.refs_3_ = bf16[16,4224]{1,0:T(8,128)(2,1)S(1)} collective-permute-done((bf16[16,4224]{1,0:T(8,128)(2,1)S(1)}, bf16[16,4224]{1,0:T(8,128)(2,1)S(1)}, u32[]{:S(2)}, u32[]{:S(2)}) %collective-permute-start.3) | collective-permute-done | bytes 135200 | tf_op jit(solution)/shard_map/ppermute | solution.py:26
  18.2 1.5 %collective-permute-start.6 = (bf16[16,4224]{1,0:T(8,128)(2,1)S(1)}, bf16[16,4224]{1,0:T(8,128)(2,1)S(1)}, u32[]{:S(2)}, u32[]{:S(2)}) collective-permute-start(bf16[16,4224]{1,0:T(8,128)(2,1)S(1)} %collective-permute-done.3.refs_3_), channel_id=1, source_target_pairs={{0,1},{1,0},{2,3},{3,2},{4,5},{5,4},{6,7},{7,6},{8,9},{9,8},{10,11... | collective-permute-start | bytes 405512 | tf_op jit(solution)/shard_map/ppermute | solution.py:26
  19.7 0.0 collective-permute-done.4.refs_5_
  19.7 1.0 %collective-permute-done.5.refs_6_ = bf16[16,4224]{1,0:T(8,128)(2,1)S(1)} collective-permute-done((bf16[16,4224]{1,0:T(8,128)(2,1)S(1)}, bf16[16,4224]{1,0:T(8,128)(2,1)S(1)}, u32[]{:S(2)}, u32[]{:S(2)}) %collective-permute-start.5) | collective-permute-done | bytes 135200 | tf_op jit(solution)/shard_map/ppermute | solution.py:26
  20.7 2.6 %collective-permute-done.6.refs_7_ = bf16[16,4224]{1,0:T(8,128)(2,1)S(1)} collective-permute-done((bf16[16,4224]{1,0:T(8,128)(2,1)S(1)}, bf16[16,4224]{1,0:T(8,128)(2,1)S(1)}, u32[]{:S(2)}, u32[]{:S(2)}) %collective-permute-start.6) | collective-permute-done | bytes 135200 | tf_op jit(solution)/shard_map/ppermute | solution.py:26
  23.2 22.3 %experts.1 = (bf16[16,4096]{1,0:T(8,128)(2,1)S(1)}, bf16[16,4096]{1,0:T(8,128)(2,1)S(1)}, bf16[16,4096]{1,0:T(8,128)(2,1)S(1)}, bf16[16,4096]{1,0:T(8,128)(2,1)S...) custom-call(s32[1]{0:T(128)} %bitcast.shard_ref, ...), custom_call_target="tpu_custom_call" | custom-call | flops 2415919104 | bytes 37748736 | tf_op jit(solution)/shard_map/experts/pallas_call | solution.py:246
  45.6 1.5 %collective-permute-start.7 = (bf16[16,4096]{1,0:T(8,128)(2,1)S(1)}, bf16[16,4096]{1,0:T(8,128)(2,1)S(1)}, u32[]{:S(2)}, u32[]{:S(2)}) collective-permute-start(bf16[16,4096]{1,0:T(8,128)(2,1)S(1)} %get-tuple-element.63), channel_id=1, source_target_pairs={{0,1},{1,0},{2,3},{3,2},{4,5},{5,4},{6,7},{7,6},{8,9},{9,8},{10,11... | collective-permute-start | bytes 393224 | tf_op jit(solution)/shard_map/ppermute | solution.py:26
  47.1 0.6 collective-permute-start.8
  47.7 1.4 %collective-permute-start.12 = (bf16[16,4096]{1,0:T(8,128)(2,1)S(1)}, bf16[16,4096]{1,0:T(8,128)(2,1)S(1)}, u32[]{:S(2)}, u32[]{:S(2)}) collective-permute-start(bf16[16,4096]{1,0:T(8,128)(2,1)S(1)} %get-tuple-element.70), channel_id=1, source_target_pairs={{0,1},{1,0},{2,3},{3,2},{4,5},{5,4},{6,7},{7,6},{8,9},{9,8},{10,11... | collective-permute-start | bytes 393224 | tf_op jit(solution)/shard_map/ppermute | solution.py:26
  49.1 0.6 collective-permute-start.16
  49.7 1.4 %collective-permute-start.9 = (bf16[128,512]{1,0:T(8,128)(2,1)S(1)}, bf16[128,512]{1,0:T(8,128)(2,1)S(1)}, u32[]{:S(2)}, u32[]{:S(2)}) collective-permute-start(bf16[128,512]{1,0:T(8,128)(2,1)S(1)} %join.1.refs_0_), channel_id=1, source_target_pairs={{0,16},{8,24},{16,0},{24,8},{1,17},{9,25},{17,1},{25,9},{2,18},{10... | collective-permute-start | bytes 393224 | tf_op jit(solution)/shard_map/ppermute | solution.py:26
  51.1 0.9 %collective-permute-done.7 = bf16[16,4096]{1,0:T(8,128)(2,1)S(1)} collective-permute-done((bf16[16,4096]{1,0:T(8,128)(2,1)S(1)}, bf16[16,4096]{1,0:T(8,128)(2,1)S(1)}, u32[]{:S(2)}, u32[]{:S(2)}) %collective-permute-start.7) | collective-permute-done | bytes 131104 | tf_op jit(solution)/shard_map/ppermute | solution.py:26
  52.1 1.2 %collective-permute-start.11 = (bf16[16,4096]{1,0:T(8,128)(2,1)S(1)}, bf16[16,4096]{1,0:T(8,128)(2,1)S(1)}, u32[]{:S(2)}, u32[]{:S(2)}) collective-permute-start(bf16[16,4096]{1,0:T(8,128)(2,1)S(1)} %add_convert_fusion.3), channel_id=1, source_target_pairs={{0,2},{2,0},{4,6},{6,4},{1,3},{3,1},{5,7},{7,5},{8,10},{10,8},{12,... | collective-permute-start | bytes 393224 | tf_op jit(solution)/shard_map/ppermute | solution.py:26
  53.3 0.7 %collective-permute-done.8 = bf16[16,4096]{1,0:T(8,128)(2,1)S(1)} collective-permute-done((bf16[16,4096]{1,0:T(8,128)(2,1)S(1)}, bf16[16,4096]{1,0:T(8,128)(2,1)S(1)}, u32[]{:S(2)}, u32[]{:S(2)}) %collective-permute-start.8) | collective-permute-done | bytes 131104 | tf_op jit(solution)/shard_map/ppermute | solution.py:26
  54.1 0.6 collective-permute-done.9.refs_1_
  54.7 0.0 copy-done
  54.7 0.0 copy-start.1
  54.7 0.0 collective-permute-start.13
  54.7 0.5 collective-permute-start.14
  55.2 0.2 collective-permute-done.12
  55.5 1.1 %collective-permute-start.10 = (bf16[16,4096]{1,0:T(8,128)(2,1)S(1)}, bf16[16,4096]{1,0:T(8,128)(2,1)S(1)}, u32[]{:S(2)}, u32[]{:S(2)}) collective-permute-start(bf16[16,4096]{1,0:T(8,128)(2,1)S(1)} %add_convert_fusion.2), channel_id=1, source_target_pairs={{0,2},{2,0},{4,6},{6,4},{1,3},{3,1},{5,7},{7,5},{8,10},{10,8},{12,... | collective-permute-start | bytes 393224 | tf_op jit(solution)/shard_map/ppermute | solution.py:26
  56.5 0.6 collective-permute-done.11
  57.1 0.0 collective-permute-done.13.refs_2_
  57.1 0.0 copy-start.2
  57.1 0.0 collective-permute-done.14.refs_3_
  57.2 0.0 copy-start.3
  57.2 0.1 add_convert_fusion.1
  57.2 2.8 %collective-permute-start.15 = (bf16[16,4096]{1,0:T(8,128)(2,1)S(1)}, bf16[16,4096]{1,0:T(8,128)(2,1)S(1)}, u32[]{:S(2)}, u32[]{:S(2)}) collective-permute-start(bf16[16,4096]{1,0:T(8,128)(2,1)S(1)} %add_convert_fusion.1), channel_id=1, source_target_pairs={{0,4},{2,6},{4,0},{6,2},{1,5},{3,7},{5,1},{7,3},{8,12},{10,14},{12... | collective-permute-start | bytes 393224 | tf_op jit(solution)/shard_map/ppermute | solution.py:26
  60.0 0.6 pad_add_fusion.base_ref
  60.7 0.0 copy-done.1
  60.7 0.0 copy-done.2
  60.7 0.0 copy-done.3
  60.7 3.6 %attention.1 = bf16[128,2048]{1,0:T(8,128)(2,1)} custom-call(s32[4]{0:T(128)} %pad_add_fusion.base_ref, bf16[128,2048]{1,0:T(8,128)(2,1)} %bitcast.27, bf16[128,512]{1,0:T(8,128)(2,1)} %copy-done, bf16[128,512]{1,0:T(8,128)(2,1)} %copy-done.1, bf16[128,512]{1,0:T(8,128)(2,1)} %copy-done.2, bf16[128,512]{1,0:T(8,128)(2,1)} %copy-done.3), custom_call_target="tpu_custom_call" | custom-call | flops 536870912 | bytes 1048576 | tf_op jit(solution)/shard_map/attention/pallas_call | solution.py:110
  64.2 0.0 collective-permute-done.16
  64.2 0.0 collective-permute-done.10
  64.2 2.1 %collective-permute-done.15 = bf16[16,4096]{1,0:T(8,128)(2,1)S(1)} collective-permute-done((bf16[16,4096]{1,0:T(8,128)(2,1)S(1)}, bf16[16,4096]{1,0:T(8,128)(2,1)S(1)}, u32[]{:S(2)}, u32[]{:S(2)}) %collective-permute-start.15) | collective-permute-done | bytes 131104 | tf_op jit(solution)/shard_map/ppermute | solution.py:26
  66.3 0.1 add_convert_fusion
  66.4 0.7 slice_bitcast_fusion
  (2 shorter events, 0.1 us)
Async XLA Ops:
  1.6 10.7 %collective-permute-start.2 = (bf16[16,4224]{1,0:T(8,128)(2,1)S(1)}, bf16[16,4224]{1,0:T(8,128)(2,1)S(1)}, u32[]{:S(2)}, u32[]{:S(2)}) collective-permute-start(bf16[16,4224]{1,0:T(8,128)(2,1)S(1)} %get-tuple-element.47), channel_id=1, source_target_pairs={{0,4},{2,6},{4,0},{6,2},{1,5},{3,7},{5,1},{7,3},{8,12},{10,14},{12... | collective-permute-start | bytes 405512 | tf_op jit(solution)/shard_map/ppermute | solution.py:26
  6.6 48.1 %copy-start = (bf16[128,512]{1,0:T(8,128)(2,1)}, bf16[128,512]{1,0:T(8,128)(2,1)S(1)}, u32[]{:S(2)}) copy-start(bf16[128,512]{1,0:T(8,128)(2,1)S(1)} %join.1.refs_0_) | copy-start | bytes 393220
  6.6 6.8 %collective-permute-start.1 = (bf16[16,4224]{1,0:T(8,128)(2,1)S(1)}, bf16[16,4224]{1,0:T(8,128)(2,1)S(1)}, u32[]{:S(2)}, u32[]{:S(2)}) collective-permute-start(bf16[16,4224]{1,0:T(8,128)(2,1)S(1)} %get-tuple-element.47), channel_id=1, source_target_pairs={{0,2},{2,0},{4,6},{6,4},{1,3},{3,1},{5,7},{7,5},{8,10},{10,8},{12,... | collective-permute-start | bytes 405512 | tf_op jit(solution)/shard_map/ppermute | solution.py:26
  8.2 5.2 %collective-permute-start = (bf16[16,4224]{1,0:T(8,128)(2,1)S(1)}, bf16[16,4224]{1,0:T(8,128)(2,1)S(1)}, u32[]{:S(2)}, u32[]{:S(2)}) collective-permute-start(bf16[16,4224]{1,0:T(8,128)(2,1)S(1)} %get-tuple-element.47), channel_id=1, source_target_pairs={{0,1},{1,0},{2,3},{3,2},{4,5},{5,4},{6,7},{7,6},{8,9},{9,8},{10,11... | collective-permute-start | bytes 405512 | tf_op jit(solution)/shard_map/ppermute | solution.py:26
  12.3 6.0 %collective-permute-start.3 = (bf16[16,4224]{1,0:T(8,128)(2,1)S(1)}, bf16[16,4224]{1,0:T(8,128)(2,1)S(1)}, u32[]{:S(2)}, u32[]{:S(2)}) collective-permute-start(bf16[16,4224]{1,0:T(8,128)(2,1)S(1)} %collective-permute-done.2.refs_2_), channel_id=1, source_target_pairs={{0,2},{2,0},{4,6},{6,4},{1,3},{3,1},{5,7},{7,5},{8,10},{10,8},{12,... | collective-permute-start | bytes 405512 | tf_op jit(solution)/shard_map/ppermute | solution.py:26
  13.4 6.3 %collective-permute-start.4 = (bf16[16,4224]{1,0:T(8,128)(2,1)S(1)}, bf16[16,4224]{1,0:T(8,128)(2,1)S(1)}, u32[]{:S(2)}, u32[]{:S(2)}) collective-permute-start(bf16[16,4224]{1,0:T(8,128)(2,1)S(1)} %collective-permute-done.refs_4_), channel_id=1, source_target_pairs={{0,2},{2,0},{4,6},{6,4},{1,3},{3,1},{5,7},{7,5},{8,10},{10,8},{12,... | collective-permute-start | bytes 405512 | tf_op jit(solution)/shard_map/ppermute | solution.py:26
  14.3 6.3 %collective-permute-start.5 = (bf16[16,4224]{1,0:T(8,128)(2,1)S(1)}, bf16[16,4224]{1,0:T(8,128)(2,1)S(1)}, u32[]{:S(2)}, u32[]{:S(2)}) collective-permute-start(bf16[16,4224]{1,0:T(8,128)(2,1)S(1)} %collective-permute-done.2.refs_2_), channel_id=1, source_target_pairs={{0,1},{1,0},{2,3},{3,2},{4,5},{5,4},{6,7},{7,6},{8,9},{9,8},{10,11... | collective-permute-start | bytes 405512 | tf_op jit(solution)/shard_map/ppermute | solution.py:26
  18.2 5.0 %collective-permute-start.6 = (bf16[16,4224]{1,0:T(8,128)(2,1)S(1)}, bf16[16,4224]{1,0:T(8,128)(2,1)S(1)}, u32[]{:S(2)}, u32[]{:S(2)}) collective-permute-start(bf16[16,4224]{1,0:T(8,128)(2,1)S(1)} %collective-permute-done.3.refs_3_), channel_id=1, source_target_pairs={{0,1},{1,0},{2,3},{3,2},{4,5},{5,4},{6,7},{7,6},{8,9},{9,8},{10,11... | collective-permute-start | bytes 405512 | tf_op jit(solution)/shard_map/ppermute | solution.py:26
  45.6 6.5 %collective-permute-start.7 = (bf16[16,4096]{1,0:T(8,128)(2,1)S(1)}, bf16[16,4096]{1,0:T(8,128)(2,1)S(1)}, u32[]{:S(2)}, u32[]{:S(2)}) collective-permute-start(bf16[16,4096]{1,0:T(8,128)(2,1)S(1)} %get-tuple-element.63), channel_id=1, source_target_pairs={{0,1},{1,0},{2,3},{3,2},{4,5},{5,4},{6,7},{7,6},{8,9},{9,8},{10,11... | collective-permute-start | bytes 393224 | tf_op jit(solution)/shard_map/ppermute | solution.py:26
  47.1 7.0 %collective-permute-start.8 = (bf16[16,4096]{1,0:T(8,128)(2,1)S(1)}, bf16[16,4096]{1,0:T(8,128)(2,1)S(1)}, u32[]{:S(2)}, u32[]{:S(2)}) collective-permute-start(bf16[16,4096]{1,0:T(8,128)(2,1)S(1)} %get-tuple-element.65), channel_id=1, source_target_pairs={{0,1},{1,0},{2,3},{3,2},{4,5},{5,4},{6,7},{7,6},{8,9},{9,8},{10,11... | collective-permute-start | bytes 393224 | tf_op jit(solution)/shard_map/ppermute | solution.py:26
  47.7 7.8 %collective-permute-start.12 = (bf16[16,4096]{1,0:T(8,128)(2,1)S(1)}, bf16[16,4096]{1,0:T(8,128)(2,1)S(1)}, u32[]{:S(2)}, u32[]{:S(2)}) collective-permute-start(bf16[16,4096]{1,0:T(8,128)(2,1)S(1)} %get-tuple-element.70), channel_id=1, source_target_pairs={{0,1},{1,0},{2,3},{3,2},{4,5},{5,4},{6,7},{7,6},{8,9},{9,8},{10,11... | collective-permute-start | bytes 393224 | tf_op jit(solution)/shard_map/ppermute | solution.py:26
  49.1 15.1 %collective-permute-start.16 = (bf16[16,4096]{1,0:T(8,128)(2,1)S(1)}, bf16[16,4096]{1,0:T(8,128)(2,1)S(1)}, u32[]{:S(2)}, u32[]{:S(2)}) collective-permute-start(bf16[16,4096]{1,0:T(8,128)(2,1)S(1)} %get-tuple-element.76), channel_id=1, source_target_pairs={{0,1},{1,0},{2,3},{3,2},{4,5},{5,4},{6,7},{7,6},{8,9},{9,8},{10,11... | collective-permute-start | bytes 393224 | tf_op jit(solution)/shard_map/ppermute | solution.py:26
  49.7 5.0 %collective-permute-start.9 = (bf16[128,512]{1,0:T(8,128)(2,1)S(1)}, bf16[128,512]{1,0:T(8,128)(2,1)S(1)}, u32[]{:S(2)}, u32[]{:S(2)}) collective-permute-start(bf16[128,512]{1,0:T(8,128)(2,1)S(1)} %join.1.refs_0_), channel_id=1, source_target_pairs={{0,16},{8,24},{16,0},{24,8},{1,17},{9,25},{17,1},{25,9},{2,18},{10... | collective-permute-start | bytes 393224 | tf_op jit(solution)/shard_map/ppermute | solution.py:26
  52.1 5.0 %collective-permute-start.11 = (bf16[16,4096]{1,0:T(8,128)(2,1)S(1)}, bf16[16,4096]{1,0:T(8,128)(2,1)S(1)}, u32[]{:S(2)}, u32[]{:S(2)}) collective-permute-start(bf16[16,4096]{1,0:T(8,128)(2,1)S(1)} %add_convert_fusion.3), channel_id=1, source_target_pairs={{0,2},{2,0},{4,6},{6,4},{1,3},{3,1},{5,7},{7,5},{8,10},{10,8},{12,... | collective-permute-start | bytes 393224 | tf_op jit(solution)/shard_map/ppermute | solution.py:26
  54.7 6.0 %copy-start.1 = (bf16[128,512]{1,0:T(8,128)(2,1)}, bf16[128,512]{1,0:T(8,128)(2,1)S(1)}, u32[]{:S(2)}) copy-start(bf16[128,512]{1,0:T(8,128)(2,1)S(1)} %collective-permute-done.9.refs_1_) | copy-start | bytes 393220
  54.7 2.5 %collective-permute-start.13 = (bf16[128,512]{1,0:T(8,128)(2,1)S(1)}, bf16[128,512]{1,0:T(8,128)(2,1)S(1)}, u32[]{:S(2)}, u32[]{:S(2)}) collective-permute-start(bf16[128,512]{1,0:T(8,128)(2,1)S(1)} %join.1.refs_0_), channel_id=1, source_target_pairs={{0,8},{8,0},{16,24},{24,16},{1,9},{9,1},{17,25},{25,17},{2,10},{10... | collective-permute-start | bytes 393224 | tf_op jit(solution)/shard_map/ppermute | solution.py:26
  54.7 2.5 %collective-permute-start.14 = (bf16[128,512]{1,0:T(8,128)(2,1)S(1)}, bf16[128,512]{1,0:T(8,128)(2,1)S(1)}, u32[]{:S(2)}, u32[]{:S(2)}) collective-permute-start(bf16[128,512]{1,0:T(8,128)(2,1)S(1)} %collective-permute-done.9.refs_1_), channel_id=1, source_target_pairs={{0,8},{8,0},{16,24},{24,16},{1,9},{9,1},{17,25},{25,17},{2,10},{10... | collective-permute-start | bytes 393224 | tf_op jit(solution)/shard_map/ppermute | solution.py:26
  55.5 8.8 %collective-permute-start.10 = (bf16[16,4096]{1,0:T(8,128)(2,1)S(1)}, bf16[16,4096]{1,0:T(8,128)(2,1)S(1)}, u32[]{:S(2)}, u32[]{:S(2)}) collective-permute-start(bf16[16,4096]{1,0:T(8,128)(2,1)S(1)} %add_convert_fusion.2), channel_id=1, source_target_pairs={{0,2},{2,0},{4,6},{6,4},{1,3},{3,1},{5,7},{7,5},{8,10},{10,8},{12,... | collective-permute-start | bytes 393224 | tf_op jit(solution)/shard_map/ppermute | solution.py:26
  57.1 3.5 %copy-start.2 = (bf16[128,512]{1,0:T(8,128)(2,1)}, bf16[128,512]{1,0:T(8,128)(2,1)S(1)}, u32[]{:S(2)}) copy-start(bf16[128,512]{1,0:T(8,128)(2,1)S(1)} %collective-permute-done.13.refs_2_) | copy-start | bytes 393220
  57.2 3.5 %copy-start.3 = (bf16[128,512]{1,0:T(8,128)(2,1)}, bf16[128,512]{1,0:T(8,128)(2,1)S(1)}, u32[]{:S(2)}) copy-start(bf16[128,512]{1,0:T(8,128)(2,1)S(1)} %collective-permute-done.14.refs_3_) | copy-start | bytes 393220
  57.2 9.1 %collective-permute-start.15 = (bf16[16,4096]{1,0:T(8,128)(2,1)S(1)}, bf16[16,4096]{1,0:T(8,128)(2,1)S(1)}, u32[]{:S(2)}, u32[]{:S(2)}) collective-permute-start(bf16[16,4096]{1,0:T(8,128)(2,1)S(1)} %add_convert_fusion.1), channel_id=1, source_target_pairs={{0,4},{2,6},{4,0},{6,2},{1,5},{3,7},{5,1},{7,3},{8,12},{10,14},{12... | collective-permute-start | bytes 393224 | tf_op jit(solution)/shard_map/ppermute | solution.py:26

commit v9 on v8

--- a/solution.py
+++ b/solution.py
@@ -293,7 +293,7 @@
 def collect(pieces, kv, beside):
     seq, tp = lax.axis_size("seq"), lax.axis_size("tp")
     terms = [[pieces[d]] for d in range(seq)]
-    order = sorted(range(seq), key=lambda d: (-d.bit_count(), d))
+    order = sorted(range(seq), key=lambda d: (-d.bit_count(), -d))
     step = lax.axis_size("group") // 2
     kv, offsets = [kv], [0]
     last = None

time: 67.3 us -> 67.8 us (level)
  starting transfers between devices: 23 us -> 25 us
  waiting for transfers between devices: 14.2 us -> 12.7 us
    ppermute x17, starting transfers between devices: 23 us -> 25 us  [swap(): return lax.ppermute(array, axis, [(i, i ^ offset) for i in range(count)])]
    ppermute x17, waiting for transfers between devices: 14.2 us -> 12.7 us  [swap(): return lax.ppermute(array, axis, [(i, i ^ offset) for i in range(count)])]
  transfers between devices with their start and end apart: 17 -> 17, of which waited for: 11 -> 9; matrix products, arithmetic and copies ran while one was open for 1% -> 1% of each run, Pallas kernels for 7% -> 7%
where the time goes in v9:
time: 67.8 us; the launch traced here: 67.6 us
  Pallas kernels  27.7 us (41%)
  starting transfers between devices  25 us (37%)
  waiting for transfers between devices  12.7 us (19%)
  other arithmetic  0.8 us (1%)
  between operations  0.71 us (1%)
  local copies, waits for them, and re-layouts  0.68 us (1%)
    ppermute x17, starting transfers between devices, swap(): return lax.ppermute(array, axis, [(i, i ^ offset) for i in range(count)])  25 us
    pallas_call x1, Pallas kernels, experts(): pl.pallas_call(functools.partial(experts_kernel, count=count, slots=slots...  22.3 us
    ppermute x17, waiting for transfers between devices, swap(): return lax.ppermute(array, axis, [(i, i ^ offset) for i in range(count)])  12.7 us
    pallas_call x1, Pallas kernels, attend(): pl.pallas_call(attention_kernel, in_specs=[SMEM] + [VMEM] * (1 + len(kv))...  3.55 us
  transfers between devices with their start and end apart: 17, of which 9 were waited for; matrix products, arithmetic and copies ran while one was open for 1% of the time, Pallas kernels for 7%

profile of v9, /device:TPU:0, one launch (start us, length us, event | category | flops | bytes accessed | tf_op | source)
XLA Modules:
  0.0 67.6 jit_solution(409685138384188112)
XLA Ops:
  0.6 1.0 %pack_rows.1 = (bf16[16,4224]{1,0:T(8,128)(2,1)S(1)}, bf16[16,4224]{1,0:T(8,128)(2,1)S(1)}) custom-call(s32[8,16]{1,0:T(8,128)} %bitcast.25, f32[8,16]{1,0:T(8,128)} %bitcast.26, bf16[16,2048]{1,0:T(8,128)(2,1)} %bitcast.21, bf16[16,2048]{1,0:T(8,128)(2,1)} %bitcast.22), custom_call_target="tpu_custom_call" | custom-call | tf_op jit(solution)/shard_map/pack_rows/pallas_call | solution.py:47
  1.6 4.1 %collective-permute-start.2 = (bf16[16,4224]{1,0:T(8,128)(2,1)S(1)}, bf16[16,4224]{1,0:T(8,128)(2,1)S(1)}, u32[]{:S(2)}, u32[]{:S(2)}) collective-permute-start(bf16[16,4224]{1,0:T(8,128)(2,1)S(1)} %get-tuple-element.47), channel_id=1, source_target_pairs={{0,4},{2,6},{4,0},{6,2},{1,5},{3,7},{5,1},{7,3},{8,12},{10,14},{12... | collective-permute-start | bytes 405512 | tf_op jit(solution)/shard_map/ppermute | solution.py:26
  5.7 0.9 %join.1.refs_0_ = bf16[128,512]{1,0:T(8,128)(2,1)S(1)} custom-call(bf16[128,256]{1,0:T(8,128)(2,1)} %bitcast.23, bf16[128,256]{1,0:T(8,128)(2,1)} %bitcast.24), custom_call_target="tpu_custom_call" | custom-call | bytes 262144 | tf_op jit(solution)/shard_map/join/pallas_call | solution.py:67
  6.6 0.0 copy-start
  6.6 1.6 %collective-permute-start.1 = (bf16[16,4224]{1,0:T(8,128)(2,1)S(1)}, bf16[16,4224]{1,0:T(8,128)(2,1)S(1)}, u32[]{:S(2)}, u32[]{:S(2)}) collective-permute-start(bf16[16,4224]{1,0:T(8,128)(2,1)S(1)} %get-tuple-element.47), channel_id=1, source_target_pairs={{0,2},{2,0},{4,6},{6,4},{1,3},{3,1},{5,7},{7,5},{8,10},{10,8},{12,... | collective-permute-start | bytes 405512 | tf_op jit(solution)/shard_map/ppermute | solution.py:26
  8.2 1.5 %collective-permute-start = (bf16[16,4224]{1,0:T(8,128)(2,1)S(1)}, bf16[16,4224]{1,0:T(8,128)(2,1)S(1)}, u32[]{:S(2)}, u32[]{:S(2)}) collective-permute-start(bf16[16,4224]{1,0:T(8,128)(2,1)S(1)} %get-tuple-element.47), channel_id=1, source_target_pairs={{0,1},{1,0},{2,3},{3,2},{4,5},{5,4},{6,7},{7,6},{8,9},{9,8},{10,11... | collective-permute-start | bytes 405512 | tf_op jit(solution)/shard_map/ppermute | solution.py:26
  9.7 2.5 %collective-permute-done.2.refs_2_ = bf16[16,4224]{1,0:T(8,128)(2,1)S(1)} collective-permute-done((bf16[16,4224]{1,0:T(8,128)(2,1)S(1)}, bf16[16,4224]{1,0:T(8,128)(2,1)S(1)}, u32[]{:S(2)}, u32[]{:S(2)}) %collective-permute-start.2) | collective-permute-done | bytes 135200 | tf_op jit(solution)/shard_map/ppermute | solution.py:26
  12.3 0.7 collective-permute-start.3
  12.9 0.5 collective-permute-done.1.refs_1_
  13.4 0.0 collective-permute-done.refs_4_
  13.4 0.9 %collective-permute-start.4 = (bf16[16,4224]{1,0:T(8,128)(2,1)S(1)}, bf16[16,4224]{1,0:T(8,128)(2,1)S(1)}, u32[]{:S(2)}, u32[]{:S(2)}) collective-permute-start(bf16[16,4224]{1,0:T(8,128)(2,1)S(1)} %collective-permute-done.refs_4_), channel_id=1, source_target_pairs={{0,2},{2,0},{4,6},{6,4},{1,3},{3,1},{5,7},{7,5},{8,10},{10,8},{12,... | collective-permute-start | bytes 405512 | tf_op jit(solution)/shard_map/ppermute | solution.py:26
  14.3 1.6 %collective-permute-start.5 = (bf16[16,4224]{1,0:T(8,128)(2,1)S(1)}, bf16[16,4224]{1,0:T(8,128)(2,1)S(1)}, u32[]{:S(2)}, u32[]{:S(2)}) collective-permute-start(bf16[16,4224]{1,0:T(8,128)(2,1)S(1)} %collective-permute-done.2.refs_2_), channel_id=1, source_target_pairs={{0,1},{1,0},{2,3},{3,2},{4,5},{5,4},{6,7},{7,6},{8,9},{9,8},{10,11... | collective-permute-start | bytes 405512 | tf_op jit(solution)/shard_map/ppermute | solution.py:26
  15.9 2.4 %collective-permute-done.3.refs_3_ = bf16[16,4224]{1,0:T(8,128)(2,1)S(1)} collective-permute-done((bf16[16,4224]{1,0:T(8,128)(2,1)S(1)}, bf16[16,4224]{1,0:T(8,128)(2,1)S(1)}, u32[]{:S(2)}, u32[]{:S(2)}) %collective-permute-start.3) | collective-permute-done | bytes 135200 | tf_op jit(solution)/shard_map/ppermute | solution.py:26
  18.2 1.5 %collective-permute-start.6 = (bf16[16,4224]{1,0:T(8,128)(2,1)S(1)}, bf16[16,4224]{1,0:T(8,128)(2,1)S(1)}, u32[]{:S(2)}, u32[]{:S(2)}) collective-permute-start(bf16[16,4224]{1,0:T(8,128)(2,1)S(1)} %collective-permute-done.3.refs_3_), channel_id=1, source_target_pairs={{0,1},{1,0},{2,3},{3,2},{4,5},{5,4},{6,7},{7,6},{8,9},{9,8},{10,11... | collective-permute-start | bytes 405512 | tf_op jit(solution)/shard_map/ppermute | solution.py:26
  19.7 0.0 collective-permute-done.4.refs_5_
  19.7 1.0 %collective-permute-done.5.refs_6_ = bf16[16,4224]{1,0:T(8,128)(2,1)S(1)} collective-permute-done((bf16[16,4224]{1,0:T(8,128)(2,1)S(1)}, bf16[16,4224]{1,0:T(8,128)(2,1)S(1)}, u32[]{:S(2)}, u32[]{:S(2)}) %collective-permute-start.5) | collective-permute-done | bytes 135200 | tf_op jit(solution)/shard_map/ppermute | solution.py:26
  20.7 2.6 %collective-permute-done.6.refs_7_ = bf16[16,4224]{1,0:T(8,128)(2,1)S(1)} collective-permute-done((bf16[16,4224]{1,0:T(8,128)(2,1)S(1)}, bf16[16,4224]{1,0:T(8,128)(2,1)S(1)}, u32[]{:S(2)}, u32[]{:S(2)}) %collective-permute-start.6) | collective-permute-done | bytes 135200 | tf_op jit(solution)/shard_map/ppermute | solution.py:26
  23.2 22.3 %experts.1 = (bf16[16,4096]{1,0:T(8,128)(2,1)S(1)}, bf16[16,4096]{1,0:T(8,128)(2,1)S(1)}, bf16[16,4096]{1,0:T(8,128)(2,1)S(1)}, bf16[16,4096]{1,0:T(8,128)(2,1)S...) custom-call(s32[1]{0:T(128)} %bitcast.shard_ref, ...), custom_call_target="tpu_custom_call" | custom-call | flops 2415919104 | bytes 37748736 | tf_op jit(solution)/shard_map/experts/pallas_call | solution.py:246
  45.6 1.5 %collective-permute-start.7 = (bf16[16,4096]{1,0:T(8,128)(2,1)S(1)}, bf16[16,4096]{1,0:T(8,128)(2,1)S(1)}, u32[]{:S(2)}, u32[]{:S(2)}) collective-permute-start(bf16[16,4096]{1,0:T(8,128)(2,1)S(1)} %get-tuple-element.63), channel_id=1, source_target_pairs={{0,1},{1,0},{2,3},{3,2},{4,5},{5,4},{6,7},{7,6},{8,9},{9,8},{10,11... | collective-permute-start | bytes 393224 | tf_op jit(solution)/shard_map/ppermute | solution.py:26
  47.1 0.6 collective-permute-start.9
  47.7 1.4 %collective-permute-start.10 = (bf16[128,512]{1,0:T(8,128)(2,1)S(1)}, bf16[128,512]{1,0:T(8,128)(2,1)S(1)}, u32[]{:S(2)}, u32[]{:S(2)}) collective-permute-start(bf16[128,512]{1,0:T(8,128)(2,1)S(1)} %join.1.refs_0_), channel_id=1, source_target_pairs={{0,16},{8,24},{16,0},{24,8},{1,17},{9,25},{17,1},{25,9},{2,18},{10... | collective-permute-start | bytes 393224 | tf_op jit(solution)/shard_map/ppermute | solution.py:26
  49.1 1.7 %collective-permute-done.7 = bf16[16,4096]{1,0:T(8,128)(2,1)S(1)} collective-permute-done((bf16[16,4096]{1,0:T(8,128)(2,1)S(1)}, bf16[16,4096]{1,0:T(8,128)(2,1)S(1)}, u32[]{:S(2)}, u32[]{:S(2)}) %collective-permute-start.7) | collective-permute-done | bytes 131104 | tf_op jit(solution)/shard_map/ppermute | solution.py:26
  50.9 1.4 %collective-permute-start.8 = (bf16[16,4096]{1,0:T(8,128)(2,1)S(1)}, bf16[16,4096]{1,0:T(8,128)(2,1)S(1)}, u32[]{:S(2)}, u32[]{:S(2)}) collective-permute-start(bf16[16,4096]{1,0:T(8,128)(2,1)S(1)} %add_convert_fusion.3), channel_id=1, source_target_pairs={{0,2},{2,0},{4,6},{6,4},{1,3},{3,1},{5,7},{7,5},{8,10},{10,8},{12,... | collective-permute-start | bytes 393224 | tf_op jit(solution)/shard_map/ppermute | solution.py:26
  52.3 1.6 %collective-permute-start.12 = (bf16[16,4096]{1,0:T(8,128)(2,1)S(1)}, bf16[16,4096]{1,0:T(8,128)(2,1)S(1)}, u32[]{:S(2)}, u32[]{:S(2)}) collective-permute-start(bf16[16,4096]{1,0:T(8,128)(2,1)S(1)} %get-tuple-element.71), channel_id=1, source_target_pairs={{0,1},{1,0},{2,3},{3,2},{4,5},{5,4},{6,7},{7,6},{8,9},{9,8},{10,11... | collective-permute-start | bytes 393224 | tf_op jit(solution)/shard_map/ppermute | solution.py:26
  53.9 0.4 collective-permute-start.16
  54.3 0.0 collective-permute-done.9
  54.3 0.0 collective-permute-done.10.refs_1_
  54.3 0.0 copy-start.1
  54.3 1.6 %collective-permute-done.8 = bf16[16,4096]{1,0:T(8,128)(2,1)S(1)} collective-permute-done((bf16[16,4096]{1,0:T(8,128)(2,1)S(1)}, bf16[16,4096]{1,0:T(8,128)(2,1)S(1)}, u32[]{:S(2)}, u32[]{:S(2)}) %collective-permute-start.8) | collective-permute-done | bytes 131104 | tf_op jit(solution)/shard_map/ppermute | solution.py:26
  55.9 0.0 copy-done
  55.9 0.0 collective-permute-start.13
  55.9 0.5 collective-permute-start.14
  56.4 0.1 add_convert_fusion.2
  56.5 3.6 %collective-permute-start.11 = (bf16[16,4096]{1,0:T(8,128)(2,1)S(1)}, bf16[16,4096]{1,0:T(8,128)(2,1)S(1)}, u32[]{:S(2)}, u32[]{:S(2)}) collective-permute-start(bf16[16,4096]{1,0:T(8,128)(2,1)S(1)} %add_convert_fusion.2), channel_id=1, source_target_pairs={{0,4},{2,6},{4,0},{6,2},{1,5},{3,7},{5,1},{7,3},{8,12},{10,14},{12... | collective-permute-start | bytes 393224 | tf_op jit(solution)/shard_map/ppermute | solution.py:26
  60.1 0.0 collective-permute-done.12
  60.1 0.0 collective-permute-done.13.refs_2_
  60.1 0.0 copy-start.2
  60.1 0.0 collective-permute-done.14.refs_3_
  60.1 0.0 copy-start.3
  60.2 2.1 %collective-permute-start.15 = (bf16[16,4096]{1,0:T(8,128)(2,1)S(1)}, bf16[16,4096]{1,0:T(8,128)(2,1)S(1)}, u32[]{:S(2)}, u32[]{:S(2)}) collective-permute-start(bf16[16,4096]{1,0:T(8,128)(2,1)S(1)} %add_convert_fusion.1), channel_id=1, source_target_pairs={{0,2},{2,0},{4,6},{6,4},{1,3},{3,1},{5,7},{7,5},{8,10},{10,8},{12,... | collective-permute-start | bytes 393224 | tf_op jit(solution)/shard_map/ppermute | solution.py:26
  62.2 0.6 pad_add_fusion.base_ref
  62.9 0.0 copy-done.1
  62.9 0.0 copy-done.2
  62.9 0.0 copy-done.3
  62.9 3.6 %attention.1 = bf16[128,2048]{1,0:T(8,128)(2,1)} custom-call(s32[4]{0:T(128)} %pad_add_fusion.base_ref, bf16[128,2048]{1,0:T(8,128)(2,1)} %bitcast.27, bf16[128,512]{1,0:T(8,128)(2,1)} %copy-done, bf16[128,512]{1,0:T(8,128)(2,1)} %copy-done.1, bf16[128,512]{1,0:T(8,128)(2,1)} %copy-done.2, bf16[128,512]{1,0:T(8,128)(2,1)} %copy-done.3), custom_call_target="tpu_custom_call" | custom-call | flops 536870912 | bytes 1048576 | tf_op jit(solution)/shard_map/attention/pallas_call | solution.py:110
  66.4 0.0 collective-permute-done.16
  66.4 0.2 collective-permute-done.11
  66.7 0.2 collective-permute-done.15
  66.9 0.1 add_convert_fusion
  66.9 0.7 slice_bitcast_fusion
  (2 shorter events, 0.1 us)
Async XLA Ops:
  1.6 10.7 %collective-permute-start.2 = (bf16[16,4224]{1,0:T(8,128)(2,1)S(1)}, bf16[16,4224]{1,0:T(8,128)(2,1)S(1)}, u32[]{:S(2)}, u32[]{:S(2)}) collective-permute-start(bf16[16,4224]{1,0:T(8,128)(2,1)S(1)} %get-tuple-element.47), channel_id=1, source_target_pairs={{0,4},{2,6},{4,0},{6,2},{1,5},{3,7},{5,1},{7,3},{8,12},{10,14},{12... | collective-permute-start | bytes 405512 | tf_op jit(solution)/shard_map/ppermute | solution.py:26
  6.6 49.3 %copy-start = (bf16[128,512]{1,0:T(8,128)(2,1)}, bf16[128,512]{1,0:T(8,128)(2,1)S(1)}, u32[]{:S(2)}) copy-start(bf16[128,512]{1,0:T(8,128)(2,1)S(1)} %join.1.refs_0_) | copy-start | bytes 393220
  6.6 6.8 %collective-permute-start.1 = (bf16[16,4224]{1,0:T(8,128)(2,1)S(1)}, bf16[16,4224]{1,0:T(8,128)(2,1)S(1)}, u32[]{:S(2)}, u32[]{:S(2)}) collective-permute-start(bf16[16,4224]{1,0:T(8,128)(2,1)S(1)} %get-tuple-element.47), channel_id=1, source_target_pairs={{0,2},{2,0},{4,6},{6,4},{1,3},{3,1},{5,7},{7,5},{8,10},{10,8},{12,... | collective-permute-start | bytes 405512 | tf_op jit(solution)/shard_map/ppermute | solution.py:26
  8.2 5.2 %collective-permute-start = (bf16[16,4224]{1,0:T(8,128)(2,1)S(1)}, bf16[16,4224]{1,0:T(8,128)(2,1)S(1)}, u32[]{:S(2)}, u32[]{:S(2)}) collective-permute-start(bf16[16,4224]{1,0:T(8,128)(2,1)S(1)} %get-tuple-element.47), channel_id=1, source_target_pairs={{0,1},{1,0},{2,3},{3,2},{4,5},{5,4},{6,7},{7,6},{8,9},{9,8},{10,11... | collective-permute-start | bytes 405512 | tf_op jit(solution)/shard_map/ppermute | solution.py:26
  12.3 6.0 %collective-permute-start.3 = (bf16[16,4224]{1,0:T(8,128)(2,1)S(1)}, bf16[16,4224]{1,0:T(8,128)(2,1)S(1)}, u32[]{:S(2)}, u32[]{:S(2)}) collective-permute-start(bf16[16,4224]{1,0:T(8,128)(2,1)S(1)} %collective-permute-done.2.refs_2_), channel_id=1, source_target_pairs={{0,2},{2,0},{4,6},{6,4},{1,3},{3,1},{5,7},{7,5},{8,10},{10,8},{12,... | collective-permute-start | bytes 405512 | tf_op jit(solution)/shard_map/ppermute | solution.py:26
  13.4 6.3 %collective-permute-start.4 = (bf16[16,4224]{1,0:T(8,128)(2,1)S(1)}, bf16[16,4224]{1,0:T(8,128)(2,1)S(1)}, u32[]{:S(2)}, u32[]{:S(2)}) collective-permute-start(bf16[16,4224]{1,0:T(8,128)(2,1)S(1)} %collective-permute-done.refs_4_), channel_id=1, source_target_pairs={{0,2},{2,0},{4,6},{6,4},{1,3},{3,1},{5,7},{7,5},{8,10},{10,8},{12,... | collective-permute-start | bytes 405512 | tf_op jit(solution)/shard_map/ppermute | solution.py:26
  14.3 6.3 %collective-permute-start.5 = (bf16[16,4224]{1,0:T(8,128)(2,1)S(1)}, bf16[16,4224]{1,0:T(8,128)(2,1)S(1)}, u32[]{:S(2)}, u32[]{:S(2)}) collective-permute-start(bf16[16,4224]{1,0:T(8,128)(2,1)S(1)} %collective-permute-done.2.refs_2_), channel_id=1, source_target_pairs={{0,1},{1,0},{2,3},{3,2},{4,5},{5,4},{6,7},{7,6},{8,9},{9,8},{10,11... | collective-permute-start | bytes 405512 | tf_op jit(solution)/shard_map/ppermute | solution.py:26
  18.2 5.0 %collective-permute-start.6 = (bf16[16,4224]{1,0:T(8,128)(2,1)S(1)}, bf16[16,4224]{1,0:T(8,128)(2,1)S(1)}, u32[]{:S(2)}, u32[]{:S(2)}) collective-permute-start(bf16[16,4224]{1,0:T(8,128)(2,1)S(1)} %collective-permute-done.3.refs_3_), channel_id=1, source_target_pairs={{0,1},{1,0},{2,3},{3,2},{4,5},{5,4},{6,7},{7,6},{8,9},{9,8},{10,11... | collective-permute-start | bytes 405512 | tf_op jit(solution)/shard_map/ppermute | solution.py:26
  45.6 5.3 %collective-permute-start.7 = (bf16[16,4096]{1,0:T(8,128)(2,1)S(1)}, bf16[16,4096]{1,0:T(8,128)(2,1)S(1)}, u32[]{:S(2)}, u32[]{:S(2)}) collective-permute-start(bf16[16,4096]{1,0:T(8,128)(2,1)S(1)} %get-tuple-element.63), channel_id=1, source_target_pairs={{0,1},{1,0},{2,3},{3,2},{4,5},{5,4},{6,7},{7,6},{8,9},{9,8},{10,11... | collective-permute-start | bytes 393224 | tf_op jit(solution)/shard_map/ppermute | solution.py:26
  47.1 7.2 %collective-permute-start.9 = (bf16[16,4096]{1,0:T(8,128)(2,1)S(1)}, bf16[16,4096]{1,0:T(8,128)(2,1)S(1)}, u32[]{:S(2)}, u32[]{:S(2)}) collective-permute-start(bf16[16,4096]{1,0:T(8,128)(2,1)S(1)} %get-tuple-element.65), channel_id=1, source_target_pairs={{0,1},{1,0},{2,3},{3,2},{4,5},{5,4},{6,7},{7,6},{8,9},{9,8},{10,11... | collective-permute-start | bytes 393224 | tf_op jit(solution)/shard_map/ppermute | solution.py:26
  47.7 6.7 %collective-permute-start.10 = (bf16[128,512]{1,0:T(8,128)(2,1)S(1)}, bf16[128,512]{1,0:T(8,128)(2,1)S(1)}, u32[]{:S(2)}, u32[]{:S(2)}) collective-permute-start(bf16[128,512]{1,0:T(8,128)(2,1)S(1)} %join.1.refs_0_), channel_id=1, source_target_pairs={{0,16},{8,24},{16,0},{24,8},{1,17},{9,25},{17,1},{25,9},{2,18},{10... | collective-permute-start | bytes 393224 | tf_op jit(solution)/shard_map/ppermute | solution.py:26
  50.9 5.0 %collective-permute-start.8 = (bf16[16,4096]{1,0:T(8,128)(2,1)S(1)}, bf16[16,4096]{1,0:T(8,128)(2,1)S(1)}, u32[]{:S(2)}, u32[]{:S(2)}) collective-permute-start(bf16[16,4096]{1,0:T(8,128)(2,1)S(1)} %add_convert_fusion.3), channel_id=1, source_target_pairs={{0,2},{2,0},{4,6},{6,4},{1,3},{3,1},{5,7},{7,5},{8,10},{10,8},{12,... | collective-permute-start | bytes 393224 | tf_op jit(solution)/shard_map/ppermute | solution.py:26
  52.3 7.8 %collective-permute-start.12 = (bf16[16,4096]{1,0:T(8,128)(2,1)S(1)}, bf16[16,4096]{1,0:T(8,128)(2,1)S(1)}, u32[]{:S(2)}, u32[]{:S(2)}) collective-permute-start(bf16[16,4096]{1,0:T(8,128)(2,1)S(1)} %get-tuple-element.71), channel_id=1, source_target_pairs={{0,1},{1,0},{2,3},{3,2},{4,5},{5,4},{6,7},{7,6},{8,9},{9,8},{10,11... | collective-permute-start | bytes 393224 | tf_op jit(solution)/shard_map/ppermute | solution.py:26
  53.9 12.5 %collective-permute-start.16 = (bf16[16,4096]{1,0:T(8,128)(2,1)S(1)}, bf16[16,4096]{1,0:T(8,128)(2,1)S(1)}, u32[]{:S(2)}, u32[]{:S(2)}) collective-permute-start(bf16[16,4096]{1,0:T(8,128)(2,1)S(1)} %get-tuple-element.76), channel_id=1, source_target_pairs={{0,1},{1,0},{2,3},{3,2},{4,5},{5,4},{6,7},{7,6},{8,9},{9,8},{10,11... | collective-permute-start | bytes 393224 | tf_op jit(solution)/shard_map/ppermute | solution.py:26
  54.3 8.5 %copy-start.1 = (bf16[128,512]{1,0:T(8,128)(2,1)}, bf16[128,512]{1,0:T(8,128)(2,1)S(1)}, u32[]{:S(2)}) copy-start(bf16[128,512]{1,0:T(8,128)(2,1)S(1)} %collective-permute-done.10.refs_1_) | copy-start | bytes 393220
  55.9 4.2 %collective-permute-start.13 = (bf16[128,512]{1,0:T(8,128)(2,1)S(1)}, bf16[128,512]{1,0:T(8,128)(2,1)S(1)}, u32[]{:S(2)}, u32[]{:S(2)}) collective-permute-start(bf16[128,512]{1,0:T(8,128)(2,1)S(1)} %join.1.refs_0_), channel_id=1, source_target_pairs={{0,8},{8,0},{16,24},{24,16},{1,9},{9,1},{17,25},{25,17},{2,10},{10... | collective-permute-start | bytes 393224 | tf_op jit(solution)/shard_map/ppermute | solution.py:26
  55.9 4.2 %collective-permute-start.14 = (bf16[128,512]{1,0:T(8,128)(2,1)S(1)}, bf16[128,512]{1,0:T(8,128)(2,1)S(1)}, u32[]{:S(2)}, u32[]{:S(2)}) collective-permute-start(bf16[128,512]{1,0:T(8,128)(2,1)S(1)} %collective-permute-done.10.refs_1_), channel_id=1, source_target_pairs={{0,8},{8,0},{16,24},{24,16},{1,9},{9,1},{17,25},{25,17},{2,10},{10... | collective-permute-start | bytes 393224 | tf_op jit(solution)/shard_map/ppermute | solution.py:26
  56.5 10.2 %collective-permute-start.11 = (bf16[16,4096]{1,0:T(8,128)(2,1)S(1)}, bf16[16,4096]{1,0:T(8,128)(2,1)S(1)}, u32[]{:S(2)}, u32[]{:S(2)}) collective-permute-start(bf16[16,4096]{1,0:T(8,128)(2,1)S(1)} %add_convert_fusion.2), channel_id=1, source_target_pairs={{0,4},{2,6},{4,0},{6,2},{1,5},{3,7},{5,1},{7,3},{8,12},{10,14},{12... | collective-permute-start | bytes 393224 | tf_op jit(solution)/shard_map/ppermute | solution.py:26
  60.1 2.8 %copy-start.2 = (bf16[128,512]{1,0:T(8,128)(2,1)}, bf16[128,512]{1,0:T(8,128)(2,1)S(1)}, u32[]{:S(2)}) copy-start(bf16[128,512]{1,0:T(8,128)(2,1)S(1)} %collective-permute-done.13.refs_2_) | copy-start | bytes 393220
  60.1 2.8 %copy-start.3 = (bf16[128,512]{1,0:T(8,128)(2,1)}, bf16[128,512]{1,0:T(8,128)(2,1)S(1)}, u32[]{:S(2)}) copy-start(bf16[128,512]{1,0:T(8,128)(2,1)S(1)} %collective-permute-done.14.refs_3_) | copy-start | bytes 393220
  60.2 6.7 %collective-permute-start.15 = (bf16[16,4096]{1,0:T(8,128)(2,1)S(1)}, bf16[16,4096]{1,0:T(8,128)(2,1)S(1)}, u32[]{:S(2)}, u32[]{:S(2)}) collective-permute-start(bf16[16,4096]{1,0:T(8,128)(2,1)S(1)} %add_convert_fusion.1), channel_id=1, source_target_pairs={{0,2},{2,0},{4,6},{6,4},{1,3},{3,1},{5,7},{7,5},{8,10},{10,8},{12,... | collective-permute-start | bytes 393224 | tf_op jit(solution)/shard_map/ppermute | solution.py:26
